TPU v7x, 32 devices: a whole 2x2x4 slice. The times are simulated.
32 devices in a mesh: dp: 16 (over z, y, core), mp: 2 (over x).
Axes of the slice: x: 2, y: 2, z: 4, core: 2. Of those that a mesh axis runs over, the one named last changes fastest.
Arguments:
- hidden_in: bfloat16 [32768, 1024], P(('dp', 'mp')), may hold values from -46 to 46
- seq_lengths: int32 [16, 4], P('dp'), may hold values from 0 to 2048, as said below
- ln_scale: float32 [1024], replicated, may hold values from 0.25 to 1.75
- ln_bias: float32 [1024], replicated, may hold values from -3 to 3
- qkv_weight: bfloat16 [1024, 3072], P(None, 'mp'), may hold values from -0.1875 to 0.1875
- out_weight: bfloat16 [1024, 1024], P('mp'), may hold values from -1.5 to 1.5
- in_weight: bfloat16 [1024, 4096], P(None, 'mp'), may hold values from -0.1875 to 0.1875
- down_weight: bfloat16 [4096, 1024], P('mp'), may hold values from -0.09375 to 0.09375
- out_grad: bfloat16 [32768, 1024], P(('dp', 'mp')), may hold values from -6 to 6
Outputs:
- hidden_out: bfloat16 [32768, 1024], P(('dp', 'mp'))
- grad_hidden: float32 [32768, 1024], P(('dp', 'mp'))
- grad_scale: float32 [1024], replicated
- grad_bias: float32 [1024], replicated
- grad_qkv_weight: float32 [1024, 3072], P(None, 'mp')
- grad_out_weight: float32 [1024, 1024], P('mp')
- grad_in_weight: float32 [1024, 4096], P(None, 'mp')
- grad_down_weight: float32 [4096, 1024], P('mp')
- stats: float32 [3], replicated
Inputs may be any that keep to these rules, and one draw needn't show every extreme that they name: `seq_lengths`: each group's lengths sum to 2048; every run of 2048 tokens of a group, from the group's start, holds whole sequences of 512, 1024 or 2048 tokens, listed in order, with zeros in the slots that a run leaves unused; some group holds a sequence of 2048 tokens.
All inputs are finite; a program needn't handle non-finite values.
Results may differ from a plain program's by a relative error of at most 0.015.
Values may be sent and summed in bfloat16 or wider, within the bound.
A program may use at most 192 MiB of HBM per device.

v0:
```python
import jax
import jax.numpy as jnp
from jax import lax
from jax.sharding import PartitionSpec as P

HEAD = 64
ROT = 16
SEQ_UNIT = 512


epsilon = 1e-05
rope_base = 10000.0
masked_score = -1e30


def layout(lengths, group_rows):
    seg_ends = jnp.cumsum(lengths)
    positions = jnp.arange(group_rows, dtype=jnp.int32)
    closed = seg_ends[None, :] <= positions[:, None]
    segment = jnp.sum(closed.astype(jnp.int32), axis=1)
    seg_start = jnp.sum(jnp.where(closed, lengths[None, :], 0), axis=1)
    return (segment, positions - seg_start)


def rotary_tables(offset):
    half_rot = ROT // 2
    inv_freq = jnp.power(rope_base, -2.0 * jnp.arange(half_rot, dtype=jnp.float32) / ROT)
    angles = offset.astype(jnp.float32)[:, None] * inv_freq[None, :]
    return (jnp.cos(angles), jnp.sin(angles))


def rotate(values, cosine_table, sine_table):
    half_rot = ROT // 2
    front_half = values[..., :half_rot]
    back_half = values[..., half_rot:ROT]
    cosine = cosine_table[:, None, :]
    sine_rows = sine_table[:, None, :]
    return jnp.concatenate(
        [
            front_half * cosine - back_half * sine_rows,
            back_half * cosine + front_half * sine_rows,
            values[..., ROT:],
        ],
        axis=-1,
    )


def along_rows(left_side, right_side):
    return lax.dot_general(
        left_side, right_side, (((0,), (0,)), ((), ())), preferred_element_type=jnp.float32
    )


def against(left_side, right_side):
    return lax.dot_general(
        left_side, right_side, (((1,), (1,)), ((), ())), preferred_element_type=jnp.float32
    )


def to_items(values, quad_rows):
    group_rows, heads_dev, head_dim = values.shape
    quad_count = group_rows // quad_rows
    return (
        values.reshape(quad_count, quad_rows, heads_dev, head_dim)
        .transpose(2, 0, 1, 3)
        .reshape(heads_dev * quad_count, quad_rows, head_dim)
    )


def from_items(items_arr, heads_dev):
    total_items, quad_rows, head_dim = items_arr.shape
    quad_count = total_items // heads_dev
    return (
        items_arr.reshape(heads_dev, quad_count, quad_rows, head_dim)
        .transpose(1, 2, 0, 3)
        .reshape(quad_count * quad_rows, heads_dev, head_dim)
    )


def scored(queries, key_rows, segment):
    score_scale = queries.shape[1] ** (-0.5)
    raw_score = against(queries, key_rows) * score_scale
    positions = jnp.arange(segment.shape[0])
    allowed = (segment[:, None] == segment[None, :]) & (positions[None, :] <= positions[:, None])
    return jnp.where(allowed, raw_score, masked_score)


def attend_forward(packed):
    queries, key_rows, values, segment = packed
    scores = scored(queries, key_rows, segment)
    row_max = jnp.max(scores, axis=1, keepdims=True)
    weight = jnp.exp(scores - row_max)
    row_total = jnp.sum(weight, axis=1, keepdims=True)
    attn_prob = (weight / row_total).astype(jnp.bfloat16)
    context = jnp.dot(attn_prob, values, preferred_element_type=jnp.float32)
    return (context, (row_max + jnp.log(row_total))[:, 0])


def attend_backward(packed):
    queries, key_rows, values, segment, logsum, grad_context = packed
    scores = scored(queries, key_rows, segment)
    attn_prob = jnp.exp(scores - logsum[:, None])
    grad_prob = against(grad_context, values)
    grad_values = along_rows(attn_prob.astype(jnp.bfloat16), grad_context)
    grad_scores = (
        attn_prob * (grad_prob - jnp.sum(attn_prob * grad_prob, axis=1, keepdims=True))
    ).astype(jnp.bfloat16)
    score_scale = queries.shape[1] ** (-0.5)
    grad_queries = jnp.dot(grad_scores, key_rows, preferred_element_type=jnp.float32) * score_scale
    grad_keys = along_rows(grad_scores, queries) * score_scale
    return (grad_queries, grad_keys, grad_values)


def gelu_slope(values):
    normal_cdf = 0.5 * (1.0 + lax.erf(values * 0.7071067811865476))
    return normal_cdf + values * jnp.exp(-0.5 * values * values) * 0.3989422804014327


def on_device(
    hidden_in,
    seq_lengths,
    ln_scale,
    ln_bias,
    qkv_weight,
    out_weight,
    in_weight,
    down_weight,
    out_grad,
):
    tok_rows, model_width = hidden_in.shape
    head_width = out_weight.shape[0]
    heads_dev = head_width // HEAD
    hidden_dev = in_weight.shape[1]
    group_rows = tok_rows * lax.axis_size("mp")
    quad_rows = 4 * SEQ_UNIT
    segment, offset = layout(seq_lengths[0], group_rows)
    cosine_table, sine_table = rotary_tables(offset)
    item_segment = jnp.tile(segment.reshape(group_rows // quad_rows, quad_rows), (heads_dev, 1))
    residual = hidden_in.astype(jnp.float32)
    row_mean = jnp.mean(residual, axis=1, keepdims=True)
    centred = residual - row_mean
    row_var = jnp.mean(centred * centred, axis=1, keepdims=True)
    inv_std = lax.rsqrt(row_var + epsilon)
    unit_rows = centred * inv_std
    normed = (unit_rows * ln_scale + ln_bias).astype(jnp.bfloat16)
    gathered = lax.all_gather(normed, "mp", axis=0, tiled=True)
    qkv_rows = jnp.dot(gathered, qkv_weight, preferred_element_type=jnp.float32).reshape(
        group_rows, heads_dev, 3, HEAD
    )
    queries = rotate(qkv_rows[:, :, 0], cosine_table, sine_table).astype(jnp.bfloat16)
    key_rows = rotate(qkv_rows[:, :, 1], cosine_table, sine_table).astype(jnp.bfloat16)
    values = qkv_rows[:, :, 2].astype(jnp.bfloat16)
    query_items = to_items(queries, quad_rows)
    key_items = to_items(key_rows, quad_rows)
    value_items = to_items(values, quad_rows)
    context_items, logsum = lax.map(
        attend_forward, (query_items, key_items, value_items, item_segment)
    )
    context = (
        from_items(context_items, heads_dev).reshape(group_rows, head_width).astype(jnp.bfloat16)
    )
    pre_act = jnp.dot(gathered, in_weight, preferred_element_type=jnp.float32)
    active = jax.nn.gelu(pre_act, approximate=False).astype(jnp.bfloat16)
    update = lax.psum_scatter(
        (
            jnp.dot(context, out_weight, preferred_element_type=jnp.float32)
            + jnp.dot(active, down_weight, preferred_element_type=jnp.float32)
        ).astype(jnp.bfloat16),
        "mp",
        scatter_dimension=0,
        tiled=True,
    ).astype(jnp.float32)
    result = residual + update
    context_wide = context.astype(jnp.float32)
    active_wide = active.astype(jnp.float32)
    local_stats = jnp.stack(
        [
            jnp.sum(result * result),
            jnp.sum(context_wide * context_wide),
            jnp.sum(active_wide * active_wide),
        ]
    )
    stat_sums = lax.psum(local_stats, ("dp", "mp"))
    grad_rows = lax.all_gather(out_grad, "mp", axis=0, tiled=True)
    grad_down = along_rows(active, grad_rows)
    grad_outw = along_rows(context, grad_rows)
    grad_pre = (against(grad_rows, down_weight) * gelu_slope(pre_act)).astype(jnp.bfloat16)
    grad_inw = along_rows(gathered, grad_pre)
    grad_context = (
        against(grad_rows, out_weight).astype(jnp.bfloat16).reshape(group_rows, heads_dev, HEAD)
    )
    grad_q_items, grad_k_items, grad_v_items = lax.map(
        attend_backward,
        (
            query_items,
            key_items,
            value_items,
            item_segment,
            logsum,
            to_items(grad_context, quad_rows),
        ),
    )
    grad_queries = rotate(from_items(grad_q_items, heads_dev), cosine_table, -sine_table)
    grad_keys = rotate(from_items(grad_k_items, heads_dev), cosine_table, -sine_table)
    grad_values = from_items(grad_v_items, heads_dev)
    grad_qkv = (
        jnp.stack([grad_queries, grad_keys, grad_values], axis=2)
        .reshape(group_rows, 3 * head_width)
        .astype(jnp.bfloat16)
    )
    grad_qkvw = along_rows(gathered, grad_qkv)
    grad_normed = lax.psum_scatter(
        (against(grad_qkv, qkv_weight) + against(grad_pre, in_weight)).astype(jnp.bfloat16),
        "mp",
        scatter_dimension=0,
        tiled=True,
    ).astype(jnp.float32)
    grad_unit = grad_normed * ln_scale
    grad_hidden = out_grad.astype(jnp.float32) + inv_std * (
        grad_unit
        - jnp.mean(grad_unit, axis=1, keepdims=True)
        - unit_rows * jnp.mean(grad_unit * unit_rows, axis=1, keepdims=True)
    )
    scale_part = jnp.sum(grad_normed * unit_rows, axis=0)
    bias_part = jnp.sum(grad_normed, axis=0)
    grad_scale, grad_bias = lax.psum((scale_part, bias_part), ("dp", "mp"))
    grad_qkvw, grad_outw, grad_inw, grad_down = (
        lax.psum(grad_qkvw.astype(jnp.bfloat16), "dp").astype(jnp.float32),
        lax.psum(grad_outw.astype(jnp.bfloat16), "dp").astype(jnp.float32),
        lax.psum(grad_inw.astype(jnp.bfloat16), "dp").astype(jnp.float32),
        lax.psum(grad_down.astype(jnp.bfloat16), "dp").astype(jnp.float32),
    )
    devices = lax.axis_size("dp") * lax.axis_size("mp")
    counts = jnp.array(
        [
            tok_rows * model_width * devices,
            tok_rows * model_width * devices,
            tok_rows * hidden_dev * lax.axis_size("mp") * devices,
        ],
        jnp.float32,
    )
    stats = jnp.sqrt(stat_sums / counts)
    return (
        result.astype(jnp.bfloat16),
        grad_hidden,
        grad_scale,
        grad_bias,
        grad_qkvw,
        grad_outw,
        grad_inw,
        grad_down,
        stats,
    )


def solution(mesh):
    placed = (
        P(("dp", "mp"), None),
        P("dp", None),
        P(),
        P(),
        P(None, "mp"),
        P("mp", None),
        P(None, "mp"),
        P("mp", None),
        P(("dp", "mp"), None),
    )
    return jax.shard_map(
        on_device,
        mesh=mesh,
        in_specs=placed,
        out_specs=(
            P(("dp", "mp"), None),
            P(("dp", "mp"), None),
            P(),
            P(),
            P(None, "mp"),
            P("mp", None),
            P(None, "mp"),
            P("mp", None),
            P(),
        ),
        check_vma=False,
    )
```

profile of v0, /device:TPU:0, one launch (start us, length us, event | category | flops | bytes accessed | tf_op | source)
XLA Modules:
  0.0 1262.9 jit_solution(18198605747822626611)
XLA Ops:
  21.3 52.8 %all-gather.3.cloned.1.call-done = bf16[2048,1024]{1,0:T(8,128)(2,1)} async-done(((bf16[1024,1024]{1,0:T(8,128)(2,1)}), bf16[2048,1024]{1,0:T(8,128)(2,1)}) %all-gather.3.cloned.1.call-update) | async-done | bytes 4194320 | tf_op jit(solution)/shard_map/all_gather | solution.py:146
  74.1 11.4 fusion.89
  115.6 226.7 %while.28 = (s32[]{:T(128)}, bf16[8,2048,64]{1,2,0:T(8,128)(2,1)}, f32[8,2048]{1,0:T(8,128)}, s32[8,2048]{1,0:T(8,128)S(1)}, bf16[8,2048,64]{2,1,0:T(8,128)(2,1)...) while((s32[]{:T(128)}, bf16[8,2048,64]{1,2,0:T(8,128)(2,1)}, ...), condition=%wide.region_8.9_spmd.clone, body=%wide.region_5.8_spmd.sunk.clone | while | flops 1119877120 | bytes 52545620 | solution.py:156
  134.5 9.5 fusion.153
  162.9 9.5 fusion.153
  191.2 9.5 fusion.153
  219.5 9.5 fusion.153
  247.9 9.5 fusion.153
  276.2 9.5 fusion.153
  304.5 9.5 fusion.153
  332.8 9.5 fusion.153
  353.3 388.4 %while.29 = (s32[]{:T(128)}, f32[8,2048,64]{1,2,0:T(8,128)}, f32[8,2048,64]{1,2,0:T(8,128)}, bf16[8,2048,64]{1,2,0:T(8,128)(2,1)}, s32[8,2048]{1,0:T(8,128)S(1)}...) while((s32[]{:T(128)}, f32[8,2048,64]{1,2,0:T(8,128)}, ...), condition=%wide.region_12.13_spmd.clone, body=%wide.region_10.12_spmd.sunk.clone | while | flops 2734946304 | bytes 131150952 | solution.py:192
  353.5 9.3 fusion.162
  363.6 10.5 multiply_reduce_fusion.6
  374.1 10.7 multiply_convert_fusion.3
  401.9 9.3 fusion.162
  412.1 10.5 multiply_reduce_fusion.6
  422.6 10.7 multiply_convert_fusion.3
  450.4 9.3 fusion.162
  460.5 10.5 multiply_reduce_fusion.6
  471.0 10.7 multiply_convert_fusion.3
  498.9 9.3 fusion.162
  509.0 10.5 multiply_reduce_fusion.6
  519.5 10.7 multiply_convert_fusion.3
  547.4 9.3 fusion.162
  557.5 10.5 multiply_reduce_fusion.6
  568.0 10.7 multiply_convert_fusion.3
  595.8 9.3 fusion.162
  606.0 10.5 multiply_reduce_fusion.6
  616.5 10.7 multiply_convert_fusion.3
  644.3 9.3 fusion.162
  654.4 10.5 multiply_reduce_fusion.6
  664.9 10.7 multiply_convert_fusion.3
  692.8 9.3 fusion.162
  702.9 10.5 multiply_reduce_fusion.6
  713.4 10.7 multiply_convert_fusion.3
  751.2 11.4 convolution_convert_fusion
  766.2 46.8 %multiply_reduce_fusion.1 = (f32[]{:T(128)}, bf16[2048,2048]{1,0:T(8,128)(2,1)}, f32[2048,2048]{1,0:T(8,128)}) fusion(bf16[2048,1024]{1,0:T(8,128)(2,1)S(1)} %copy-done.22, bf16[1024,2048]{1,0:T(8,128)(2,1)S(1)} %copy-done.20), kind=kOutput, calls=%fused_computation.67 | convolution fusion | flops 8875147264 | bytes 33554436 | tf_op jit(solution)/shard_map/dot_general | solution.py:162
  813.0 16.3 %fusion.54 = bf16[2048,2048]{1,0:T(8,128)(2,1)S(1)} fusion(f32[2048,2048]{1,0:T(8,128)} %get-tuple-element.248, bf16[2048,1024]{1,0:T(8,128)(2,1)S(1)} %copy-done.23, bf16[2048,1024]{1,0:T(8,128)(2,1)S(1)} %copy-done.21), kind=kOutput, calls=%fused_computation.66 | convolution fusion | flops 8631877632 | bytes 33554432 | tf_op jit(solution)/shard_map/dot_general | solution.py:55
  829.4 11.1 convolution_convert_fusion.1
  840.4 12.9 %convolution_convert_fusion.2 = bf16[2048,1024]{1,0:T(8,128)(2,1)} fusion(bf16[2048,2048]{1,0:T(8,128)(2,1)} %get-tuple-element.223, bf16[2048,1024]{1,0:T(8,128)(2,1)S(1)} %copy-done.23), kind=kOutput, calls=%fused_computation.115 | convolution fusion | flops 8592031744 | bytes 16777216 | tf_op jit(solution)/shard_map/dot_general | solution.py:49
  853.3 12.8 %fusion.91 = f32[2048,1024]{1,0:T(8,128)S(1)} fusion(bf16[2048,2048]{1,0:T(8,128)(2,1)} %copy-done.26, bf16[1024,2048]{1,0:T(8,128)(2,1)} %param.20), kind=kOutput, calls=%fused_computation.160 | convolution fusion | flops 8589934592 | bytes 20971520 | tf_op jit(solution)/shard_map/dot_general | solution.py:55
  866.1 11.2 add_convert_fusion
  877.4 13.0 %fusion.90 = f32[2048,1024]{1,0:T(8,128)S(1)} fusion(bf16[2048,2048]{1,0:T(8,128)(2,1)} %get-tuple-element.223, bf16[2048,1024]{1,0:T(8,128)(2,1)} %param.21), kind=kOutput, calls=%fused_computation.159 | convolution fusion | flops 8589934592 | bytes 20971520 | tf_op jit(solution)/shard_map/dot_general | solution.py:167
  898.4 190.0 %all-reduce.4.cloned.1.call-done = (bf16[1024,1536]{1,0:T(8,128)(2,1)}, bf16[512,1024]{1,0:T(8,128)(2,1)}, bf16[1024,2048]{1,0:T(8,128)(2,1)}, bf16[2048,1024]{1,0:T(8,128)(2,1)}) async-done(((bf16[1024,1536]{1,0:T(8,128)(2,1)}, bf16[512,1024]{1,0:T(8,128)(2,1)}, bf16[1024,2048]{1,0:T(8,128)(2,1)}, bf16[2048,1024]{1,0:T(8,128)(2,1)}), (bf16[1024,1536]{1,0:T(8,128)(2,1)}, bf16[512,1024]{1,0:T(8,128)(2,1)}, ...) | async-done | bytes 12582928 | tf_op jit(solution)/shard_map/psum | solution.py:228
  1104.8 40.6 %reduce-scatter.5.cloned.1.call-done = bf16[1024,1024]{1,0:T(8,128)(2,1)} async-done(((bf16[2048,1024]{1,0:T(8,128)(2,1)}), bf16[1024,1024]{1,0:T(8,128)(2,1)}) %reduce-scatter.5.cloned.1.call-update) | async-done | bytes 2097168 | tf_op jit(solution)/shard_map/reduce_scatter | solution.py:212
  1145.5 56.6 %reduce-scatter.3.cloned.1.call-done = bf16[1024,1024]{1,0:T(8,128)(2,1)} async-done(((bf16[2048,1024]{1,0:T(8,128)(2,1)}), bf16[1024,1024]{1,0:T(8,128)(2,1)}) %reduce-scatter.3.cloned.1.call-update) | async-done | bytes 2097168 | tf_op jit(solution)/shard_map/reduce_scatter | solution.py:164
  1211.0 39.5 %all-reduce = (f32[1024]{0:T(1024)}, f32[1024]{0:T(1024)}, f32[3]{0:T(128)S(1)}) all-reduce(f32[1024]{0:T(1024)S(1)} %get-tuple-element.174, f32[1024]{0:T(1024)S(1)} %get-tuple-element.178, f32[3]{0:T(128)S(1)} %pad_maximum_fusion.1), channel_id=1, replica_groups=mesh['dp'=16,'mp'=2] {'dp','mp'}, use_global_device_ids=true, to_apply=%region_17.18 | all-reduce | flops 2051 | bytes 16408 | tf_op jit(solution)/shard_map/psum | solution.py:226
  (192 shorter events, 401.4 us)
Async XLA Ops:
  7.2 66.9 %copy-start = (bf16[1024,1536]{1,0:T(8,128)(2,1)S(1)}, bf16[1024,1536]{1,0:T(8,128)(2,1)}, u32[]{:S(2)}) copy-start(bf16[1024,1536]{1,0:T(8,128)(2,1)} %param.18) | copy-start | bytes 9437188
  7.2 5.1 copy-start.16
  7.2 5.1 copy-start.18
  7.2 66.9 %all-gather.3.cloned.1.call-start = ((), (), s32[]{:S(2)}) async-start(), calls=%async_computation.2 | async-start | bytes 6291456 | tf_op jit(solution)/shard_map/all_gather | solution.py:146
  7.3 5.1 copy-start.1
  9.4 2.4 copy-start.12
  11.7 0.6 copy-start.14
  14.5 2.4 copy-start.19
  14.5 327.8 %all-gather.5.cloned.1.call-start = ((), (), s32[]{:S(2)}) async-start(), calls=%async_computation.4 | async-start | bytes 6291456 | tf_op jit(solution)/shard_map/all_gather | solution.py:184
  15.2 1073.2 %all-reduce.4.cloned.1.call-start = ((), (), s32[]{:S(2)}) async-start(), calls=%async_computation.6 | async-start | bytes 25165824 | tf_op jit(solution)/shard_map/psum | solution.py:228
  21.3 74.3 %copy-start.9 = (f32[2048,8]{0,1:T(8,128)}, f32[2048,8]{0,1:T(8,128)S(1)}, u32[]{:S(2)}) copy-start(f32[2048,8]{0,1:T(8,128)S(1)} %get-tuple-element.247) | copy-start | bytes 196612
  741.6 4.3 copy-start.10
  741.6 4.3 copy-start.11
  747.8 1.6 copy-start.2
  751.2 11.5 copy-start.5
  751.2 11.5 copy-start.3
  751.2 11.5 copy-start.23
  762.6 3.4 copy-start.20
  762.7 3.6 copy-start.22
  766.2 46.8 %copy-start.21 = (bf16[2048,1024]{1,0:T(8,128)(2,1)S(1)}, bf16[2048,1024]{1,0:T(8,128)(2,1)}, u32[]{:S(2)}) copy-start(bf16[2048,1024]{1,0:T(8,128)(2,1)} %param.21) | copy-start | bytes 12582916
  829.3 11.1 copy-start.26
  853.3 292.2 %reduce-scatter.5.cloned.1.call-start = ((), (), s32[]{:S(2)}) async-start(), calls=%async_computation.5 | async-start | bytes 6291456 | tf_op jit(solution)/shard_map/reduce_scatter | solution.py:212
  877.4 324.7 %reduce-scatter.3.cloned.1.call-start = ((), (), s32[]{:S(2)}) async-start(), calls=%async_computation.3 | async-start | bytes 6291456 | tf_op jit(solution)/shard_map/reduce_scatter | solution.py:164
  877.4 13.1 %copy-start.4 = (bf16[8,2048,64]{1,2,0:T(8,128)(2,1)S(1)}, bf16[8,2048,64]{1,2,0:T(8,128)(2,1)}, u32[]{:S(2)}) copy-start(bf16[8,2048,64]{1,2,0:T(8,128)(2,1)} %get-tuple-element.101) | copy-start | bytes 6291460
  877.4 13.1 %copy-start.24 = (bf16[512,1024]{1,0:T(8,128)(2,1)S(1)}, bf16[512,1024]{1,0:T(8,128)(2,1)}, u32[]{:S(2)}) copy-start(bf16[512,1024]{1,0:T(8,128)(2,1)} %param.19) | copy-start | bytes 3145732
  1088.4 6.8 copy-start.6
  1095.2 4.5 copy-start.7
  1099.7 3.6 copy-start.8
  1099.7 102.4 %copy-start.13 = (f32[1024]{0:T(1024)S(1)}, f32[1024]{0:T(1024)}, u32[]{:S(2)}) copy-start(f32[1024]{0:T(1024)} %copy-done.12) | copy-start | bytes 12292
  1099.7 102.4 %copy-start.15 = (f32[1024]{0:T(1024)S(1)}, f32[1024]{0:T(1024)}, u32[]{:S(2)}) copy-start(f32[1024]{0:T(1024)} %copy-done.14) | copy-start | bytes 12292
  1099.7 102.4 %copy-start.17 = (f32[1024]{0:T(1024)S(1)}, f32[1024]{0:T(1024)}, u32[]{:S(2)}) copy-start(f32[1024]{0:T(1024)} %param.16) | copy-start | bytes 12292
  1104.8 145.6 %copy-start.25 = (f32[3]{0:T(128)S(1)}, f32[3]{0:T(128)}, u32[]{:S(2)}) copy-start(f32[3]{0:T(128)} %constant.136) | copy-start | bytes 40
Sparse Core Ops, SparseCore 0:
  14.6 59.4 all-gather.2
  75.6 56.7 all-gather.4
  853.4 234.9 all-reduce.3
  1091.1 54.2 reduce-scatter.4
  1147.7 54.3 reduce-scatter.2
where the time goes:
time: 1270 us; the launch traced here: 1260 us
  matrix products  606 us (48%)
  waiting for transfers between devices  341 us (27%)
  other arithmetic  202 us (16%)
  local copies, waits for them, and re-layouts  59 us (5%)
  blocking collectives  39.5 us (3%)
  between operations  14.6 us (1%)
    dot_general x28, matrix products, against(): lax.dot_general(left_side, right_side, (((1,), (1,)), ((), ())), preferre...  278 us
    psum x1, waiting for transfers between devices, on_device(): lax.psum(grad_qkvw.astype(jnp.bfloat16), 'dp').astype(jnp.float32)  190 us
    dot_general x20, matrix products, along_rows(): lax.dot_general(left_side, right_side, (((0,), (0,)), ((), ())), preferre...  129 us
    convert_element_type x8, other arithmetic, attend_backward(): grad_scores = (attn_prob * (grad_prob - jnp.sum(attn_prob * grad_prob, ax...  85.7 us
    dot_general x8, matrix products, attend_forward(): context = jnp.dot(attn_prob, values, preferred_element_type=jnp.float32)  76.1 us
    reduce_sum x8, other arithmetic, attend_forward(): row_total = jnp.sum(weight, axis=1, keepdims=True)  64.6 us
    reduce_scatter x1, waiting for transfers between devices, on_device(): lax.psum_scatter((jnp.dot(context, out_weight, preferred_element_type=jnp...  56.6 us
    all_gather x1, waiting for transfers between devices, on_device(): gathered = lax.all_gather(normed, 'mp', axis=0, tiled=True)  52.8 us
  transfers between devices with their start and end apart: 5, of which 4 were waited for; matrix products, arithmetic and copies ran while one was open for 27% of the time, Pallas kernels for 0%

commit v1 on v0

v1 whole, which is shorter than its diff:
```python
import functools

import jax
import jax.numpy as jnp
from jax import lax
from jax.experimental import pallas as pl
from jax.experimental.pallas import tpu as pltpu
from jax.sharding import PartitionSpec as P

HEAD = 64
ROT = 16
LANES = 128
TILE = 256
F32 = jnp.float32
BF = jnp.bfloat16

epsilon = 1e-05
rope_base = 10000.0
excluded = -1e20


def nn(a, b):
    return jnp.dot(a, b, preferred_element_type=F32)


def nt(a, b):
    return lax.dot_general(a, b, (((1,), (1,)), ((), ())), preferred_element_type=F32)


def tn(a, b):
    return lax.dot_general(a, b, (((0,), (0,)), ((), ())), preferred_element_type=F32)


def whole(shape):
    zeros = (0,) * len(shape)
    return pl.BlockSpec(shape, lambda *_: zeros, pipeline_mode=pl.Buffered(1))


def struct(shape, dtype):
    return jax.ShapeDtypeStruct(shape, dtype)


def cost(flops, nbytes, trans=0):
    return pl.CostEstimate(flops=int(flops), bytes_accessed=int(nbytes), transcendentals=int(trans))


def params(**kw):
    return pltpu.CompilerParams(vmem_limit_bytes=60 * 2**20, **kw)


def lane_ids(rows):
    return lax.broadcasted_iota(jnp.int32, (rows, LANES), 1)


def turn(x, cos, fwd, back):
    return x * cos + pltpu.roll(x, LANES - ROT // 2, 1) * fwd + pltpu.roll(x, ROT // 2, 1) * back


def gelu_parts(v):
    x = jnp.abs(v)
    bell = jnp.exp(v * v * (-0.5))
    t = 1.0 / (1.0 + x * (0.3275911 * 0.7071067811865476))
    poly = t * (
        0.254829592
        + t * (-0.284496736 + t * (1.421413741 + t * (-1.453152027 + t * 1.061405429)))
    )
    tail = 0.5 * poly * bell
    cdf = jnp.where(v >= 0, 1.0 - tail, tail)
    return v * cdf, cdf + v * bell * 0.3989422804014327


def project_kernel(
    pos, nrm, wqkv, win, cos, fwd, back, hot, neg, *rest
):
    q_out, k_out, v_out, act, slope, sq = rest[-6:]
    rows = nrm.shape[0]
    lane = lane_ids(rows)
    low = lane < HEAD
    x = nrm[...]
    c, f, b = cos[...], fwd[...], back[...]
    for p in range(wqkv.shape[1] // 384):
        y = nn(x, wqkv[:, p * 384 : (p + 1) * 384])
        g0, g1, g2 = y[:, :128], y[:, 128:256], y[:, 256:]
        r1, r2 = pltpu.roll(g1, HEAD, 1), pltpu.roll(g2, HEAD, 1)
        for h, (qk, v) in enumerate(((g0, g1), (jnp.where(low, r1, r2), r2))):
            qk = turn(qk, c, f, b)
            q_out[2 * p + h] = jnp.where(low, qk * HEAD**-0.5, hot[...].astype(F32)).astype(BF)
            k_out[2 * p + h] = jnp.where(low, pltpu.roll(qk, HEAD, 1), neg[...].astype(F32)).astype(BF)
            v_out[2 * p + h] = jnp.where(low, v, jnp.where(lane < HEAD + 2, 1.0, 0.0)).astype(BF)

    @pl.when(pl.program_id(0) == 0)
    def _():
        sq[...] = jnp.zeros_like(sq)

    step = min(512, win.shape[1])
    for j in range(win.shape[1] // step):
        cols = pl.ds(j * step, step)
        a, s = gelu_parts(nn(x, win[:, cols]))
        a = a.astype(BF)
        act[:, cols] = a
        slope[:, cols] = s.astype(BF)
        wide = a.astype(F32)
        sq[...] += jnp.sum((wide * wide).reshape(-1, 8, LANES), axis=0) if False else sum(
            jnp.sum(
                (wide[:, i * LANES : (i + 1) * LANES] ** 2).reshape(rows // 8, 8, LANES), axis=0
            )
            for i in range(step // LANES)
        )


def project(pos, total, heads, prior, nrm, wqkv, win, cos, fwd, back, hot, neg):
    rows, d = nrm.shape
    f = win.shape[1]
    row = lambda w: pl.BlockSpec((TILE, w), lambda i, pos: (i, 0))
    at = lambda w: pl.BlockSpec((TILE, w), lambda i, pos: (pos[0] + i, 0))
    hd = pl.BlockSpec((heads, TILE, LANES), lambda i, pos: (0, pos[0] + i, 0))
    any_ = pl.BlockSpec(memory_space=pl.ANY)
    big = struct((heads, total, LANES), BF)
    return pl.pallas_call(
        project_kernel,
        grid_spec=pltpu.PrefetchScalarGridSpec(
            num_scalar_prefetch=1,
            grid=(rows // TILE,),
            in_specs=[row(d), whole(wqkv.shape), whole(win.shape), at(LANES), at(LANES), at(LANES), at(LANES), at(LANES)]
            + [any_] * len(prior),
            out_specs=[hd, hd, hd, row(f), row(f), pl.BlockSpec((8, LANES), lambda i, pos: (0, 0))],
        ),
        out_shape=[big, big, big, struct((rows, f), BF), struct((rows, f), BF), struct((8, LANES), F32)],
        input_output_aliases={9 + i: i for i in range(len(prior))},
        compiler_params=params(),
        cost_estimate=cost(2 * rows * d * (f + wqkv.shape[1]), 2 * (d * (f + wqkv.shape[1]) + 6 * rows * d)),
        name="project",
    )(pos, nrm, wqkv, win, cos, fwd, back, hot, neg, *prior)


def cotangent_kernel(pos, dy, wout, wdown, slope, *rest):
    do_out, gpre = rest[-2:]
    x = dy[...]
    low = lane_ids(x.shape[0]) < HEAD
    g = nt(x, wout[...])
    for p in range(g.shape[1] // LANES):
        y = g[:, p * LANES : (p + 1) * LANES]
        do_out[2 * p] = jnp.where(low, y, 0.0).astype(BF)
        do_out[2 * p + 1] = jnp.where(low, pltpu.roll(y, HEAD, 1), 0.0).astype(BF)
    f = wdown.shape[0]
    step = min(512, f)
    for j in range(f // step):
        cols = pl.ds(j * step, step)
        gpre[:, cols] = (nt(x, wdown[cols, :]) * slope[:, cols].astype(F32)).astype(BF)


def cotangent(pos, total, heads, prior, dy, wout, wdown, slope):
    rows, d = dy.shape
    f = wdown.shape[0]
    row = lambda w: pl.BlockSpec((TILE, w), lambda i, pos: (i, 0))
    hd = pl.BlockSpec((heads, TILE, LANES), lambda i, pos: (0, pos[0] + i, 0))
    return pl.pallas_call(
        cotangent_kernel,
        grid_spec=pltpu.PrefetchScalarGridSpec(
            num_scalar_prefetch=1,
            grid=(rows // TILE,),
            in_specs=[row(d), whole(wout.shape), whole(wdown.shape), row(f)]
            + [pl.BlockSpec(memory_space=pl.ANY)] * len(prior),
            out_specs=[hd, row(f)],
        ),
        out_shape=[struct((heads, total, LANES), BF), struct((rows, f), BF)],
        input_output_aliases={5 + i: i for i in range(len(prior))},
        compiler_params=params(),
        cost_estimate=cost(2 * rows * d * (f + wout.shape[0]), 2 * (d * (f + wout.shape[0]) + 5 * rows * d)),
        name="cotangent",
    )(pos, dy, wout, wdown, slope, *prior)


def attend_kernel(q_ref, k_ref, v_ref, ctx, wide, keep, sq):
    h = pl.program_id(1)
    total = q_ref.shape[1]
    b = TILE
    tri = lax.broadcasted_iota(jnp.int32, (b, b), 0) >= lax.broadcasted_iota(jnp.int32, (b, b), 1)
    low = lane_ids(b) < HEAD

    @pl.when((h == 0) & (pl.program_id(0) == 0))
    def _():
        sq[...] = jnp.zeros_like(sq)

    for i in range(total // b):
        n = (i + 1) * b
        rows = pl.ds(i * b, b)
        s = nt(q_ref[0, rows, :], k_ref[0, :n, :])
        s_diag = jnp.where(tri, s[:, n - b :], excluded)
        top = jnp.max(s_diag, axis=1, keepdims=True)
        if i:
            top = jnp.maximum(top, jnp.max(s[:, : n - b], axis=1, keepdims=True))
        w = jnp.exp(s_diag - top).astype(BF)
        if i:
            w = jnp.concatenate([jnp.exp(s[:, : n - b] - top).astype(BF), w], axis=1)
        for j in range(i + 1):
            keep[0, i * (i + 1) // 2 + j] = w[:, j * b : (j + 1) * b]
        acc = nn(w, v_ref[0, :n, :])
        inv = 1.0 / acc[:, HEAD : HEAD + 1]
        acc = acc * inv
        wide[0, rows, :] = jnp.where(low, acc, inv)
        out = acc.astype(BF)
        real = jnp.where(low, out.astype(F32), 0.0)
        sq[...] += jnp.sum((real * real).reshape(b // 8, 8, LANES), axis=0)

        @pl.when(h == 0)
        def _():
            ctx[rows, :] = out

        @pl.when(h == 1)
        def _():
            both = jnp.where(low, ctx[rows, :].astype(F32), pltpu.roll(out.astype(F32), HEAD, 1))
            ctx[rows, :] = both.astype(BF)


def attend(q, k, v):
    heads, total, _ = q.shape
    tiles = total // TILE
    tiles = tiles * (tiles + 1) // 2
    hd = pl.BlockSpec((1, total, LANES), lambda p, h: (2 * p + h, 0, 0))
    return pl.pallas_call(
        attend_kernel,
        grid=(heads // 2, 2),
        in_specs=[hd, hd, hd],
        out_specs=[
            pl.BlockSpec((total, LANES), lambda p, h: (0, p)),
            hd,
            pl.BlockSpec((1, tiles, TILE, TILE), lambda p, h: (2 * p + h, 0, 0, 0)),
            pl.BlockSpec((8, LANES), lambda p, h: (0, 0)),
        ],
        out_shape=[
            struct((total, heads * HEAD), BF),
            struct((heads, total, LANES), F32),
            struct((heads, tiles, TILE, TILE), BF),
            struct((8, LANES), F32),
        ],
        compiler_params=params(),
        cost_estimate=cost(4 * heads * tiles * TILE * TILE * 256, heads * total * LANES * 20, heads * tiles * TILE * TILE),
        name="attend",
    )(q, k, v)


def attend_back_kernel(q_ref, k_ref, v_ref, do_ref, wide, keep, cos, fwd, back, out, dk_acc, dv_acc, dq_acc, hold):
    h = pl.program_id(1)
    total = q_ref.shape[1]
    b = TILE
    lane = lane_ids(b)
    low = lane < HEAD
    dk_acc[...] = jnp.zeros_like(dk_acc)
    dv_acc[...] = jnp.zeros_like(dv_acc)
    for i in range(total // b):
        n = (i + 1) * b
        rows = pl.ds(i * b, b)
        q = q_ref[0, rows, :]
        w = [keep[0, i * (i + 1) // 2 + j] for j in range(i + 1)]
        w = w[0] if i == 0 else jnp.concatenate(w, axis=1)
        context = wide[0, rows, :]
        inv = context[:, HEAD : HEAD + 1]
        scaled = (do_ref[0, rows, :].astype(F32) * inv).astype(BF)
        grad = scaled.astype(F32)
        delta = jnp.sum(jnp.where(low, grad * context, 0.0), axis=1, keepdims=True)
        delta_hi = delta.astype(BF).astype(F32)
        delta_lo = delta - delta_hi
        joined = jnp.where(lane == HEAD, -delta_hi, jnp.where(lane == HEAD + 1, -delta_lo, grad)).astype(BF)
        ds = w * nt(joined, v_ref[0, :n, :]).astype(BF)
        dq_acc[rows, :] = nn(ds, k_ref[0, :n, :]) * HEAD**-0.5
        dk_acc[:n, :] += tn(ds, q)
        dv_acc[:n, :] += tn(w, scaled)
    for i in range(total // b):
        rows = pl.ds(i * b, b)
        x = jnp.where(low, dq_acc[rows, :], pltpu.roll(dk_acc[rows, :], HEAD, 1))
        x = turn(x, cos[rows, :], -fwd[rows, :], -back[rows, :])
        dv = dv_acc[rows, :]

        @pl.when(h == 0)
        def _():
            out[rows, :LANES] = x.astype(BF)
            hold[rows, :] = dv

        @pl.when(h == 1)
        def _():
            r = pltpu.roll(x, HEAD, 1)
            out[rows, LANES : 2 * LANES] = jnp.where(low, hold[rows, :], r).astype(BF)
            out[rows, 2 * LANES :] = jnp.where(low, r, pltpu.roll(dv, HEAD, 1)).astype(BF)


def attend_back(q, k, v, do, wide, keep, cos, fwd, back):
    heads, total, _ = q.shape
    hd = pl.BlockSpec((1, total, LANES), lambda p, h: (2 * p + h, 0, 0))
    acc = pltpu.VMEM((total, LANES), F32)
    tiles = keep.shape[1]
    return pl.pallas_call(
        attend_back_kernel,
        grid=(heads // 2, 2),
        in_specs=[hd, hd, hd, hd, hd, pl.BlockSpec((1,) + keep.shape[1:], lambda p, h: (2 * p + h, 0, 0, 0))]
        + [whole(cos.shape)] * 3,
        out_specs=pl.BlockSpec((total, 384), lambda p, h: (0, p)),
        out_shape=struct((total, heads * 3 * HEAD), BF),
        scratch_shapes=[acc] * 4,
        compiler_params=params(),
        cost_estimate=cost(8 * heads * tiles * TILE * TILE * 256, heads * total * LANES * 40),
        name="attend_back",
    )(q, k, v, do, wide, keep, cos, fwd, back)


def pair_kernel(transposed, pos, a, b, c, d, out):
    dot = nt if transposed else nn
    out[...] = (dot(a[...], b[...]) + dot(c[...], d[...])).astype(BF)


def pair_matmul(pos, transposed, a, b, c, d):
    rows = c.shape[0]
    width = b.shape[0] if transposed else b.shape[1]
    return pl.pallas_call(
        functools.partial(pair_kernel, transposed),
        grid_spec=pltpu.PrefetchScalarGridSpec(
            num_scalar_prefetch=1,
            grid=(rows // TILE,),
            in_specs=[
                pl.BlockSpec((TILE, a.shape[1]), lambda i, pos: (pos[0] + i, 0)),
                whole(b.shape),
                pl.BlockSpec((TILE, c.shape[1]), lambda i, pos: (i, 0)),
                whole(d.shape),
            ],
            out_specs=pl.BlockSpec((TILE, width), lambda i, pos: (i, 0)),
        ),
        out_shape=struct((rows, width), BF),
        compiler_params=params(),
        cost_estimate=cost(2 * rows * width * (a.shape[1] + c.shape[1]), 2 * (b.size + d.size + rows * (width + a.shape[1] + c.shape[1]))),
        name="pair_matmul",
    )(pos, a, b, c, d)


def weight_kernel(n, slots, *refs):
    xs, ys, out = refs[:n], refs[n : 2 * n], refs[2 * n]
    d = out.shape[1]
    for c in range(d // 512):
        cols = pl.ds(c * 512, 512)
        out[:, cols] = sum(tn(x[...], y[:, cols]) for x, y in zip(xs, ys)).astype(BF)


def weight_grad(slots, xs, ys, tile=256):
    n = len(ys)
    rows, d = ys[0].shape
    if len(xs) == n and n > 1 or xs[0].shape[0] == rows:
        specs = [pl.BlockSpec((rows, tile), lambda j, slots: (0, j)) for _ in xs]
    else:
        specs = [
            pl.BlockSpec((rows, tile), functools.partial(lambda s, j, slots: (slots[s], j), s))
            for s in range(n)
        ]
        xs = list(xs) * n
    width = xs[0].shape[1]
    return pl.pallas_call(
        functools.partial(weight_kernel, n),
        grid_spec=pltpu.PrefetchScalarGridSpec(
            num_scalar_prefetch=1,
            grid=(width // tile,),
            in_specs=specs + [whole(y.shape) for y in ys],
            out_specs=pl.BlockSpec((tile, d), lambda j, slots: (j, 0)),
        ),
        out_shape=struct((width, d), BF),
        compiler_params=params(),
        cost_estimate=cost(2 * n * rows * d * width, 2 * (n * rows * (d + width) + d * width)),
        name="weight_grad",
    )(slots, *xs, *ys)


def layout(lengths, group_rows):
    seg_ends = jnp.cumsum(lengths)
    positions = jnp.arange(group_rows, dtype=jnp.int32)
    closed = seg_ends[None, :] <= positions[:, None]
    segment = jnp.sum(closed.astype(jnp.int32), axis=1)
    seg_start = jnp.sum(jnp.where(closed, lengths[None, :], 0), axis=1)
    return segment, positions - seg_start


def tables(lengths, group_rows):
    half = ROT // 2
    segment, offset = layout(lengths, group_rows)
    inv_freq = jnp.power(rope_base, -2.0 * jnp.arange(half, dtype=F32) / ROT)
    angles = offset.astype(F32)[:, None] * inv_freq[None, :]
    cos, sin = jnp.cos(angles), jnp.sin(angles)
    ones = jnp.ones((group_rows, HEAD - ROT), F32)
    none = jnp.zeros_like(ones)
    flat = jnp.zeros_like(sin)
    double = lambda parts: jnp.concatenate(parts + parts, axis=1)
    lane = jnp.arange(LANES)[None, :] - HEAD
    same = segment[:, None] == lane
    hot = jnp.where(same, 1.0, 0.0).astype(BF)
    neg = jnp.where(same | (lane < 0) | (lane >= lengths.shape[0]), 0.0, excluded).astype(BF)
    return double([cos, cos, ones]), double([-sin, flat, none]), double([flat, sin, none]), hot, neg


def on_device(hidden_in, seq_lengths, ln_scale, ln_bias, wqkv, wout, win, wdown, out_grad):
    rows, d = hidden_in.shape
    n = lax.axis_size("mp")
    me = lax.axis_index("mp")
    total = rows * n
    heads = wout.shape[0] // HEAD
    f = win.shape[1]
    cos, fwd, back, hot, neg = tables(seq_lengths[0], total)

    residual = hidden_in.astype(F32)
    row_mean = jnp.mean(residual, axis=1, keepdims=True)
    centred = residual - row_mean
    row_var = jnp.mean(centred * centred, axis=1, keepdims=True)
    inv_std = lax.rsqrt(row_var + epsilon)
    unit = centred * inv_std
    normed = (unit * ln_scale + ln_bias).astype(BF)

    ring = lambda s: [((i + s) % n, i) for i in range(n)]
    nrm = [normed] + [lax.ppermute(normed, "mp", ring(s)) for s in range(1, n)]
    dys = [out_grad] + [lax.ppermute(out_grad, "mp", ring(s)) for s in range(1, n)]
    slots = jnp.stack([(me + s) % n for s in range(n)]).astype(jnp.int32)
    pos = [(slots[s : s + 1] * (rows // TILE)).astype(jnp.int32) for s in range(n)]

    qkv, do = [], []
    acts, gpres, act_sq = [], [], 0.0
    slopes = []
    for s in range(n):
        *qkv, a, sl, sq = project(pos[s], total, heads, qkv, nrm[s], wqkv, win, cos, fwd, back, hot, neg)
        acts.append(a)
        slopes.append(sl)
        act_sq = act_sq + jnp.sum(sq)
    context, wide, keep, ctx_sq = attend(*qkv)
    for s in range(n):
        *do, g = cotangent(pos[s], total, heads, do, dys[s], wout, wdown, slopes[s])
        gpres.append(g)
    update = None
    others = [
        lax.ppermute(pair_matmul(pos[s], False, context, wout, acts[s], wdown), "mp", ring(n - s))
        for s in range(1, n)
    ]
    update = pair_matmul(pos[0], False, context, wout, acts[0], wdown).astype(F32)
    for o in others:
        update = update + o.astype(F32)
    gdown = weight_grad(slots, acts, dys)
    gin = weight_grad(slots, gpres, nrm)
    gdown, gin = lax.psum((gdown, gin), "dp")
    gqkv = attend_back(*qkv, do[0], wide, keep, cos, fwd, back)
    backs = [
        lax.ppermute(pair_matmul(pos[s], True, gqkv, wqkv, gpres[s], win), "mp", ring(n - s))
        for s in range(1, n)
    ]
    grad_normed = pair_matmul(pos[0], True, gqkv, wqkv, gpres[0], win).astype(F32)
    gqw = weight_grad(slots, [gqkv], nrm)
    gow = weight_grad(slots, [context], dys)
    gqw, gow = lax.psum((gqw, gow), "dp")
    for o in backs:
        grad_normed = grad_normed + o.astype(F32)

    result = residual + update
    grad_unit = grad_normed * ln_scale
    grad_hidden = out_grad.astype(F32) + inv_std * (
        grad_unit
        - jnp.mean(grad_unit, axis=1, keepdims=True)
        - unit * jnp.mean(grad_unit * unit, axis=1, keepdims=True)
    )
    devices = lax.axis_size("dp") * n
    sums = lax.psum(
        (
            jnp.sum(grad_normed * unit, axis=0),
            jnp.sum(grad_normed, axis=0),
            jnp.stack([jnp.sum(result * result), jnp.sum(ctx_sq), act_sq]),
        ),
        ("dp", "mp"),
    )
    counts = jnp.array([rows * d * devices, rows * d * devices, rows * f * n * devices], F32)
    return (
        result.astype(BF),
        grad_hidden,
        sums[0],
        sums[1],
        gqw.T.astype(F32),
        gow.astype(F32),
        gin.T.astype(F32),
        gdown.astype(F32),
        jnp.sqrt(sums[2] / counts),
    )


def solution(mesh):
    tok = P(("dp", "mp"), None)
    cols, rows = P(None, "mp"), P("mp", None)
    return jax.shard_map(
        on_device,
        mesh=mesh,
        in_specs=(tok, P("dp", None), P(), P(), cols, rows, cols, rows, tok),
        out_specs=(tok, tok, P(), P(), cols, rows, cols, rows, P()),
        check_vma=False,
    )
```

time: 1270 us -> 559 us (0.44)
  matrix products: 606 us -> 0 us
  Pallas kernels: 0 us -> 294 us
  waiting for transfers between devices: 341 us -> 129 us
  other arithmetic: 202 us -> 39.4 us
  local copies, waits for them, and re-layouts: 59 us -> 24.8 us
    dot_general x68 -> x0, matrix products: 606 us -> none  [the longest x28 278 us: against(): lax.dot_general(left_side, right_side, (((1,), (1,)), ((), ())), preferre...]
    pallas_call x0 -> x14, Pallas kernels: none -> 294 us  [the longest x1 71.8 us: attend_back(): pl.pallas_call(attend_back_kernel, grid=(heads // 2, 2), in_specs=[hd, hd...]
    psum x1, waiting for transfers between devices: 190 us -> 65 us  [on_device(): gqw, gow = lax.psum((gqw, gow), 'dp')]
    reduce_scatter x2 -> x0, waiting for transfers between devices: 97.2 us -> none  [the longest x1 56.6 us: on_device(): lax.psum_scatter((jnp.dot(context, out_weight, preferred_element_type=jnp...]
    convert_element_type x14 -> x5, other arithmetic: 104 us -> 11.6 us  [the longest x1 6.63 us: on_device(): gdown.astype(F32)]
    reduce_sum x11 -> x5, other arithmetic: 74.9 us -> 9.88 us  [the longest x1 7.97 us: on_device(): jnp.sum(grad_normed * unit, axis=0)]
    ppermute x0 -> x4, waiting for transfers between devices: none -> 63.6 us  [the longest x1 43.2 us: on_device(): lax.ppermute(pair_matmul(pos[s], False, context, wout, acts[s], wdown), '...]
    all_gather x2 -> x0, waiting for transfers between devices: 52.8 us -> none  [the longest x1 52.8 us: on_device(): gathered = lax.all_gather(normed, 'mp', axis=0, tiled=True)]
  transfers between devices with their start and end apart: 5 -> 5, of which waited for: 4 -> 3; matrix products, arithmetic and copies ran while one was open for 27% -> 7% of each run, Pallas kernels for 0% -> 30%
where the time goes in v1:
time: 559 us; the launch traced here: 550 us
  Pallas kernels  294 us (53%)
  waiting for transfers between devices  129 us (23%)
  blocking collectives  42.1 us (8%)
  other arithmetic  39.4 us (7%)
  local copies, waits for them, and re-layouts  24.8 us (4%)
  between operations  16 us (3%)
    pallas_call x1, Pallas kernels, attend_back(): pl.pallas_call(attend_back_kernel, grid=(heads // 2, 2), in_specs=[hd, hd...  71.8 us
    psum x1, waiting for transfers between devices, on_device(): gqw, gow = lax.psum((gqw, gow), 'dp')  65 us
    pallas_call x1, Pallas kernels, attend(): pl.pallas_call(attend_kernel, grid=(heads // 2, 2), in_specs=[hd, hd, hd]...  55.6 us
    pallas_call x2, Pallas kernels, project(): pl.pallas_call(project_kernel, grid_spec=pltpu.PrefetchScalarGridSpec(num...  49.8 us
    pallas_call x4, Pallas kernels, weight_grad(): pl.pallas_call(functools.partial(weight_kernel, n), grid_spec=pltpu.Prefe...  48.3 us
    pallas_call x4, Pallas kernels, pair_matmul(): pl.pallas_call(functools.partial(pair_kernel, transposed), grid_spec=pltp...  46.7 us
    ppermute x1, waiting for transfers between devices, on_device(): lax.ppermute(pair_matmul(pos[s], False, context, wout, acts[s], wdown), '...  43.2 us
    psum x1, blocking collectives, on_device(): lax.psum((jnp.sum(grad_normed * unit, axis=0), jnp.sum(grad_normed, axis=...  42.1 us
  transfers between devices with their start and end apart: 5, of which 3 were waited for; matrix products, arithmetic and copies ran while one was open for 7% of the time, Pallas kernels for 30%

profile of v1, /device:TPU:0, one launch (start us, length us, event | category | flops | bytes accessed | tf_op | source)
XLA Modules:
  0.0 550.3 jit_solution(13924360427849252960)
XLA Ops:
  7.2 0.0 all-reduce.4.cloned.1.call-start
  7.3 2.1 convert_reduce_fusion
  9.4 2.3 fusion.13
  11.7 2.1 fusion.7.nrm.refs_2_
  13.8 2.9 collective-permute-start
  16.8 0.1 collective-permute-start.2
  16.9 0.2 reduce-window.8
  17.0 0.1 convert_reduce_fusion.1
  17.2 5.5 %multiply_sine_fusion = (f32[2048,8]{1,0:T(8,128)}, f32[2048,8]{1,0:T(8,128)}, f32[2048,8]{1,0:T(8,128)S(1)}) fusion(f32[2048]{0:T(1024)S(1)} %subtract_convert_fusion, f32[8]{0:T(128)S(1)} %multiply_power_fusion), kind=kLoop, calls=%fused_computation.23 | loop fusion | flops 32768 | bytes 204832 | tf_op jit(solution)/shard_map/sin | solution.py:383
  22.7 0.1 broadcast_in_dim.52
  22.8 0.1 broadcast_in_dim.53
  22.9 4.4 concatenate.10.fwd
  27.3 4.5 concatenate.11.back
  31.8 0.1 broadcast_in_dim.51
  31.9 3.0 concatenate.9.cos
  34.9 0.7 pad_add_fusion.slots
  35.6 1.3 select_convert_fusion
  36.8 24.8 %project.2 = (bf16[8,2048,128]{2,1,0:T(8,128)(2,1)}, bf16[8,2048,128]{2,1,0:T(8,128)(2,1)}, bf16[8,2048,128]{2,1,0:T(8,128)(2,1)}, bf16[1024,2048]{1,0:T(8,128)(...) custom-call(s32[1]{0:T(128)S(6)} %mul.69.pos, bf16[1024,1024]{1,0:T(8,128)(2,1)} %fusion.7.nrm.refs_2_, ...), custom_call_target="tpu_custom_call" | custom-call | flops 7516192768 | bytes 19922944 | tf_op jit(solution)/shard_map/project/pallas_call | solution.py:119
  61.6 11.0 %cotangent.2 = (bf16[8,2048,128]{2,1,0:T(8,128)(2,1)}, bf16[1024,2048]{1,0:T(8,128)(2,1)}) custom-call(s32[1]{0:T(128)S(6)} %mul.69.pos, bf16[1024,1024]{1,0:T(8,128)(2,1)} %refs_2_.3, bf16[512,1024]{1,0:T(8,128)(2,1)} %wout.3, bf16[2048,1024]{1,0:T(8,128)(2,1)} %wdown.3, bf16[1024,2048]{1,0:T(8,128)(2,1)} %get-tuple-element.39.slope), custom_call_target="tpu_custom_call" | custom-call | flops 5368709120 | bytes 15728640 | tf_op jit(solution)/shard_map/cotangent/pallas_call | solution.py:157
  72.6 25.0 %project.3 = (bf16[8,2048,128]{2,1,0:T(8,128)(2,1)}, bf16[8,2048,128]{2,1,0:T(8,128)(2,1)}, bf16[8,2048,128]{2,1,0:T(8,128)(2,1)}, bf16[1024,2048]{1,0:T(8,128)(...) custom-call(s32[1]{0:T(128)S(6)} %mul.70.pos, ...), custom_call_target="tpu_custom_call", output_to_operand_aliasing={{0}: (9, {}), {1}: (10, {}), {2}: (11, {})} | custom-call | flops 7516192768 | bytes 19922944 | tf_op jit(solution)/shard_map/project/pallas_call | solution.py:119
  97.6 55.6 %attend.1 = (bf16[2048,512]{1,0:T(8,128)(2,1)}, f32[8,2048,128]{2,1,0:T(8,128)}, bf16[8,36,256,256]{3,2,1,0:T(8,128)(2,1)}, f32[8,128]{1,0:T(8,128)}) custom-call(bf16[8,2048,128]{2,1,0:T(8,128)(2,1)} %get-tuple-element.32.q_ref, bf16[8,2048,128]{2,1,0:T(8,128)(2,1)} %get-tuple-element.33.k_ref, bf16[8,2048,128]{2,1,0:T(8,128)(2,1)} %get-tuple-element.34.v_ref), custom_call_target="tpu_custom_call" | custom-call | flops 19327352832 | bytes 41943040 | tf_op jit(solution)/shard_map/attend/pallas_call | solution.py:221
  153.2 11.0 %cotangent.3 = (bf16[8,2048,128]{2,1,0:T(8,128)(2,1)}, bf16[1024,2048]{1,0:T(8,128)(2,1)}) custom-call(s32[1]{0:T(128)S(6)} %mul.70.pos, bf16[1024,1024]{1,0:T(8,128)(2,1)} %collective-permute-done.2.dy.refs_3_, bf16[512,1024]{1,0:T(8,128)(2,1)} %wout.3, bf16[2048,1024]{1,0:T(8,128)(2,1)} %wdown.3, ...), custom_call_target="tpu_custom_call", output_to_operand_aliasing={{0}: (5, {})} | custom-call | flops 5368709120 | bytes 15728640 | tf_op jit(solution)/shard_map/cotangent/pallas_call | solution.py:157
  164.2 71.8 %attend_back.1.a.refs_0_.refs_1_ = bf16[2048,1536]{1,0:T(8,128)(2,1)} custom-call(bf16[8,2048,128]{2,1,0:T(8,128)(2,1)} %get-tuple-element.32.q_ref, bf16[8,2048,128]{2,1,0:T(8,128)(2,1)} %get-tuple-element.33.k_ref, bf16[8,2048,128]{2,1,0:T(8,128)(2,1)} %get-tuple-element.34.v_ref, bf16[8,2048,128]{2,1,0:T(8,128)(2,1)} %get-tuple-element.41.do_ref, ...), custom_call_target="tpu_custom_call" | custom-call | flops 38654705664 | bytes 83886080 | tf_op jit(solution)/shard_map/attend_back/pallas_call | solution.py:292
  236.0 12.1 %weight_grad.4 = bf16[1536,1024]{1,0:T(8,128)(2,1)} custom-call(s32[2]{0:T(128)} %pad_add_fusion.slots, bf16[2048,1536]{1,0:T(8,128)(2,1)} %attend_back.1.a.refs_0_.refs_1_, bf16[2048,1536]{1,0:T(8,128)(2,1)} %attend_back.1.a.refs_0_.refs_1_, bf16[1024,1024]{1,0:T(8,128)(2,1)} %fusion.7.nrm.refs_2_, bf16[1024,1024]{1,0:T(8,128)(2,1)} %collective-permute-done.nrm.refs_3_), custom_call_target="tpu_custom_call" | custom-call | flops 6442450944 | bytes 13631488 | tf_op jit(solution)/shard_map/weight_grad/pallas_call | solution.py:354
  248.1 6.7 %weight_grad.5 = bf16[512,1024]{1,0:T(8,128)(2,1)} custom-call(s32[2]{0:T(128)} %pad_add_fusion.slots, bf16[2048,512]{1,0:T(8,128)(2,1)} %get-tuple-element.35.a.refs_0_.refs_1_, bf16[2048,512]{1,0:T(8,128)(2,1)} %get-tuple-element.35.a.refs_0_.refs_1_, bf16[1024,1024]{1,0:T(8,128)(2,1)} %refs_2_.3, bf16[1024,1024]{1,0:T(8,128)(2,1)} %collective-permute-done.2.dy.refs_3_), custom_call_target="tpu_custom_call" | custom-call | flops 2147483648 | bytes 7340032 | tf_op jit(solution)/shard_map/weight_grad/pallas_call | solution.py:354
  254.8 14.8 %weight_grad.6 = bf16[2048,1024]{1,0:T(8,128)(2,1)} custom-call(s32[2]{0:T(128)} %pad_add_fusion.slots, bf16[1024,2048]{1,0:T(8,128)(2,1)} %get-tuple-element.44.c.refs_0_, bf16[1024,2048]{1,0:T(8,128)(2,1)} %get-tuple-element.45.c.refs_1_, bf16[1024,1024]{1,0:T(8,128)(2,1)} %fusion.7.nrm.refs_2_, bf16[1024,1024]{1,0:T(8,128)(2,1)} %collective-permute-done.nrm.refs_3_), custom_call_target="tpu_custom_call" | custom-call | flops 8589934592 | bytes 16777216 | tf_op jit(solution)/shard_map/weight_grad/pallas_call | solution.py:354
  269.6 14.8 %weight_grad.7 = bf16[2048,1024]{1,0:T(8,128)(2,1)} custom-call(s32[2]{0:T(128)} %pad_add_fusion.slots, bf16[1024,2048]{1,0:T(8,128)(2,1)} %get-tuple-element.36.c.refs_0_, bf16[1024,2048]{1,0:T(8,128)(2,1)} %get-tuple-element.37.c.refs_1_, bf16[1024,1024]{1,0:T(8,128)(2,1)} %refs_2_.3, bf16[1024,1024]{1,0:T(8,128)(2,1)} %collective-permute-done.2.dy.refs_3_), custom_call_target="tpu_custom_call" | custom-call | flops 8589934592 | bytes 16777216 | tf_op jit(solution)/shard_map/weight_grad/pallas_call | solution.py:354
  284.4 10.0 %pair_matmul.5 = bf16[1024,1024]{1,0:T(8,128)(2,1)} custom-call(s32[1]{0:T(128)S(6)} %mul.70.pos, bf16[2048,512]{1,0:T(8,128)(2,1)} %get-tuple-element.35.a.refs_0_.refs_1_, bf16[512,1024]{1,0:T(8,128)(2,1)} %wout.3, bf16[1024,2048]{1,0:T(8,128)(2,1)} %get-tuple-element.37.c.refs_1_, bf16[2048,1024]{1,0:T(8,128)(2,1)} %wdown.3), custom_call_target="tpu_custom_call" | custom-call | flops 5368709120 | bytes 12582912 | tf_op jit(solution)/shard_map/pair_matmul/pallas_call | solution.py:314
  294.4 13.3 %pair_matmul.7 = bf16[1024,1024]{1,0:T(8,128)(2,1)} custom-call(s32[1]{0:T(128)S(6)} %mul.70.pos, bf16[2048,1536]{1,0:T(8,128)(2,1)} %attend_back.1.a.refs_0_.refs_1_, bf16[1024,1536]{1,0:T(8,128)(2,1)} %b.7, bf16[1024,2048]{1,0:T(8,128)(2,1)} %get-tuple-element.45.c.refs_1_, bf16[1024,2048]{1,0:T(8,128)(2,1)} %d.7), custom_call_target="tpu_custom_call" | custom-call | flops 7516192768 | bytes 16777216 | tf_op jit(solution)/shard_map/pair_matmul/pallas_call | solution.py:314
  307.7 2.2 collective-permute-start.3
  309.9 0.0 collective-permute-start.1
  310.0 0.6 reduce_sum.118
  310.6 0.6 reduce_sum.119
  311.2 0.6 reduce_sum.117
  313.1 10.0 %pair_matmul.4 = bf16[1024,1024]{1,0:T(8,128)(2,1)} custom-call(s32[1]{0:T(128)S(6)} %mul.69.pos, bf16[2048,512]{1,0:T(8,128)(2,1)} %get-tuple-element.35.a.refs_0_.refs_1_, bf16[512,1024]{1,0:T(8,128)(2,1)} %wout.3, bf16[1024,2048]{1,0:T(8,128)(2,1)} %get-tuple-element.36.c.refs_0_, bf16[2048,1024]{1,0:T(8,128)(2,1)} %wdown.3), custom_call_target="tpu_custom_call" | custom-call | flops 5368709120 | bytes 12582912 | tf_op jit(solution)/shard_map/pair_matmul/pallas_call | solution.py:314
  323.1 13.3 %pair_matmul.6 = bf16[1024,1024]{1,0:T(8,128)(2,1)} custom-call(s32[1]{0:T(128)S(6)} %mul.69.pos, bf16[2048,1536]{1,0:T(8,128)(2,1)} %attend_back.1.a.refs_0_.refs_1_, bf16[1024,1536]{1,0:T(8,128)(2,1)} %b.7, bf16[1024,2048]{1,0:T(8,128)(2,1)} %get-tuple-element.44.c.refs_0_, bf16[1024,2048]{1,0:T(8,128)(2,1)} %d.7), custom_call_target="tpu_custom_call" | custom-call | flops 7516192768 | bytes 16777216 | tf_op jit(solution)/shard_map/pair_matmul/pallas_call | solution.py:314
  336.4 20.4 %collective-permute-done.3 = bf16[1024,1024]{1,0:T(8,128)(2,1)} collective-permute-done((bf16[1024,1024]{1,0:T(8,128)(2,1)}, bf16[1024,1024]{1,0:T(8,128)(2,1)}, u32[]{:S(2)}, u32[]{:S(2)}) %collective-permute-start.3) | collective-permute-done | bytes 2097184 | tf_op jit(solution)/shard_map/ppermute | solution.py:443
  356.8 43.2 %collective-permute-done.1 = bf16[1024,1024]{1,0:T(8,128)(2,1)} collective-permute-done((bf16[1024,1024]{1,0:T(8,128)(2,1)}, bf16[1024,1024]{1,0:T(8,128)(2,1)}, u32[]{:S(2)}, u32[]{:S(2)}) %collective-permute-start.1) | collective-permute-done | bytes 2097184 | tf_op jit(solution)/shard_map/ppermute | solution.py:432
  400.0 8.0 %fusion.12 = (f32[1024]{0:T(1024)S(1)}, f32[1024]{0:T(1024)S(1)}, f32[1024]{0:T(1024)S(1)}, f32[1024]{0:T(1024)S(1)}, f32[]{:T(128)}, /*index=5*/bf16[1024,1024]{1,0:T(8,128)(2,1)}) fusion(bf16[1024,1024]{1,0:T(8,128)(2,1)S(1)} %copy-done.1, bf16[1024,1024]{1,0:T(8,128)(2,1)} %collective-permute-done.3, bf16[1024,1024]{1,0:T(8,128)(2,1)} %pair_matmul.6, ...), kind=kLoop, calls=%fused_computation.15 | loop fusion | flops 20967424 | bytes 12611588 | tf_op jit(solution)/shard_map/reduce_sum | solution.py:463
  407.9 1.4 pad_maximum_fusion
  409.3 42.1 %all-reduce = (f32[1024]{0:T(1024)}, f32[1024]{0:T(1024)}, f32[3]{0:T(128)S(1)}) all-reduce(f32[1024]{0:T(1024)S(1)} %get-tuple-element.76, f32[1024]{0:T(1024)S(1)} %get-tuple-element.79, f32[3]{0:T(128)S(1)} %pad_maximum_fusion), channel_id=1, replica_groups=mesh['dp'=16,'mp'=2] {'dp','mp'}, use_global_device_ids=true, to_apply=%region_8.9 | all-reduce | flops 2051 | bytes 16408 | tf_op jit(solution)/shard_map/psum | solution.py:461
  451.5 0.5 multiply_sqrt_fusion
  452.0 5.2 fusion.11
  457.2 65.0 %all-reduce.4.cloned.1.call-done = (bf16[1024,1536]{0,1:T(8,128)(2,1)}, bf16[1024,2048]{0,1:T(8,128)(2,1)}, bf16[512,1024]{1,0:T(8,128)(2,1)}, bf16[2048,1024]{1,0:T(8,128)(2,1)}) async-done(((bf16[1024,1536]{0,1:T(8,128)(2,1)}, bf16[1024,2048]{0,1:T(8,128)(2,1)}, bf16[512,1024]{1,0:T(8,128)(2,1)}, bf16[2048,1024]{1,0:T(8,128)(2,1)}), (bf16[1024,1536]{0,1:T(8,128)(2,1)}, bf16[1024,2048]{0,1:T(8,128)(2,1)}, ...) | async-done | bytes 12582928 | tf_op jit(solution)/shard_map/psum | solution.py:449
  522.2 5.5 copy.28
  527.7 1.6 convert_element_type.72
  529.3 7.1 %copy.29 = f32[1024,2048]{1,0:T(8,128)} copy(bf16[1024,2048]{0,1:T(8,128)(2,1)} %get-tuple-element.87) | data formatting | bytes 12582912
  536.4 6.6 %convert_element_type.75 = f32[2048,1024]{1,0:T(8,128)} convert(bf16[2048,1024]{1,0:T(8,128)(2,1)} %get-tuple-element.89) | non-fusion elementwise | flops 2097152 | bytes 12582912 | tf_op jit(solution)/shard_map/convert_element_type | solution.py:478
  (41 shorter events, 0.1 us)
Async XLA Ops:
  7.2 4.5 copy-start
  7.2 4.5 copy-start.12
  7.2 4.5 copy-start.7
  7.2 9.6 %copy-start.13 = (s32[1,4]{1,0:T(1,128)S(1)}, s32[1,4]{1,0:T(1,128)}, u32[]{:S(2)}) copy-start(s32[1,4]{1,0:T(1,128)} %param.11) | copy-start | bytes 52
  7.2 515.0 %all-reduce.4.cloned.1.call-start = ((), (), s32[]{:S(2)}) async-start(), calls=%async_computation | async-start | bytes 25165824 | tf_op jit(solution)/shard_map/psum | solution.py:449
  9.3 4.5 copy-start.3
  11.7 5.1 copy-start.5
  13.8 58.8 %collective-permute-start = (bf16[1024,1024]{1,0:T(8,128)(2,1)}, bf16[1024,1024]{1,0:T(8,128)(2,1)}, u32[]{:S(2)}, u32[]{:S(2)}) collective-permute-start(bf16[1024,1024]{1,0:T(8,128)(2,1)} %fusion.7.nrm.refs_2_), channel_id=1, source_target_pairs={{1,0},{0,1},{3,2},{2,3},{5,4},{4,5},{7,6},{6,7},{9,8},{8,9},{11,10... | collective-permute-start | bytes 6291464 | tf_op jit(solution)/shard_map/ppermute | solution.py:413
  16.8 136.5 %collective-permute-start.2 = (bf16[1024,1024]{1,0:T(8,128)(2,1)}, bf16[1024,1024]{1,0:T(8,128)(2,1)}, u32[]{:S(2)}, u32[]{:S(2)}) collective-permute-start(bf16[1024,1024]{1,0:T(8,128)(2,1)} %refs_2_.3), channel_id=1, source_target_pairs={{1,0},{0,1},{3,2},{2,3},{5,4},{4,5},{7,6},{6,7},{9,8},{8,9},{11,10... | collective-permute-start | bytes 6291464 | tf_op jit(solution)/shard_map/ppermute | solution.py:414
  294.4 15.5 %copy-start.9 = (f32[8,128]{1,0:T(8,128)S(1)}, f32[8,128]{1,0:T(8,128)}, u32[]{:S(2)}) copy-start(f32[8,128]{1,0:T(8,128)} %get-tuple-element.47) | copy-start | bytes 12292
  294.4 16.1 %copy-start.10 = (f32[8,128]{1,0:T(8,128)S(1)}, f32[8,128]{1,0:T(8,128)}, u32[]{:S(2)}) copy-start(f32[8,128]{1,0:T(8,128)} %get-tuple-element.48) | copy-start | bytes 12292
  294.4 16.7 %copy-start.11 = (f32[8,128]{1,0:T(8,128)S(1)}, f32[8,128]{1,0:T(8,128)}, u32[]{:S(2)}) copy-start(f32[8,128]{1,0:T(8,128)} %get-tuple-element.46) | copy-start | bytes 12292
  307.7 49.0 %collective-permute-start.3 = (bf16[1024,1024]{1,0:T(8,128)(2,1)}, bf16[1024,1024]{1,0:T(8,128)(2,1)}, u32[]{:S(2)}, u32[]{:S(2)}) collective-permute-start(bf16[1024,1024]{1,0:T(8,128)(2,1)} %pair_matmul.7), channel_id=1, source_target_pairs={{1,0},{0,1},{3,2},{2,3},{5,4},{4,5},{7,6},{6,7},{9,8},{8,9},{11,10... | collective-permute-start | bytes 6291464 | tf_op jit(solution)/shard_map/ppermute | solution.py:443
  309.9 90.0 %collective-permute-start.1 = (bf16[1024,1024]{1,0:T(8,128)(2,1)}, bf16[1024,1024]{1,0:T(8,128)(2,1)}, u32[]{:S(2)}, u32[]{:S(2)}) collective-permute-start(bf16[1024,1024]{1,0:T(8,128)(2,1)} %pair_matmul.5), channel_id=1, source_target_pairs={{1,0},{0,1},{3,2},{2,3},{5,4},{4,5},{7,6},{6,7},{9,8},{8,9},{11,10... | collective-permute-start | bytes 6291464 | tf_op jit(solution)/shard_map/ppermute | solution.py:432
  323.1 76.9 %copy-start.1 = (bf16[1024,1024]{1,0:T(8,128)(2,1)S(1)}, bf16[1024,1024]{1,0:T(8,128)(2,1)}, u32[]{:S(2)}) copy-start(bf16[1024,1024]{1,0:T(8,128)(2,1)} %param.10) | copy-start | bytes 6291460
  323.1 76.9 %copy-start.4 = (f32[1024]{0:T(1024)S(1)}, f32[1024]{0:T(1024)}, u32[]{:S(2)}) copy-start(f32[1024]{0:T(1024)} %copy-done.3) | copy-start | bytes 12292
  323.1 76.9 %copy-start.6 = (f32[1024]{0:T(1024)S(1)}, f32[1024]{0:T(1024)}, u32[]{:S(2)}) copy-start(f32[1024]{0:T(1024)} %copy-done.5) | copy-start | bytes 12292
  323.1 76.9 %copy-start.8 = (f32[1024]{0:T(1024)S(1)}, f32[1024]{0:T(1024)}, u32[]{:S(2)}) copy-start(f32[1024]{0:T(1024)} %param.12) | copy-start | bytes 12292
  336.4 115.0 %copy-start.14 = (f32[3]{0:T(128)S(1)}, f32[3]{0:T(128)}, u32[]{:S(2)}) copy-start(f32[3]{0:T(128)} %constant.62) | copy-start | bytes 40
  522.2 5.5 copy-start.2
Sparse Core Ops, SparseCore 0:
  284.5 237.7 all-reduce.3

commit v2 on v1

v2 whole, which is shorter than its diff:
```python
import functools

import jax
import jax.numpy as jnp
from jax import lax
from jax.experimental import pallas as pl
from jax.experimental.pallas import tpu as pltpu
from jax.sharding import PartitionSpec as P

HEAD = 64
ROT = 16
LANES = 128
TILE = 256
F32 = jnp.float32
BF = jnp.bfloat16

epsilon = 1e-05
rope_base = 10000.0
excluded = -1e20


def nn(a, b):
    return jnp.dot(a, b, preferred_element_type=F32)


def nt(a, b):
    return lax.dot_general(a, b, (((1,), (1,)), ((), ())), preferred_element_type=F32)


def tn(a, b):
    return lax.dot_general(a, b, (((0,), (0,)), ((), ())), preferred_element_type=F32)


def whole(shape):
    zeros = (0,) * len(shape)
    return pl.BlockSpec(shape, lambda *_: zeros, pipeline_mode=pl.Buffered(1))


def struct(shape, dtype):
    return jax.ShapeDtypeStruct(shape, dtype)


def cost(flops, nbytes, trans=0):
    return pl.CostEstimate(flops=int(flops), bytes_accessed=int(nbytes), transcendentals=int(trans))


def params(**kw):
    return pltpu.CompilerParams(vmem_limit_bytes=60 * 2**20, **kw)


def lane_ids(rows):
    return lax.broadcasted_iota(jnp.int32, (rows, LANES), 1)


def turn(x, cos, fwd, back):
    return x * cos + pltpu.roll(x, LANES - ROT // 2, 1) * fwd + pltpu.roll(x, ROT // 2, 1) * back


def gelu_parts(v):
    x = jnp.abs(v)
    bell = jnp.exp(v * v * (-0.5))
    t = 1.0 / (1.0 + x * (0.3275911 * 0.7071067811865476))
    poly = t * (
        0.254829592
        + t * (-0.284496736 + t * (1.421413741 + t * (-1.453152027 + t * 1.061405429)))
    )
    tail = 0.5 * poly * bell
    cdf = jnp.where(v >= 0, 1.0 - tail, tail)
    return v * cdf, cdf + v * bell * 0.3989422804014327


def project_kernel(pairs, slot, nrm, wqkv, win, cos, fwd, back, hot, neg, *rest):
    q_out, k_out, v_out, act, slope, sq = rest[-6:]
    j = pl.program_id(0)
    rows = nrm.shape[0]
    chunk = min(TILE, rows)

    @pl.when(j == 0)
    def _():
        sq[...] = jnp.zeros_like(sq)

    @pl.when(j < pairs)
    def _():
        lane = lane_ids(chunk)
        low = lane < HEAD
        one = jnp.where(lane < HEAD + 2, 1.0, 0.0)
        for i in range(rows // chunk):
            r = pl.ds(i * chunk, chunk)
            y = nn(nrm[r, :], wqkv[...])
            g0, g1, g2 = y[:, :128], y[:, 128:256], y[:, 256:]
            r1, r2 = pltpu.roll(g1, HEAD, 1), pltpu.roll(g2, HEAD, 1)
            for h, (qk, v) in enumerate(((g0, g1), (jnp.where(low, r1, r2), r2))):
                qk = turn(qk, cos[r, :], fwd[r, :], back[r, :])
                q_out[h, r, :] = jnp.where(low, qk * HEAD**-0.5, hot[r, :].astype(F32)).astype(BF)
                k_out[h, r, :] = jnp.where(low, pltpu.roll(qk, HEAD, 1), neg[r, :].astype(F32)).astype(BF)
                v_out[h, r, :] = jnp.where(low, v, one).astype(BF)

    @pl.when(j >= pairs)
    def _():
        for i in range(rows // chunk):
            r = pl.ds(i * chunk, chunk)
            a, sl = gelu_parts(nn(nrm[r, :], win[...]))
            a = a.astype(BF)
            act[r, :] = a
            slope[r, :] = sl.astype(BF)
            wide = a.astype(F32)
            sq[...] += jnp.sum((wide * wide).reshape(chunk // 8, 8, -1), axis=0)


def project(slot, total, heads, prior, nrm, wqkv, win, cos, fwd, back, hot, neg):
    rows, d = nrm.shape
    f = win.shape[1]
    pairs = heads // 2
    tile = min(512, f)
    lead = lambda j: jnp.minimum(j, pairs - 1)
    late = lambda j: jnp.maximum(j - pairs, 0)
    at = pl.BlockSpec((rows, LANES), lambda j, slot: (slot[0], 0), pipeline_mode=pl.Buffered(1))
    hd = pl.BlockSpec((2, rows, LANES), lambda j, slot: (lead(j), slot[0], 0))
    ff = pl.BlockSpec((rows, tile), lambda j, slot: (0, late(j)))
    big = struct((heads, total, LANES), BF)
    return pl.pallas_call(
        functools.partial(project_kernel, pairs),
        grid_spec=pltpu.PrefetchScalarGridSpec(
            num_scalar_prefetch=1,
            grid=(pairs + f // tile,),
            in_specs=[
                whole(nrm.shape),
                pl.BlockSpec((d, 384), lambda j, slot: (0, lead(j))),
                pl.BlockSpec((d, tile), lambda j, slot: (0, late(j))),
                at, at, at, at, at,
            ]
            + [pl.BlockSpec(memory_space=pl.ANY)] * len(prior),
            out_specs=[hd, hd, hd, ff, ff, pl.BlockSpec((8, tile), lambda j, slot: (0, 0))],
        ),
        out_shape=[big, big, big, struct((rows, f), BF), struct((rows, f), BF), struct((8, tile), F32)],
        input_output_aliases={9 + i: i for i in range(len(prior))},
        compiler_params=params(),
        cost_estimate=cost(2 * rows * d * (f + wqkv.shape[1]), 2 * (d * (f + wqkv.shape[1]) + 6 * rows * d)),
        name="project",
    )(slot, nrm, wqkv, win, cos, fwd, back, hot, neg, *prior)


def cotangent_kernel(slot, dy, wout, wdown, slope, *rest):
    do_out, gpre = rest[-2:]
    j = pl.program_id(0)
    rows = dy.shape[0]
    chunk = min(512, rows)

    @pl.when(j == 0)
    def _():
        low = lane_ids(chunk) < HEAD
        for i in range(rows // chunk):
            r = pl.ds(i * chunk, chunk)
            g = nt(dy[r, :], wout[...])
            for p in range(g.shape[1] // LANES):
                y = g[:, p * LANES : (p + 1) * LANES]
                do_out[2 * p, r, :] = jnp.where(low, y, 0.0).astype(BF)
                do_out[2 * p + 1, r, :] = jnp.where(low, pltpu.roll(y, HEAD, 1), 0.0).astype(BF)

    @pl.when(j > 0)
    def _():
        for i in range(rows // chunk):
            r = pl.ds(i * chunk, chunk)
            gpre[r, :] = (nt(dy[r, :], wdown[...]) * slope[r, :].astype(F32)).astype(BF)


def cotangent(slot, total, heads, prior, dy, wout, wdown, slope):
    rows, d = dy.shape
    f = wdown.shape[0]
    tile = min(512, f)
    late = lambda j: jnp.maximum(j - 1, 0)
    ff = pl.BlockSpec((rows, tile), lambda j, slot: (0, late(j)))
    return pl.pallas_call(
        cotangent_kernel,
        grid_spec=pltpu.PrefetchScalarGridSpec(
            num_scalar_prefetch=1,
            grid=(1 + f // tile,),
            in_specs=[whole(dy.shape), whole(wout.shape), pl.BlockSpec((tile, d), lambda j, slot: (late(j), 0)), ff]
            + [pl.BlockSpec(memory_space=pl.ANY)] * len(prior),
            out_specs=[pl.BlockSpec((heads, rows, LANES), lambda j, slot: (0, slot[0], 0)), ff],
        ),
        out_shape=[struct((heads, total, LANES), BF), struct((rows, f), BF)],
        input_output_aliases={5 + i: i for i in range(len(prior))},
        compiler_params=params(),
        cost_estimate=cost(2 * rows * d * (f + wout.shape[0]), 2 * (d * (f + wout.shape[0]) + 5 * rows * d)),
        name="cotangent",
    )(slot, dy, wout, wdown, slope, *prior)


def attend_kernel(q_ref, k_ref, v_ref, ctx, wide, keep, sq):
    h = pl.program_id(1)
    total = q_ref.shape[1]
    b = TILE
    tri = lax.broadcasted_iota(jnp.int32, (b, b), 0) >= lax.broadcasted_iota(jnp.int32, (b, b), 1)
    low = lane_ids(b) < HEAD

    @pl.when((h == 0) & (pl.program_id(0) == 0))
    def _():
        sq[...] = jnp.zeros_like(sq)

    for i in range(total // b):
        n = (i + 1) * b
        rows = pl.ds(i * b, b)
        s = nt(q_ref[0, rows, :], k_ref[0, :n, :])
        s_diag = jnp.where(tri, s[:, n - b :], excluded)
        top = jnp.max(s_diag, axis=1, keepdims=True)
        if i:
            top = jnp.maximum(top, jnp.max(s[:, : n - b], axis=1, keepdims=True))
        w = jnp.exp(s_diag - top).astype(BF)
        if i:
            w = jnp.concatenate([jnp.exp(s[:, : n - b] - top).astype(BF), w], axis=1)
        for j in range(i + 1):
            keep[0, i * (i + 1) // 2 + j] = w[:, j * b : (j + 1) * b]
        acc = nn(w, v_ref[0, :n, :])
        inv = 1.0 / acc[:, HEAD : HEAD + 1]
        acc = acc * inv
        wide[0, rows, :] = jnp.where(low, acc, inv)
        out = acc.astype(BF)
        real = jnp.where(low, out.astype(F32), 0.0)
        sq[...] += jnp.sum((real * real).reshape(b // 8, 8, LANES), axis=0)

        @pl.when(h == 0)
        def _():
            ctx[rows, :] = out

        @pl.when(h == 1)
        def _():
            both = jnp.where(low, ctx[rows, :].astype(F32), pltpu.roll(out.astype(F32), HEAD, 1))
            ctx[rows, :] = both.astype(BF)


def attend(q, k, v):
    heads, total, _ = q.shape
    tiles = total // TILE
    tiles = tiles * (tiles + 1) // 2
    hd = pl.BlockSpec((1, total, LANES), lambda p, h: (2 * p + h, 0, 0))
    return pl.pallas_call(
        attend_kernel,
        grid=(heads // 2, 2),
        in_specs=[hd, hd, hd],
        out_specs=[
            pl.BlockSpec((total, LANES), lambda p, h: (0, p)),
            hd,
            pl.BlockSpec((1, tiles, TILE, TILE), lambda p, h: (2 * p + h, 0, 0, 0)),
            pl.BlockSpec((8, LANES), lambda p, h: (0, 0)),
        ],
        out_shape=[
            struct((total, heads * HEAD), BF),
            struct((heads, total, LANES), F32),
            struct((heads, tiles, TILE, TILE), BF),
            struct((8, LANES), F32),
        ],
        compiler_params=params(),
        cost_estimate=cost(4 * heads * tiles * TILE * TILE * 256, heads * total * LANES * 20, heads * tiles * TILE * TILE),
        name="attend",
    )(q, k, v)


def attend_back_kernel(q_ref, k_ref, v_ref, do_ref, wide, keep, cos, fwd, back, out, dk_acc, dv_acc, dq_acc, hold):
    h = pl.program_id(1)
    total = q_ref.shape[1]
    b = TILE
    lane = lane_ids(b)
    low = lane < HEAD
    dk_acc[...] = jnp.zeros_like(dk_acc)
    dv_acc[...] = jnp.zeros_like(dv_acc)
    for i in range(total // b):
        n = (i + 1) * b
        rows = pl.ds(i * b, b)
        q = q_ref[0, rows, :]
        w = [keep[0, i * (i + 1) // 2 + j] for j in range(i + 1)]
        w = w[0] if i == 0 else jnp.concatenate(w, axis=1)
        context = wide[0, rows, :]
        inv = context[:, HEAD : HEAD + 1]
        scaled = (do_ref[0, rows, :].astype(F32) * inv).astype(BF)
        grad = scaled.astype(F32)
        delta = jnp.sum(jnp.where(low, grad * context, 0.0), axis=1, keepdims=True)
        delta_hi = delta.astype(BF).astype(F32)
        delta_lo = delta - delta_hi
        joined = jnp.where(lane == HEAD, -delta_hi, jnp.where(lane == HEAD + 1, -delta_lo, grad)).astype(BF)
        ds = w * nt(joined, v_ref[0, :n, :]).astype(BF)
        dq_acc[rows, :] = nn(ds, k_ref[0, :n, :]) * HEAD**-0.5
        dk_acc[:n, :] += tn(ds, q)
        dv_acc[:n, :] += tn(w, scaled)
    for i in range(total // b):
        rows = pl.ds(i * b, b)
        x = jnp.where(low, dq_acc[rows, :], pltpu.roll(dk_acc[rows, :], HEAD, 1))
        x = turn(x, cos[rows, :], -fwd[rows, :], -back[rows, :])
        dv = dv_acc[rows, :]

        @pl.when(h == 0)
        def _():
            out[rows, :LANES] = x.astype(BF)
            hold[rows, :] = dv

        @pl.when(h == 1)
        def _():
            r = pltpu.roll(x, HEAD, 1)
            out[rows, LANES : 2 * LANES] = jnp.where(low, hold[rows, :], r).astype(BF)
            out[rows, 2 * LANES :] = jnp.where(low, r, pltpu.roll(dv, HEAD, 1)).astype(BF)


def attend_back(q, k, v, do, wide, keep, cos, fwd, back):
    heads, total, _ = q.shape
    hd = pl.BlockSpec((1, total, LANES), lambda p, h: (2 * p + h, 0, 0))
    acc = pltpu.VMEM((total, LANES), F32)
    tiles = keep.shape[1]
    return pl.pallas_call(
        attend_back_kernel,
        grid=(heads // 2, 2),
        in_specs=[hd, hd, hd, hd, hd, pl.BlockSpec((1,) + keep.shape[1:], lambda p, h: (2 * p + h, 0, 0, 0))]
        + [whole(cos.shape)] * 3,
        out_specs=pl.BlockSpec((total, 384), lambda p, h: (0, p)),
        out_shape=struct((total, heads * 3 * HEAD), BF),
        scratch_shapes=[acc] * 4,
        compiler_params=params(),
        cost_estimate=cost(8 * heads * tiles * TILE * TILE * 256, heads * total * LANES * 40),
        name="attend_back",
    )(q, k, v, do, wide, keep, cos, fwd, back)


def pair_kernel(transposed, pos, a, b, c, d, out):
    dot = nt if transposed else nn
    out[...] = (dot(a[...], b[...]) + dot(c[...], d[...])).astype(BF)


def pair_matmul(slot, transposed, a, b, c, d):
    rows = c.shape[0]
    width = b.shape[0] if transposed else b.shape[1]
    tile = 256
    if transposed:
        weight = lambda w: pl.BlockSpec((tile, w.shape[1]), lambda j, slot: (j, 0))
    else:
        weight = lambda w: pl.BlockSpec((w.shape[0], tile), lambda j, slot: (0, j))
    return pl.pallas_call(
        functools.partial(pair_kernel, transposed),
        grid_spec=pltpu.PrefetchScalarGridSpec(
            num_scalar_prefetch=1,
            grid=(width // tile,),
            in_specs=[
                pl.BlockSpec((rows, a.shape[1]), lambda j, slot: (slot[0], 0), pipeline_mode=pl.Buffered(1)),
                weight(b),
                whole(c.shape),
                weight(d),
            ],
            out_specs=pl.BlockSpec((rows, tile), lambda j, slot: (0, j)),
        ),
        out_shape=struct((rows, width), BF),
        compiler_params=params(),
        cost_estimate=cost(2 * rows * width * (a.shape[1] + c.shape[1]), 2 * (b.size + d.size + rows * (width + a.shape[1] + c.shape[1]))),
        name="pair_matmul",
    )(slot, a, b, c, d)


def weight_kernel(n, slots, *refs):
    xs, ys, out = refs[:n], refs[n : 2 * n], refs[2 * n]
    width = out.shape[1]
    step = 512 if width % 512 == 0 else 128
    for c in range(width // step):
        cols = pl.ds(c * step, step)
        out[:, cols] = sum(tn(x[...], y[:, cols]) for x, y in zip(xs, ys)).astype(BF)


def weight_grad(slots, xs, ys, rows):
    n = max(len(xs), len(ys))
    tile = min(256, xs[0].shape[1])
    width = ys[0].shape[1]
    by = lambda s, one, shape, index: pl.BlockSpec(
        shape, (lambda j, slots: (slots[s], index(j))) if one else (lambda j, slots: (0, index(j))),
        **({} if shape[1] == tile else {"pipeline_mode": pl.Buffered(1)})
    )
    specs = [by(s, len(xs) < n, (rows, tile), lambda j: j) for s in range(n)]
    specs += [by(s, len(ys) < n, (rows, width), lambda j: 0) for s in range(n)]
    xs = list(xs) * (n // len(xs))
    ys = list(ys) * (n // len(ys))
    depth = xs[0].shape[1]
    return pl.pallas_call(
        functools.partial(weight_kernel, n),
        grid_spec=pltpu.PrefetchScalarGridSpec(
            num_scalar_prefetch=1,
            grid=(depth // tile,),
            in_specs=specs,
            out_specs=pl.BlockSpec((tile, width), lambda j, slots: (j, 0)),
        ),
        out_shape=struct((depth, width), BF),
        compiler_params=params(),
        cost_estimate=cost(2 * n * rows * depth * width, 2 * (n * rows * (depth + width) + depth * width)),
        name="weight_grad",
    )(slots, *xs, *ys)


def ring_kernel(chips, parts, x, out, near, part, far, core_sem, rs_send, rs_recv, ag_send, ag_recv, fin_send, fin_recv):
    dp = lax.axis_index("dp")
    core, chip = lax.rem(dp, 2), dp // 2
    y, z = lax.rem(chip, 2), chip // 2
    p = z * (1 - y) + (chips - 1 - z) * y

    def device(pos):
        high = pos // (chips // 2)
        return ((1 - high) * 2 * pos + high * (2 * (chips - 1 - pos) + 1)) * 2 + core

    peer = dp + 1 - 2 * core
    ends = [device(lax.rem(p + 1, chips)), device(lax.rem(p + chips - 1, chips))]
    barrier = pltpu.get_barrier_semaphore()
    for t in (*ends, peer):
        pl.semaphore_signal(barrier, inc=1, device_id={"dp": t}, device_id_type=pl.DeviceIdType.MESH)
    pl.semaphore_wait(barrier, 3)

    def remote(src, dst, send, recv, t):
        return pltpu.make_async_remote_copy(
            src_ref=src, dst_ref=dst, send_sem=send, recv_sem=recv,
            device_id={"dp": t}, device_id_type=pl.DeviceIdType.MESH,
        )

    def chunk(s, d):
        return lax.rem(p + 2 * chips - s, chips) if d % 2 == 0 else lax.rem(p + s, chips)

    def add(a, b):
        return (a.astype(F32) + b.astype(F32)).astype(BF)

    swaps = [remote(x.at[1 - core, c], near.at[c], core_sem.at[0, c], core_sem.at[1, c], peer) for c in range(chips)]
    for c in swaps:
        c.start()
    for c in range(chips):
        swaps[c].wait_recv()
        part[c] = add(x[core, c], near[c])

    def reduce(s, d):
        return remote(part.at[chunk(s, d), d], far.at[s, d], rs_send.at[s, d], rs_recv.at[s, d], ends[d % 2])

    def gather(s, d):
        c = chunk(chips - 1 + s, d)
        return remote(out.at[core, c, d], out.at[core, c, d], ag_send.at[s, d], ag_recv.at[s, d], ends[d % 2])

    def across(s, d, half):
        c = chunk(chips - 1 + s, d)
        return remote(out.at[core, c, d], out.at[half, c, d], fin_send.at[s, d], fin_recv.at[s, d], peer)

    for s in range(chips - 1):
        for d in range(parts):
            if s:
                reduce(s - 1, d).wait_recv()
                c = chunk(s, d)
                part[c, d] = add(part[c, d], far[s - 1, d])
            reduce(s, d).start()
    for s in range(chips):
        for d in range(parts):
            if s == 0:
                reduce(chips - 2, d).wait_recv()
                c = chunk(chips - 1, d)
                out[core, c, d] = add(part[c, d], far[chips - 2, d])
            else:
                gather(s - 1, d).wait_recv()
            if s < chips - 1:
                gather(s, d).start()
            across(s, d, core).start()
    for c in swaps:
        c.wait_send()
    for d in range(parts):
        for s in range(chips - 1):
            reduce(s, d).wait_send()
            gather(s, d).wait_send()
        for s in range(chips):
            across(s, d, core).wait_send()
            across(s, d, 1 - core).wait_recv()


def ring_sum(x, collective_id):
    chips = lax.axis_size("dp") // 2
    rows, d = x.shape
    parts = min(8, rows // (32 * chips))
    cut = x.reshape(2, chips, parts, rows // (2 * chips * parts), d)
    dma = pltpu.SemaphoreType.DMA
    vmem = pl.BlockSpec(memory_space=pltpu.VMEM)
    total = pl.pallas_call(
        functools.partial(ring_kernel, chips, parts),
        out_shape=struct(cut.shape, BF),
        in_specs=[vmem],
        out_specs=vmem,
        scratch_shapes=[pltpu.VMEM(cut.shape[1:], BF), pltpu.VMEM(cut.shape[1:], BF), pltpu.VMEM((chips - 1,) + cut.shape[2:], BF)]
        + [dma((2, chips))] + [dma((chips - 1, parts))] * 4 + [dma((chips, parts))] * 2,
        compiler_params=params(collective_id=collective_id, has_side_effects=True),
        cost_estimate=cost(0, 4 * x.size),
        name="ring_sum",
    )(cut)
    return total.reshape(rows, d)


def small_kernel(n_dp, n_mp, x, out, held, send, recv):
    me = lax.axis_index("dp") * n_mp + lax.axis_index("mp")
    count = n_dp * n_mp
    barrier = pltpu.get_barrier_semaphore()

    def target(k):
        t = lax.rem(me + k, count)
        return dict(device_id={"dp": t // n_mp, "mp": lax.rem(t, n_mp)}, device_id_type=pl.DeviceIdType.MESH)

    def greet(k, carry):
        pl.semaphore_signal(barrier, inc=1, **target(k))
        return carry

    lax.fori_loop(1, count, greet, 0)
    pl.semaphore_wait(barrier, count - 1)

    def copy(k):
        return pltpu.make_async_remote_copy(
            src_ref=x, dst_ref=held.at[me], send_sem=send.at[k], recv_sem=recv.at[k], **target(k)
        )

    def begin(k, carry):
        copy(k).start()
        return carry

    lax.fori_loop(1, count, begin, 0)
    held[me] = x[...]

    def end(k, carry):
        copy(k).wait()
        return carry

    lax.fori_loop(1, count, end, 0)
    out[...] = lax.fori_loop(0, count, lambda k, total: total + held[k], jnp.zeros(x.shape, F32))


def small_sum(x, collective_id):
    n_dp, n_mp = lax.axis_size("dp"), lax.axis_size("mp")
    dma = pltpu.SemaphoreType.DMA
    vmem = pl.BlockSpec(memory_space=pltpu.VMEM)
    return pl.pallas_call(
        functools.partial(small_kernel, n_dp, n_mp),
        out_shape=struct(x.shape, F32),
        in_specs=[vmem],
        out_specs=vmem,
        scratch_shapes=[pltpu.VMEM((n_dp * n_mp,) + x.shape, F32), dma((n_dp * n_mp,)), dma((n_dp * n_mp,))],
        compiler_params=params(collective_id=collective_id, has_side_effects=True),
        name="small_sum",
    )(x)


def norm_kernel(x_ref, scale, bias, out):
    x = x_ref[...].astype(F32)
    mean = jnp.mean(x, axis=1, keepdims=True)
    centred = x - mean
    var = jnp.mean(centred * centred, axis=1, keepdims=True)
    out[...] = (centred * lax.rsqrt(var + epsilon) * scale[...] + bias[...]).astype(BF)


def norm(x, scale, bias):
    rows, d = x.shape
    tile = pl.BlockSpec((min(TILE, rows), d), lambda i: (i, 0))
    return pl.pallas_call(
        norm_kernel,
        grid=(rows // min(TILE, rows),),
        in_specs=[tile, whole((1, d)), whole((1, d))],
        out_specs=tile,
        out_shape=struct((rows, d), BF),
        compiler_params=params(),
        cost_estimate=cost(10 * rows * d, 4 * rows * d),
        name="norm",
    )(x, scale, bias)


def output_kernel(n, x_ref, *refs):
    parts, out, sq = refs[:n], refs[n], refs[n + 1]

    @pl.when(pl.program_id(0) == 0)
    def _():
        sq[...] = jnp.zeros_like(sq)

    y = x_ref[...].astype(F32) + sum(p[...].astype(F32) for p in parts)
    out[...] = y.astype(BF)
    sq[...] += jnp.sum((y * y).reshape(y.shape[0] // 8, 8, -1), axis=0)


def output(x, parts):
    rows, d = x.shape
    tile = pl.BlockSpec((min(TILE, rows), d), lambda i: (i, 0))
    return pl.pallas_call(
        functools.partial(output_kernel, len(parts)),
        grid=(rows // min(TILE, rows),),
        in_specs=[tile] * (1 + len(parts)),
        out_specs=[tile, pl.BlockSpec((8, d), lambda i: (0, 0))],
        out_shape=[struct((rows, d), BF), struct((8, d), F32)],
        compiler_params=params(),
        cost_estimate=cost(4 * rows * d, 8 * rows * d),
        name="output",
    )(x, *parts)


def norm_back_kernel(n, x_ref, dy, scale, *refs):
    parts, out, gain, bias = refs[:n], refs[n], refs[n + 1], refs[n + 2]

    @pl.when(pl.program_id(0) == 0)
    def _():
        gain[...] = jnp.zeros_like(gain)
        bias[...] = jnp.zeros_like(bias)

    x = x_ref[...].astype(F32)
    mean = jnp.mean(x, axis=1, keepdims=True)
    centred = x - mean
    var = jnp.mean(centred * centred, axis=1, keepdims=True)
    inv = lax.rsqrt(var + epsilon)
    unit = centred * inv
    grad = sum(p[...].astype(F32) for p in parts)
    g = grad * scale[...]
    out[...] = dy[...].astype(F32) + inv * (
        g - jnp.mean(g, axis=1, keepdims=True) - unit * jnp.mean(g * unit, axis=1, keepdims=True)
    )
    fold = lambda v: jnp.sum(v.reshape(v.shape[0] // 8, 8, -1), axis=0)
    gain[...] += fold(grad * unit)
    bias[...] += fold(grad)


def norm_back(x, dy, scale, parts):
    rows, d = x.shape
    tile = pl.BlockSpec((min(TILE, rows), d), lambda i: (i, 0))
    acc = pl.BlockSpec((8, d), lambda i: (0, 0))
    return pl.pallas_call(
        functools.partial(norm_back_kernel, len(parts)),
        grid=(rows // min(TILE, rows),),
        in_specs=[tile, tile, whole((1, d))] + [tile] * len(parts),
        out_specs=[tile, acc, acc],
        out_shape=[struct((rows, d), F32), struct((8, d), F32), struct((8, d), F32)],
        compiler_params=params(),
        cost_estimate=cost(20 * rows * d, 12 * rows * d),
        name="norm_back",
    )(x, dy, scale, *parts)


def layout(lengths, group_rows):
    seg_ends = jnp.cumsum(lengths)
    positions = jnp.arange(group_rows, dtype=jnp.int32)
    closed = seg_ends[None, :] <= positions[:, None]
    segment = jnp.sum(closed.astype(jnp.int32), axis=1)
    seg_start = jnp.sum(jnp.where(closed, lengths[None, :], 0), axis=1)
    return segment, positions - seg_start


def table_kernel(ends_ref, lens_ref, freq, cos, fwd, back, hot, neg):
    rows = cos.shape[0]
    lane = lane_ids(rows)
    where = lax.broadcasted_iota(jnp.int32, (rows, LANES), 0) + pl.program_id(0) * rows
    segment = jnp.zeros((rows, LANES), jnp.int32)
    start = jnp.zeros((rows, LANES), jnp.int32)
    for j in range(ends_ref.shape[0]):
        closed = where >= ends_ref[j]
        segment = segment + closed.astype(jnp.int32)
        start = start + jnp.where(closed, lens_ref[j], 0)
    angle = (where - start).astype(F32) * freq[...]
    dim = lax.rem(lane, HEAD)
    sin = jnp.sin(angle)
    cos[...] = jnp.where(dim < ROT, jnp.cos(angle), 1.0)
    fwd[...] = jnp.where(dim < ROT // 2, -sin, 0.0)
    back[...] = jnp.where((dim >= ROT // 2) & (dim < ROT), sin, 0.0)
    same = lane - HEAD == segment
    hot[...] = jnp.where(same, 1.0, 0.0).astype(BF)
    neg[...] = jnp.where(same | (lane < HEAD) | (lane >= HEAD + ends_ref.shape[0]), 0.0, excluded).astype(BF)


def tables(lengths, group_rows):
    half = ROT // 2
    freq = jnp.power(rope_base, -2.0 * jnp.arange(half, dtype=F32) / ROT)
    freq = jnp.pad(jnp.tile(freq, 2), (0, HEAD - ROT))
    freq = jnp.tile(freq, LANES // HEAD)[None, :]
    block = pl.BlockSpec((TILE, LANES), lambda i, *_: (i, 0))
    return pl.pallas_call(
        table_kernel,
        grid_spec=pltpu.PrefetchScalarGridSpec(
            num_scalar_prefetch=2,
            grid=(group_rows // TILE,),
            in_specs=[whole((1, LANES))],
            out_specs=[block] * 5,
        ),
        out_shape=[struct((group_rows, LANES), F32)] * 3 + [struct((group_rows, LANES), BF)] * 2,
        compiler_params=params(),
        name="tables",
    )(jnp.cumsum(lengths).astype(jnp.int32), lengths, freq)


def on_device(hidden_in, seq_lengths, ln_scale, ln_bias, wqkv, wout, win, wdown, out_grad):
    rows, d = hidden_in.shape
    n = lax.axis_size("mp")
    me = lax.axis_index("mp")
    total = rows * n
    heads = wout.shape[0] // HEAD
    f = win.shape[1]
    after = lambda x, *deps: lax.optimization_barrier((x, *deps))[0]

    normed = norm(hidden_in, ln_scale[None, :], ln_bias[None, :])
    ring = lambda s: [((i + s) % n, i) for i in range(n)]
    nrm = [normed] + [lax.ppermute(normed, "mp", ring(s)) for s in range(1, n)]
    early = after(out_grad, *nrm[1:])
    dys = [out_grad] + [lax.ppermute(early, "mp", ring(s)) for s in range(1, n)]
    slots = jnp.stack([(me + s) % n for s in range(n)]).astype(jnp.int32)
    pos = [slots[s : s + 1] for s in range(n)]
    table = tables(seq_lengths[0], total)

    qkv, do = [], []
    acts, slopes, gpres, act_sq = [], [], [], []
    for s in range(n):
        *qkv, a, sl, sq = project(pos[s], total, heads, qkv, nrm[s], wqkv, win, *table)
        acts.append(a)
        slopes.append(sl)
        act_sq.append(sq)
        if s == 0:
            *do, g = cotangent(pos[0], total, heads, do, dys[0], wout, wdown, slopes[0])
            gpres.append(g)
    context, wide, keep, ctx_sq = attend(*qkv)
    others = [
        lax.ppermute(pair_matmul(pos[s], False, context, wout, acts[s], wdown), "mp", ring(n - s))
        for s in range(1, n)
    ]
    for s in range(1, n):
        *do, g = cotangent(pos[s], total, heads, do, dys[s], wout, wdown, slopes[s])
        gpres.append(g)
    gdown = weight_grad(slots, acts, dys, rows)
    gdown = lax.psum(gdown, "dp")
    gin = weight_grad(slots, nrm, gpres, rows)
    gow = weight_grad(slots, [context], dys, rows)
    update = pair_matmul(pos[0], False, context, wout, acts[0], wdown)
    gqkv = attend_back(*qkv, do[0], wide, keep, *table[:3])
    gin, gow = lax.psum((after(gin, gdown), after(gow, gdown)), "dp")
    backs = [
        lax.ppermute(pair_matmul(pos[s], True, gqkv, wqkv, gpres[s], win), "mp", ring(n - s))
        for s in range(1, n)
    ]
    result, res_sq = output(hidden_in, [update] + others)
    gqw = weight_grad(slots, nrm, [gqkv], rows)
    own = pair_matmul(pos[0], True, gqkv, wqkv, gpres[0], win)
    gqw = ring_sum(after(gqw, own), 1)
    grad_hidden, gain, bias = norm_back(hidden_in, out_grad, ln_scale[None, :], [own] + backs)

    stats = jnp.stack([jnp.sum(res_sq), jnp.sum(ctx_sq), sum(jnp.sum(s) for s in act_sq)])
    packed = jnp.concatenate(
        [jnp.sum(gain, axis=0)[None], jnp.sum(bias, axis=0)[None], jnp.pad(stats, (0, d - 3))[None], jnp.zeros((5, d), F32)]
    )
    sums = small_sum(packed, 2)
    devices = lax.axis_size("dp") * n
    counts = jnp.array([rows * d * devices, rows * d * devices, rows * f * n * devices], F32)
    return (
        result,
        grad_hidden,
        sums[0],
        sums[1],
        gqw.astype(F32),
        gow.astype(F32),
        gin.astype(F32),
        gdown.astype(F32),
        jnp.sqrt(sums[2, :3] / counts),
    )


def solution(mesh):
    tok = P(("dp", "mp"), None)
    cols, rows = P(None, "mp"), P("mp", None)
    return jax.shard_map(
        on_device,
        mesh=mesh,
        in_specs=(tok, P("dp", None), P(), P(), cols, rows, cols, rows, tok),
        out_specs=(tok, tok, P(), P(), cols, rows, cols, rows, P()),
        check_vma=False,
    )
```

time: 559 us -> 494 us (0.88)
  Pallas kernels: 294 us -> 422 us
  waiting for transfers between devices: 129 us -> 7.24 us
  blocking collectives: 42.1 us -> 0 us
  local copies, waits for them, and re-layouts: 24.8 us -> 3.56 us
  other arithmetic: 39.4 us -> 31.6 us
    pallas_call x2 -> x8, Pallas kernels: 49.8 us -> 176 us  [the longest x1 70.1 us: ring_sum(): pl.pallas_call(functools.partial(ring_kernel, chips, parts), out_shape=st...]
    psum x1 -> x2, waiting for transfers between devices: 65 us -> 7.19 us  [the longest x1 7.19 us: on_device(): gin, gow = lax.psum((after(gin, gdown), after(gow, gdown)), 'dp')]
    ppermute x1, waiting for transfers between devices: 43.2 us -> 0.01 us  [on_device(): lax.ppermute(pair_matmul(pos[s], False, context, wout, acts[s], wdown), '...]
    psum x1 -> x0, blocking collectives: 42.1 us -> none  [on_device(): lax.psum((jnp.sum(grad_normed * unit, axis=0), jnp.sum(grad_normed, axis=...]
    ppermute x1, waiting for transfers between devices: 20.4 us -> 0.01 us  [on_device(): lax.ppermute(pair_matmul(pos[s], True, gqkv, wqkv, gpres[s], win), 'mp',...]
    concatenate x3 -> x1, local copies, waits for them, and re-layouts: 12 us -> 0.08 us  [on_device(): jnp.concatenate([jnp.sum(gain, axis=0)[None], jnp.sum(bias, axis=0)[None]...]
    unnamed x32 -> x12, local copies, waits for them, and re-layouts: 12.7 us -> 1.34 us
    reduce_sum x6 -> x5, other arithmetic: 13.6 us -> 4.83 us  [the longest x2 1.91 us: on_device(): jnp.sum(s)]
  transfers between devices with their start and end apart: 5 -> 6, of which waited for: 3 -> 1; matrix products, arithmetic and copies ran while one was open for 7% -> 5% of each run, Pallas kernels for 30% -> 86%
where the time goes in v2:
time: 494 us; the launch traced here: 486 us
  Pallas kernels  422 us (85%)
  other arithmetic  31.6 us (6%)
  between operations  15.7 us (3%)
  waiting for transfers between devices  7.24 us (1%)
  starting transfers between devices  5.77 us (1%)
    pallas_call x1, Pallas kernels, attend_back(): pl.pallas_call(attend_back_kernel, grid=(heads // 2, 2), in_specs=[hd, hd...  71.7 us
    pallas_call x1, Pallas kernels, ring_sum(): pl.pallas_call(functools.partial(ring_kernel, chips, parts), out_shape=st...  70.1 us
    pallas_call x1, Pallas kernels, attend(): pl.pallas_call(attend_kernel, grid=(heads // 2, 2), in_specs=[hd, hd, hd]...  55.6 us
    pallas_call x4, Pallas kernels, weight_grad(): pl.pallas_call(functools.partial(weight_kernel, n), grid_spec=pltpu.Prefe...  49.1 us
    pallas_call x2, Pallas kernels, project(): pl.pallas_call(functools.partial(project_kernel, pairs), grid_spec=pltpu....  48.9 us
    pallas_call x4, Pallas kernels, pair_matmul(): pl.pallas_call(functools.partial(pair_kernel, transposed), grid_spec=pltp...  46.1 us
    pallas_call x1, Pallas kernels, small_sum(): pl.pallas_call(functools.partial(small_kernel, n_dp, n_mp), out_shape=str...  32.3 us
    pallas_call x2, Pallas kernels, cotangent(): pl.pallas_call(cotangent_kernel, grid_spec=pltpu.PrefetchScalarGridSpec(n...  23.8 us
  transfers between devices with their start and end apart: 6, of which 1 were waited for; matrix products, arithmetic and copies ran while one was open for 5% of the time, Pallas kernels for 86%

profile of v2, /device:TPU:0, one launch (start us, length us, event | category | flops | bytes accessed | tf_op | source)
XLA Modules:
  0.0 486.3 jit_solution(4508568080246520473)
XLA Ops:
  7.2 0.0 all-reduce.6.cloned.1.call-start
  7.2 4.5 norm.1.nrm.refs_0_
  11.7 2.9 collective-permute-start
  14.7 0.7 reduce-window.9
  15.4 0.1 tile.7
  15.5 0.6 broadcast_in_dim_tile.3.freq
  16.1 7.5 %tables.1 = (f32[2048,128]{1,0:T(8,128)}, f32[2048,128]{1,0:T(8,128)}, f32[2048,128]{1,0:T(8,128)}, bf16[2048,128]{1,0:T(8,128)(2,1)}, bf16[2048,128]{1,0:T(8,128)(2,1)}) custom-call(s32[4]{0:T(128)} %bitcast.32, s32[4]{0:T(128)} %bitcast.30, f32[1,128]{1,0:T(1,128)} %broadcast_in_dim_tile.3.freq), custom_call_target="tpu_custom_call" | custom-call | tf_op jit(solution)/shard_map/tables/pallas_call | solution.py:666
  23.5 24.3 %project.2 = (bf16[8,2048,128]{2,1,0:T(8,128)(2,1)}, bf16[8,2048,128]{2,1,0:T(8,128)(2,1)}, bf16[8,2048,128]{2,1,0:T(8,128)(2,1)}, bf16[1024,2048]{1,0:T(8,128)(...) custom-call(s32[1]{0:T(128)} %bitcast.slot.pos, bf16[1024,1024]{1,0:T(8,128)(2,1)} %norm.1.nrm.refs_0_, ...), custom_call_target="tpu_custom_call" | custom-call | flops 7516192768 | bytes 19922944 | tf_op jit(solution)/shard_map/project/pallas_call | solution.py:121
  47.9 1.3 reduce_sum.58
  49.2 0.1 pad.15.clone
  49.3 0.7 pad_add_fusion.slots
  49.9 11.9 %cotangent.2 = (bf16[8,2048,128]{2,1,0:T(8,128)(2,1)}, bf16[1024,2048]{1,0:T(8,128)(2,1)}) custom-call(s32[1]{0:T(128)} %bitcast.slot.pos, bf16[1024,1024]{1,0:T(8,128)(2,1)} %refs_2_.3, bf16[512,1024]{1,0:T(8,128)(2,1)} %wout.3, bf16[2048,1024]{1,0:T(8,128)(2,1)} %wdown.3, bf16[1024,2048]{1,0:T(8,128)(2,1)} %get-tuple-element.60.slope), custom_call_target="tpu_custom_call" | custom-call | flops 5368709120 | bytes 15728640 | tf_op jit(solution)/shard_map/cotangent/pallas_call | solution.py:173
  61.9 0.5 collective-permute-start.2
  62.4 24.6 %project.3 = (bf16[8,2048,128]{2,1,0:T(8,128)(2,1)}, bf16[8,2048,128]{2,1,0:T(8,128)(2,1)}, bf16[8,2048,128]{2,1,0:T(8,128)(2,1)}, bf16[1024,2048]{1,0:T(8,128)(...) custom-call(s32[1]{0:T(128)} %bitcast.1.slot.pos, ...), custom_call_target="tpu_custom_call", output_to_operand_aliasing={{0}: (9, {}), {1}: (10, {}), {2}: (11, {})} | custom-call | flops 7516192768 | bytes 19922944 | tf_op jit(solution)/shard_map/project/pallas_call | solution.py:121
  86.9 55.6 %attend.1 = (bf16[2048,512]{1,0:T(8,128)(2,1)}, f32[8,2048,128]{2,1,0:T(8,128)}, bf16[8,36,256,256]{3,2,1,0:T(8,128)(2,1)}, f32[8,128]{1,0:T(8,128)}) custom-call(bf16[8,2048,128]{2,1,0:T(8,128)(2,1)} %get-tuple-element.51.q_ref, bf16[8,2048,128]{2,1,0:T(8,128)(2,1)} %get-tuple-element.52.k_ref, bf16[8,2048,128]{2,1,0:T(8,128)(2,1)} %get-tuple-element.53.v_ref), custom_call_target="tpu_custom_call" | custom-call | flops 19327352832 | bytes 41943040 | tf_op jit(solution)/shard_map/attend/pallas_call | solution.py:237
  142.6 9.9 %pair_matmul.5 = bf16[1024,1024]{1,0:T(8,128)(2,1)} custom-call(s32[1]{0:T(128)} %bitcast.1.slot.pos, bf16[2048,512]{1,0:T(8,128)(2,1)} %get-tuple-element.54.a.refs_0_.refs_1_, bf16[512,1024]{1,0:T(8,128)(2,1)} %wout.3, bf16[1024,2048]{1,0:T(8,128)(2,1)} %get-tuple-element.56.c.refs_1_, bf16[2048,1024]{1,0:T(8,128)(2,1)} %wdown.3), custom_call_target="tpu_custom_call" | custom-call | flops 5368709120 | bytes 12582912 | tf_op jit(solution)/shard_map/pair_matmul/pallas_call | solution.py:335
  152.5 1.6 collective-permute-start.1
  154.1 0.6 reduce_sum.59
  154.7 0.7 reduce_sum.57
  156.5 10.0 %pair_matmul.4.refs_0_ = bf16[1024,1024]{1,0:T(8,128)(2,1)} custom-call(s32[1]{0:T(128)} %bitcast.slot.pos, bf16[2048,512]{1,0:T(8,128)(2,1)} %get-tuple-element.54.a.refs_0_.refs_1_, bf16[512,1024]{1,0:T(8,128)(2,1)} %wout.3, bf16[1024,2048]{1,0:T(8,128)(2,1)} %get-tuple-element.55.c.refs_0_, bf16[2048,1024]{1,0:T(8,128)(2,1)} %wdown.3), custom_call_target="tpu_custom_call" | custom-call | flops 5368709120 | bytes 12582912 | tf_op jit(solution)/shard_map/pair_matmul/pallas_call | solution.py:335
  166.5 15.0 %weight_grad.6 = bf16[2048,1024]{1,0:T(8,128)(2,1)} custom-call(s32[2]{0:T(128)} %pad_add_fusion.slots, bf16[1024,2048]{1,0:T(8,128)(2,1)} %get-tuple-element.55.c.refs_0_, bf16[1024,2048]{1,0:T(8,128)(2,1)} %get-tuple-element.56.c.refs_1_, bf16[1024,1024]{1,0:T(8,128)(2,1)} %refs_2_.3, bf16[1024,1024]{1,0:T(8,128)(2,1)} %collective-permute-done.2.dy.refs_3_), custom_call_target="tpu_custom_call" | custom-call | flops 8589934592 | bytes 16777216 | tf_op jit(solution)/shard_map/weight_grad/pallas_call | solution.py:377
  181.5 0.0 all-reduce.8.cloned.1.call-start
  181.6 11.9 %cotangent.3 = (bf16[8,2048,128]{2,1,0:T(8,128)(2,1)}, bf16[1024,2048]{1,0:T(8,128)(2,1)}) custom-call(s32[1]{0:T(128)} %bitcast.1.slot.pos, bf16[1024,1024]{1,0:T(8,128)(2,1)} %collective-permute-done.2.dy.refs_3_, bf16[512,1024]{1,0:T(8,128)(2,1)} %wout.3, bf16[2048,1024]{1,0:T(8,128)(2,1)} %wdown.3, ...), custom_call_target="tpu_custom_call", output_to_operand_aliasing={{0}: (5, {})} | custom-call | flops 5368709120 | bytes 15728640 | tf_op jit(solution)/shard_map/cotangent/pallas_call | solution.py:173
  193.5 71.7 %attend_back.1.a.refs_2_.refs_3_ = bf16[2048,1536]{1,0:T(8,128)(2,1)} custom-call(bf16[8,2048,128]{2,1,0:T(8,128)(2,1)} %get-tuple-element.51.q_ref, bf16[8,2048,128]{2,1,0:T(8,128)(2,1)} %get-tuple-element.52.k_ref, bf16[8,2048,128]{2,1,0:T(8,128)(2,1)} %get-tuple-element.53.v_ref, bf16[8,2048,128]{2,1,0:T(8,128)(2,1)} %get-tuple-element.62.do_ref, ...), custom_call_target="tpu_custom_call" | custom-call | flops 38654705664 | bytes 83886080 | tf_op jit(solution)/shard_map/attend_back/pallas_call | solution.py:308
  265.2 13.1 %pair_matmul.7 = bf16[1024,1024]{1,0:T(8,128)(2,1)} custom-call(s32[1]{0:T(128)} %bitcast.1.slot.pos, bf16[2048,1536]{1,0:T(8,128)(2,1)} %attend_back.1.a.refs_2_.refs_3_, bf16[1024,1536]{1,0:T(8,128)(2,1)} %b.7, bf16[1024,2048]{1,0:T(8,128)(2,1)} %get-tuple-element.66.c.refs_3_, bf16[1024,2048]{1,0:T(8,128)(2,1)} %d.7), custom_call_target="tpu_custom_call" | custom-call | flops 7516192768 | bytes 16777216 | tf_op jit(solution)/shard_map/pair_matmul/pallas_call | solution.py:335
  278.3 0.6 collective-permute-start.3
  278.9 5.0 %output.1 = (bf16[1024,1024]{1,0:T(8,128)(2,1)}, f32[8,1024]{1,0:T(8,128)}) custom-call(bf16[1024,1024]{1,0:T(8,128)(2,1)} %x_ref.5, bf16[1024,1024]{1,0:T(8,128)(2,1)} %pair_matmul.4.refs_0_, bf16[1024,1024]{1,0:T(8,128)(2,1)} %collective-permute-done.1.refs_1_), custom_call_target="tpu_custom_call" | custom-call | flops 4194304 | bytes 8388608 | tf_op jit(solution)/shard_map/output/pallas_call | solution.py:578
  283.9 1.4 reduce_sum.56
  285.3 6.7 %weight_grad.5 = bf16[512,1024]{1,0:T(8,128)(2,1)} custom-call(s32[2]{0:T(128)} %pad_add_fusion.slots, bf16[2048,512]{1,0:T(8,128)(2,1)} %get-tuple-element.54.a.refs_0_.refs_1_, bf16[2048,512]{1,0:T(8,128)(2,1)} %get-tuple-element.54.a.refs_0_.refs_1_, bf16[1024,1024]{1,0:T(8,128)(2,1)} %refs_2_.3, bf16[1024,1024]{1,0:T(8,128)(2,1)} %collective-permute-done.2.dy.refs_3_), custom_call_target="tpu_custom_call" | custom-call | flops 2147483648 | bytes 7340032 | tf_op jit(solution)/shard_map/weight_grad/pallas_call | solution.py:377
  292.0 15.2 %weight_grad.7 = bf16[1024,2048]{1,0:T(8,128)(2,1)} custom-call(s32[2]{0:T(128)} %pad_add_fusion.slots, bf16[1024,1024]{1,0:T(8,128)(2,1)} %norm.1.nrm.refs_0_, bf16[1024,1024]{1,0:T(8,128)(2,1)} %collective-permute-done.nrm.refs_1_, bf16[1024,2048]{1,0:T(8,128)(2,1)} %get-tuple-element.65.c.refs_2_, bf16[1024,2048]{1,0:T(8,128)(2,1)} %get-tuple-element.66.c.refs_3_), custom_call_target="tpu_custom_call" | custom-call | flops 8589934592 | bytes 16777216 | tf_op jit(solution)/shard_map/weight_grad/pallas_call | solution.py:377
  307.3 0.0 all-reduce.8.cloned.1.call-update
  307.3 12.1 %weight_grad.4 = bf16[1024,1536]{1,0:T(8,128)(2,1)} custom-call(s32[2]{0:T(128)} %pad_add_fusion.slots, bf16[1024,1024]{1,0:T(8,128)(2,1)} %norm.1.nrm.refs_0_, bf16[1024,1024]{1,0:T(8,128)(2,1)} %collective-permute-done.nrm.refs_1_, bf16[2048,1536]{1,0:T(8,128)(2,1)} %attend_back.1.a.refs_2_.refs_3_, bf16[2048,1536]{1,0:T(8,128)(2,1)} %attend_back.1.a.refs_2_.refs_3_), custom_call_target="tpu_custom_call" | custom-call | flops 6442450944 | bytes 13631488 | tf_op jit(solution)/shard_map/weight_grad/pallas_call | solution.py:377
  319.4 13.2 %pair_matmul.6.refs_0_ = bf16[1024,1024]{1,0:T(8,128)(2,1)} custom-call(s32[1]{0:T(128)} %bitcast.slot.pos, bf16[2048,1536]{1,0:T(8,128)(2,1)} %attend_back.1.a.refs_2_.refs_3_, bf16[1024,1536]{1,0:T(8,128)(2,1)} %b.7, bf16[1024,2048]{1,0:T(8,128)(2,1)} %get-tuple-element.65.c.refs_2_, bf16[1024,2048]{1,0:T(8,128)(2,1)} %d.7), custom_call_target="tpu_custom_call" | custom-call | flops 7516192768 | bytes 16777216 | tf_op jit(solution)/shard_map/pair_matmul/pallas_call | solution.py:335
  332.6 70.1 %ring_sum.1 = bf16[2,8,4,16,1536]{4,3,2,1,0:T(8,128)(2,1)} custom-call(bf16[2,8,4,16,1536]{4,3,2,1,0:T(8,128)(2,1)} %bitcast.21), custom_call_target="tpu_custom_call" | custom-call | bytes 6291456 | tf_op jit(solution)/shard_map/ring_sum/pallas_call | solution.py:475
  402.7 1.3 select_maximum_fusion
  404.0 5.5 %bitcast_convert_fusion = f32[1024,1536]{1,0:T(8,128)} fusion(bf16[2,8,4,16,1536]{4,3,2,1,0:T(8,128)(2,1)} %ring_sum.1), kind=kLoop, calls=%fused_computation | loop fusion | flops 1572864 | bytes 9437184 | tf_op jit(solution)/shard_map/convert_element_type | solution.py:745
  409.5 1.3 copy-done.1
  410.8 7.7 %norm_back.1 = (f32[1024,1024]{1,0:T(8,128)}, f32[8,1024]{1,0:T(8,128)}, f32[8,1024]{1,0:T(8,128)}) custom-call(bf16[1024,1024]{1,0:T(8,128)(2,1)} %x_ref.5, bf16[1024,1024]{1,0:T(8,128)(2,1)} %refs_2_.3, f32[1,1024]{1,0:T(1,128)} %bitcast.26, bf16[1024,1024]{1,0:T(8,128)(2,1)} %pair_matmul.6.refs_0_, bf16[1024,1024]{1,0:T(8,128)(2,1)} %copy-done.1), custom_call_target="tpu_custom_call" | custom-call | flops 20971520 | bytes 12582912 | tf_op jit(solution)/shard_map/norm_back/pallas_call | solution.py:618
  418.5 0.8 reduce_sum.55
  419.3 0.8 reduce_sum.54
  420.0 0.7 maximum_maximum_fusion.x
  420.7 32.3 %small_sum.1 = f32[8,1024]{1,0:T(8,128)} custom-call(f32[8,1024]{1,0:T(8,128)} %maximum_maximum_fusion.x), custom_call_target="tpu_custom_call" | custom-call | tf_op jit(solution)/shard_map/small_sum/pallas_call | solution.py:529
  453.1 6.7 %convert_element_type.23 = f32[2048,1024]{1,0:T(8,128)} convert(bf16[2048,1024]{1,0:T(8,128)(2,1)} %all-reduce.6.cloned.1.call-done) | non-fusion elementwise | flops 2097152 | bytes 12582912 | tf_op jit(solution)/shard_map/convert_element_type | solution.py:748
  459.8 1.2 sqrt_bitcast_fusion
  461.0 1.4 fusion
  462.4 7.2 %all-reduce.8.cloned.1.call-done = (bf16[512,1024]{1,0:T(8,128)(2,1)}, bf16[1024,2048]{1,0:T(8,128)(2,1)}) async-done(((bf16[512,1024]{1,0:T(8,128)(2,1)}, bf16[1024,2048]{1,0:T(8,128)(2,1)}), (bf16[512,1024]{1,0:T(8,128)(2,1)}, bf16[1024,2048]{1,0:T(8,128)(2,1)})) %all-reduce.8.cloned.1.call-update) | async-done | bytes 5242896 | tf_op jit(solution)/shard_map/psum | solution.py:722
  469.6 2.8 convert_element_type.21
  472.4 6.7 %convert_element_type.22 = f32[1024,2048]{1,0:T(8,128)} convert(bf16[1024,2048]{1,0:T(8,128)(2,1)} %get-tuple-element.78) | non-fusion elementwise | flops 2097152 | bytes 12582912 | tf_op jit(solution)/shard_map/convert_element_type | solution.py:747
  (22 shorter events, 0.1 us)
Async XLA Ops:
  7.2 7.5 %copy-start.4 = (s32[1,4]{1,0:T(1,128)S(1)}, s32[1,4]{1,0:T(1,128)}, u32[]{:S(2)}) copy-start(s32[1,4]{1,0:T(1,128)} %param.11) | copy-start | bytes 52
  7.2 300.1 %all-reduce.6.cloned.1.call-start = ((), (), s32[]{:S(2)}) async-start(), calls=%async_computation | async-start | bytes 8388608 | tf_op jit(solution)/shard_map/psum | solution.py:717
  11.7 50.1 %collective-permute-start = (bf16[1024,1024]{1,0:T(8,128)(2,1)}, bf16[1024,1024]{1,0:T(8,128)(2,1)}, u32[]{:S(2)}, u32[]{:S(2)}) collective-permute-start(bf16[1024,1024]{1,0:T(8,128)(2,1)} %norm.1.nrm.refs_0_), channel_id=1, source_target_pairs={{1,0},{0,1},{3,2},{2,3},{5,4},{4,5},{7,6},{6,7},{9,8},{8,9},{11,10... | collective-permute-start | bytes 6291464 | tf_op jit(solution)/shard_map/ppermute | solution.py:691
  49.9 11.9 %copy-start = (bf16[1024,1024]{1,0:T(8,128)(2,1)S(1)}, bf16[1024,1024]{1,0:T(8,128)(2,1)}, u32[]{:S(2)}) copy-start(bf16[1024,1024]{1,0:T(8,128)(2,1)} %refs_2_.3) | copy-start | bytes 6291460
  61.9 104.7 %collective-permute-start.2 = (bf16[1024,1024]{1,0:T(8,128)(2,1)S(1)}, bf16[1024,1024]{1,0:T(8,128)(2,1)}, u32[]{:S(2)}, u32[]{:S(2)}) collective-permute-start(bf16[1024,1024]{1,0:T(8,128)(2,1)S(1)} %copy-done), channel_id=1, source_target_pairs={{1,0},{0,1},{3,2},{2,3},{5,4},{4,5},{7,6},{6,7},{9,8},{8,9},{11,10... | collective-permute-start | bytes 6291464 | tf_op jit(solution)/shard_map/ppermute | solution.py:693
  142.5 11.5 %copy-start.2 = (f32[8,512]{1,0:T(8,128)S(1)}, f32[8,512]{1,0:T(8,128)}, u32[]{:S(2)}) copy-start(f32[8,512]{1,0:T(8,128)} %get-tuple-element.73) | copy-start | bytes 49156
  142.6 12.2 %copy-start.3 = (f32[8,128]{1,0:T(8,128)S(1)}, f32[8,128]{1,0:T(8,128)}, u32[]{:S(2)}) copy-start(f32[8,128]{1,0:T(8,128)} %get-tuple-element.71) | copy-start | bytes 12292
  152.5 126.5 %collective-permute-start.1 = (bf16[1024,1024]{1,0:T(8,128)(2,1)}, bf16[1024,1024]{1,0:T(8,128)(2,1)}, u32[]{:S(2)}, u32[]{:S(2)}) collective-permute-start(bf16[1024,1024]{1,0:T(8,128)(2,1)} %pair_matmul.5), channel_id=1, source_target_pairs={{1,0},{0,1},{3,2},{2,3},{5,4},{4,5},{7,6},{6,7},{9,8},{8,9},{11,10... | collective-permute-start | bytes 6291464 | tf_op jit(solution)/shard_map/ppermute | solution.py:710
  181.5 288.1 %all-reduce.8.cloned.1.call-start = ((), (), s32[]{:S(2)}) async-start(), calls=%async_computation.1 | async-start | bytes 10485760 | tf_op jit(solution)/shard_map/psum | solution.py:722
  278.3 131.2 %collective-permute-start.3 = (bf16[1024,1024]{1,0:T(8,128)(2,1)}, bf16[1024,1024]{1,0:T(8,128)(2,1)S(1)}, u32[]{:S(2)}, u32[]{:S(2)}) collective-permute-start(bf16[1024,1024]{1,0:T(8,128)(2,1)} %pair_matmul.7), channel_id=1, source_target_pairs={{1,0},{0,1},{3,2},{2,3},{5,4},{4,5},{7,6},{6,7},{9,8},{8,9},{11,10... | collective-permute-start | bytes 6291464 | tf_op jit(solution)/shard_map/ppermute | solution.py:724
  409.5 1.3 copy-start.1
  453.1 6.7 %copy-start.5 = (f32[1,3]{1,0:T(1,128)S(1)}, f32[1,3]{1,0:T(1,128)}, u32[]{:S(2)}) copy-start(f32[1,3]{1,0:T(1,128)} %constant.46) | copy-start | bytes 40
Sparse Core Ops, SparseCore 0:
  181.7 111.8 all-reduce.5
  307.4 162.1 all-reduce.7

commit v3 on v2

v3 whole, which is shorter than its diff:
```python
import functools

import jax
import jax.numpy as jnp
from jax import lax
from jax.experimental import pallas as pl
from jax.experimental.pallas import tpu as pltpu
from jax.sharding import PartitionSpec as P

HEAD = 64
ROT = 16
LANES = 128
TILE = 256
CHUNK = 512
POINTS = 2
F32 = jnp.float32
BF = jnp.bfloat16

epsilon = 1e-05
rope_base = 10000.0
excluded = -1e20


def nn(a, b):
    return jnp.dot(a, b, preferred_element_type=F32)


def nt(a, b):
    return lax.dot_general(a, b, (((1,), (1,)), ((), ())), preferred_element_type=F32)


def tn(a, b):
    return lax.dot_general(a, b, (((0,), (0,)), ((), ())), preferred_element_type=F32)


def whole(shape):
    zeros = (0,) * len(shape)
    return pl.BlockSpec(shape, lambda *_: zeros, pipeline_mode=pl.Buffered(1))


def struct(shape, dtype):
    return jax.ShapeDtypeStruct(shape, dtype)


def cost(flops, nbytes, trans=0):
    return pl.CostEstimate(flops=int(flops), bytes_accessed=int(nbytes), transcendentals=int(trans))


def params(**kw):
    return pltpu.CompilerParams(vmem_limit_bytes=60 * 2**20, **kw)


def lane_ids(rows):
    return lax.broadcasted_iota(jnp.int32, (rows, LANES), 1)


def turn(x, cos, fwd, back):
    return x * cos + pltpu.roll(x, LANES - ROT // 2, 1) * fwd + pltpu.roll(x, ROT // 2, 1) * back


def gelu_parts(v):
    x = jnp.abs(v)
    bell = jnp.exp(v * v * (-0.5))
    base = 1.0 + x * (0.3275911 * 0.7071067811865476)
    t = pl.reciprocal(base, approx=True)
    poly = t * (
        0.254829592
        + t * (-0.284496736 + t * (1.421413741 + t * (-1.453152027 + t * 1.061405429)))
    )
    tail = 0.5 * poly * bell
    cdf = jnp.where(v >= 0, 1.0 - tail, tail)
    return v * cdf, cdf + v * bell * 0.3989422804014327


def ahead(count, product, use):
    held = product(0)
    for i in range(count):
        later = product(i + 1) if i + 1 < count else None
        use(i, held)
        held = later


def project_kernel(slot, nrm, wqkv, cos, fwd, back, hot, neg, *rest):
    q_out, k_out, v_out = rest[-3:]
    rows = nrm.shape[0]
    chunk = min(CHUNK, rows)
    lane = lane_ids(chunk)
    low = lane < HEAD
    one = jnp.where(lane < HEAD + 2, 1.0, 0.0)

    def place(y, r):
        blocks = [y[:, i : i + LANES] for i in range(0, y.shape[1], LANES)]
        sides = []
        for g0, g1, g2 in zip(blocks[::3], blocks[1::3], blocks[2::3]):
            r1, r2 = pltpu.roll(g1, HEAD, 1), pltpu.roll(g2, HEAD, 1)
            sides += [(g0, g1), (jnp.where(low, r1, r2), r2)]
        for h, (qk, v) in enumerate(sides):
            qk = turn(qk, cos[r, :], fwd[r, :], back[r, :])
            q_out[h, r, :] = jnp.where(low, qk * HEAD**-0.5, hot[r, :].astype(F32)).astype(BF)
            k_out[h, r, :] = jnp.where(low, pltpu.roll(qk, HEAD, 1), neg[r, :].astype(F32)).astype(BF)
            v_out[h, r, :] = jnp.where(low, v, one).astype(BF)

    ahead(
        rows // chunk,
        lambda i: nn(nrm[i * chunk : (i + 1) * chunk, :], wqkv[...]),
        lambda i, y: place(y, pl.ds(i * chunk, chunk)),
    )


def project(slot, total, heads, prior, nrm, wqkv, cos, fwd, back, hot, neg):
    rows, d = nrm.shape
    per = 4 if heads % 4 == 0 else 2
    at = pl.BlockSpec((rows, LANES), lambda j, slot: (slot[0], 0), pipeline_mode=pl.Buffered(1))
    hd = pl.BlockSpec((per, rows, LANES), lambda j, slot: (j, slot[0], 0))
    big = struct((heads, total, LANES), BF)
    return pl.pallas_call(
        project_kernel,
        grid_spec=pltpu.PrefetchScalarGridSpec(
            num_scalar_prefetch=1,
            grid=(heads // per,),
            in_specs=[whole(nrm.shape), pl.BlockSpec((d, per * 3 * HEAD), lambda j, slot: (0, j)), at, at, at, at, at]
            + [pl.BlockSpec(memory_space=pl.ANY)] * len(prior),
            out_specs=[hd, hd, hd],
        ),
        out_shape=[big, big, big],
        input_output_aliases={8 + i: i for i in range(len(prior))},
        compiler_params=params(),
        cost_estimate=cost(2 * rows * d * wqkv.shape[1], 2 * (d * wqkv.shape[1] + 6 * rows * d)),
        name="project",
    )(slot, nrm, wqkv, cos, fwd, back, hot, neg, *prior)


def feed_kernel(extra, slot, nrm, dy, win, wdown, wout, *refs):
    prior = refs[:2] if extra else ()
    do_out, update, back, gdown, gin, sq, turned, act, gpre = refs[extra:]
    j = pl.program_id(0)
    rows, d = nrm.shape
    chunk = min(TILE, rows)
    span = [pl.ds(i * chunk, chunk) for i in range(rows // chunk)]

    @pl.when(j == 0)
    def _():
        sq[...] = jnp.zeros_like(sq)
        update[...] = jnp.zeros_like(update)
        back[...] = jnp.zeros_like(back)
        turned[...] = jnp.transpose(nrm[...])
        low = lane_ids(chunk) < HEAD
        for r in span:
            g = nt(dy[r, :], wout[...])
            for p in range(g.shape[1] // LANES):
                y = g[:, p * LANES : (p + 1) * LANES]
                do_out[2 * p, r, :] = jnp.where(low, y, 0.0).astype(BF)
                do_out[2 * p + 1, r, :] = jnp.where(low, pltpu.roll(y, HEAD, 1), 0.0).astype(BF)

    def products(i):
        return nn(nrm[span[i], :], win[...]), nt(dy[span[i], :], wdown[...])

    def use(i, held):
        r = span[i]
        a, slope = gelu_parts(held[0])
        a = a.astype(BF)
        g = (held[1] * slope).astype(BF)
        act[r, :] = a
        gpre[r, :] = g
        wide = a.astype(F32)
        sq[...] += jnp.sum((wide * wide).reshape(chunk // 8, 8, -1), axis=0)
        pass

    ahead(len(span), products, use)
    update[...] += nn(act[...], wdown[...])
    back[...] += nt(gpre[...], win[...])
    down, into = tn(act[...], dy[...]), nn(turned[...], gpre[...])
    if extra:
        down, into = down + prior[0][...].astype(F32), into + prior[1][...].astype(F32)
    gdown[...] = down.astype(BF)
    gin[...] = into.astype(BF)


def feed(slot, piece, pieces, total, heads, prior, nrm, dy, win, wdown, wout):
    rows, d = nrm.shape
    f = win.shape[1]
    tile = min(512, f)
    by_row = pl.BlockSpec((tile, d), lambda j, slot: (j, 0))
    by_col = pl.BlockSpec((d, tile), lambda j, slot: (0, j))
    stay = pl.BlockSpec((rows, d), lambda j, slot: (piece, 0), pipeline_mode=pl.Buffered(1))
    any_ = pl.BlockSpec(memory_space=pl.ANY)
    return pl.pallas_call(
        functools.partial(feed_kernel, len(prior)),
        grid_spec=pltpu.PrefetchScalarGridSpec(
            num_scalar_prefetch=1,
            grid=(f // tile,),
            in_specs=[whole(nrm.shape), whole(dy.shape), by_col, by_row, whole(wout.shape)]
            + [by_row, by_col, any_, any_, any_][: len(prior)],
            out_specs=[
                pl.BlockSpec((heads, rows, LANES), lambda j, slot: (0, slot[0], 0), pipeline_mode=pl.Buffered(1)),
                stay, stay, by_row, by_col,
                pl.BlockSpec((8, tile), lambda j, slot: (0, 0)),
            ],
            scratch_shapes=[pltpu.VMEM((d, rows), BF), pltpu.VMEM((rows, tile), BF), pltpu.VMEM((rows, tile), BF)],
        ),
        out_shape=[
            struct((heads, total, LANES), BF),
            struct((rows * pieces, d), F32), struct((rows * pieces, d), F32),
            struct((f, d), BF), struct((d, f), BF),
            struct((8, tile), F32),
        ],
        input_output_aliases={8 + i: i for i in range(len(prior) - 2)},
        compiler_params=params(),
        cost_estimate=cost(12 * rows * d * f, 12 * d * f + 20 * rows * d),
        name="feed",
    )(slot, nrm, dy, win, wdown, wout, *prior)


def attend_kernel(pairs, shapes, q_ref, k_ref, v_ref, *refs):
    count = len(shapes)
    xs, (ctx, wide, keep, sq), done, refs = refs[:count], refs[count : count + 4], refs[count + 4 : 2 * count + 4], refs[2 * count + 4 :]
    hold, (sems,), refs = refs[:count], refs[count : count + 1], refs[count + 1 :]
    names = Ring.SUM
    rings = [
        Ring(shape, x=xs[k], **dict(zip(names, refs[k * len(names) : (k + 1) * len(names)])))
        for k, shape in enumerate(shapes)
    ]
    chips = rings[0].chips

    def advance(s):
        for k, ring in enumerate(rings):

            def place(d, value, k=k):
                hold[k][d] = value

            ring.sum_step(s, place)

    @pl.when(pl.program_id(0) == 0)
    def _():
        rings[0].meet()
        for ring in rings:
            ring.sum_begin()

    total = q_ref.shape[1]
    b = TILE
    tri = lax.broadcasted_iota(jnp.int32, (b, b), 0) >= lax.broadcasted_iota(jnp.int32, (b, b), 1)
    low = lane_ids(b) < HEAD

    @pl.when(pl.program_id(0) == 0)
    def _():
        sq[...] = jnp.zeros_like(sq)

    def scores(h, i):
        return nt(q_ref[h, i * b : (i + 1) * b, :], k_ref[h, : (i + 1) * b, :])

    def weights(s, h, i):
        s_diag = jnp.where(tri, s[:, i * b :], excluded)
        top = jnp.max(s_diag, axis=1, keepdims=True)
        if i:
            top = jnp.maximum(top, jnp.max(s[:, : i * b], axis=1, keepdims=True))
        w = jnp.exp(s_diag - top).astype(BF)
        if i:
            w = jnp.concatenate([jnp.exp(s[:, : i * b] - top).astype(BF), w], axis=1)
        for j in range(i + 1):
            keep[h, i * (i + 1) // 2 + j] = w[:, j * b : (j + 1) * b]
        return w

    def finish(w, h, i):
        rows = pl.ds(i * b, b)
        acc = nn(w, v_ref[h, : (i + 1) * b, :])
        inv = 1.0 / acc[:, HEAD : HEAD + 1]
        acc = acc * inv
        wide[h, rows, :] = jnp.where(low, acc, inv)
        return acc

    items = [(h, i) for i in range(total // b) for h in range(2)]
    places = Places(sum(i + 1 for _, i in items), pairs, chips, advance)
    s = scores(*items[0])
    left = None
    for t, (h, i) in enumerate(items):
        s_next = scores(*items[t + 1]) if t + 1 < len(items) else None
        acc = finish(weights(s, h, i), h, i)
        if h == 0:
            left = acc
        else:
            both = jnp.where(low, left, pltpu.roll(acc, HEAD, 1)).astype(BF)
            ctx[i * b : (i + 1) * b, :] = both
            both = both.astype(F32)
            sq[...] += jnp.sum((both * both).reshape(b // 8, 8, LANES), axis=0)
        s = s_next
        places.add(i + 1)

    @pl.when(pl.program_id(0) == pairs - 1)
    def _():
        out = [pltpu.make_async_copy(hold[k], done[k], sems.at[k]) for k in range(count)]
        for c in out:
            c.start()
        for ring in rings:
            ring.sum_finish()
        for c in out:
            c.wait()


def attend(q, k, v, xs, collective_id):
    cuts = [Ring.cut(x) for x in xs]
    shapes = [c.shape for c in cuts]
    any_ = pl.BlockSpec(memory_space=pl.ANY)
    heads, total, _ = q.shape
    tiles = total // TILE
    tiles = tiles * (tiles + 1) // 2
    hd = pl.BlockSpec((2, total, LANES), lambda p: (p, 0, 0))
    return pl.pallas_call(
        functools.partial(attend_kernel, heads // 2, shapes),
        grid=(heads // 2,),
        in_specs=[hd, hd, hd] + [any_] * len(xs),
        out_specs=[
            pl.BlockSpec((total, LANES), lambda p: (0, p)),
            hd,
            pl.BlockSpec((2, tiles, TILE, TILE), lambda p: (p, 0, 0, 0)),
            pl.BlockSpec((8, LANES), lambda p: (0, 0)),
        ]
        + [any_] * len(xs),
        out_shape=[
            struct((total, heads * HEAD), BF),
            struct((heads, total, LANES), F32),
            struct((heads, tiles, TILE, TILE), BF),
            struct((8, LANES), F32),
        ]
        + [struct(c[2:], BF) for c in shapes],
        scratch_shapes=[pltpu.VMEM(c[2:], BF) for c in shapes]
        + [pltpu.SemaphoreType.DMA((len(xs),))]
        + [r for c in shapes for r in Ring.sum_scratch(c)],
        compiler_params=params(collective_id=collective_id, has_side_effects=True),
        cost_estimate=cost(4 * heads * tiles * TILE * TILE * 256, heads * total * LANES * 20, heads * tiles * TILE * TILE),
        name="attend",
    )(q, k, v, *cuts)


def attend_back_kernel(pairs, shapes, q_ref, k_ref, v_ref, do_ref, wide, keep, cos, fwd, back, *refs):
    count = len(shapes)
    done, out, totals, refs = refs[:count], refs[count], refs[count + 1 : 2 * count + 1], refs[2 * count + 1 :]
    (dk_acc, dv_acc, dq_acc, sems), refs = refs[:4], refs[4:]
    hold, refs = refs[:count], refs[count:]
    names = Ring.SPREAD
    rings = [
        Ring(shape, out=totals[k], **dict(zip(names, refs[k * len(names) : (k + 1) * len(names)])))
        for k, shape in enumerate(shapes)
    ]
    chips = rings[0].chips

    @pl.when(pl.program_id(0) == 0)
    def _():
        loads = [pltpu.make_async_copy(done[k], hold[k], sems.at[k]) for k in range(count)]
        for c in loads:
            c.start()
        rings[0].meet()
        for k, ring in enumerate(rings):
            loads[k].wait()
            for d in range(ring.parts):
                ring.full[ring.chunk(chips - 1, d), d] = hold[k][d]
                ring.spread_part(d)

    def advance(s):
        for ring in rings:
            ring.spread_step(s + 1)

    total = q_ref.shape[1]
    b = TILE
    lane = lane_ids(b)
    low = lane < HEAD

    def probs(h, i):
        w = [keep[h, i * (i + 1) // 2 + j] for j in range(i + 1)]
        return w[0] if i == 0 else jnp.concatenate(w, axis=1)

    def begin(h, i):
        rows = pl.ds(i * b, b)
        context = wide[h, rows, :]
        inv = context[:, HEAD : HEAD + 1]
        scaled = (do_ref[h, rows, :].astype(F32) * inv).astype(BF)
        grad = scaled.astype(F32)
        delta = jnp.sum(jnp.where(low, grad * context, 0.0), axis=1, keepdims=True)
        delta_hi = delta.astype(BF).astype(F32)
        delta_lo = delta - delta_hi
        joined = jnp.where(lane == HEAD, -delta_hi, jnp.where(lane == HEAD + 1, -delta_lo, grad)).astype(BF)
        return scaled, nt(joined, v_ref[h, : (i + 1) * b, :])

    def finish(h, i, scaled, dp):
        n = (i + 1) * b
        rows = pl.ds(i * b, b)
        w = probs(h, i)
        ds = w * dp.astype(BF)
        dq_acc[h, rows, :] = nn(ds, k_ref[h, :n, :]) * HEAD**-0.5
        dk = tn(ds, q_ref[h, rows, :])
        dv = tn(w, scaled)
        if i:
            dk_acc[h, : i * b, :] += dk[: i * b]
            dv_acc[h, : i * b, :] += dv[: i * b]
        dk_acc[h, rows, :] = dk[i * b :]
        dv_acc[h, rows, :] = dv[i * b :]

    items = [(h, i) for i in range(total // b) for h in range(2)]
    places = Places(sum(i + 1 for _, i in items), pairs, chips - 1, advance)
    state = begin(*items[0])
    for t, item in enumerate(items):
        later = begin(*items[t + 1]) if t + 1 < len(items) else None
        finish(*item, *state)
        state = later
        places.add(item[1] + 1)
    for i in range(total // b):
        rows = pl.ds(i * b, b)
        x = [
            turn(
                jnp.where(low, dq_acc[h, rows, :], pltpu.roll(dk_acc[h, rows, :], HEAD, 1)),
                cos[rows, :], -fwd[rows, :], -back[rows, :],
            )
            for h in range(2)
        ]
        r = pltpu.roll(x[1], HEAD, 1)
        out[rows, :LANES] = x[0].astype(BF)
        out[rows, LANES : 2 * LANES] = jnp.where(low, dv_acc[0, rows, :], r).astype(BF)
        out[rows, 2 * LANES :] = jnp.where(low, r, pltpu.roll(dv_acc[1, rows, :], HEAD, 1)).astype(BF)

    @pl.when(pl.program_id(0) == pairs - 1)
    def _():
        for ring in rings:
            ring.spread_finish()


def attend_back(q, k, v, do, wide, keep, cos, fwd, back, done, likes, collective_id):
    shapes = [jax.eval_shape(Ring.cut, x).shape for x in likes]
    any_ = pl.BlockSpec(memory_space=pl.ANY)
    heads, total, _ = q.shape
    hd = pl.BlockSpec((2, total, LANES), lambda p: (p, 0, 0))
    acc = pltpu.VMEM((2, total, LANES), F32)
    tiles = keep.shape[1]
    grad, *totals = pl.pallas_call(
        functools.partial(attend_back_kernel, heads // 2, shapes),
        grid=(heads // 2,),
        in_specs=[hd, hd, hd, hd, hd, pl.BlockSpec((2,) + keep.shape[1:], lambda p: (p, 0, 0, 0))]
        + [whole(cos.shape)] * 3
        + [any_] * len(done),
        out_specs=[pl.BlockSpec((total, 384), lambda p: (0, p))] + [any_] * len(done),
        out_shape=[struct((total, heads * 3 * HEAD), BF)] + [struct(c, BF) for c in shapes],
        scratch_shapes=[acc] * 3
        + [pltpu.SemaphoreType.DMA((len(done),))]
        + [pltpu.VMEM(c[2:], BF) for c in shapes]
        + [r for c in shapes for r in Ring.spread_scratch(c)],
        compiler_params=params(collective_id=collective_id, has_side_effects=True),
        cost_estimate=cost(8 * heads * tiles * TILE * TILE * 256, heads * total * LANES * 40),
        name="attend_back",
    )(q, k, v, do, wide, keep, cos, fwd, back, *done)
    return grad, *[t.reshape(x.shape) for t, x in zip(totals, likes)]


def join_kernel(transposed, slot, a, b, c, out):
    out[...] = ((nt if transposed else nn)(a[...], b[...]) + c[...]).astype(BF)


def join(slot, transposed, a, b, c):
    rows, width = c.shape
    tile = min(CHUNK, rows)
    step = pl.BlockSpec((tile, width), lambda i, slot: (i, 0))
    return pl.pallas_call(
        functools.partial(join_kernel, transposed),
        grid_spec=pltpu.PrefetchScalarGridSpec(
            num_scalar_prefetch=1,
            grid=(rows // tile,),
            in_specs=[
                pl.BlockSpec((tile, a.shape[1]), lambda i, slot: (slot[0] * (rows // tile) + i, 0)),
                whole(b.shape),
                step,
            ],
            out_specs=step,
        ),
        out_shape=struct((rows, width), BF),
        compiler_params=params(),
        cost_estimate=cost(2 * rows * width * a.shape[1], 2 * (b.size + rows * (3 * width + a.shape[1]))),
        name="join",
    )(slot, a, b, c)


def weight_kernel(n, index, *refs):
    groups, outs = [refs[i * n : (i + 1) * n] for i in range(4)], refs[4 * n :]
    for xs, ys, out in ((groups[0], groups[1], outs[0]), (groups[2], groups[3], outs[1])):
        width = out.shape[1]
        step = 512 if width % 512 == 0 else 128
        for c in range(width // step):
            cols = pl.ds(c * step, step)
            out[:, cols] = sum(tn(x[...], y[:, cols]) for x, y in zip(xs, ys)).astype(BF)


def weight_grads(index, x1, y1, x2, y2):
    n, d = len(x1), x1[0].shape[1]
    tile = 256
    left = [pl.BlockSpec((x.shape[0], tile), lambda j, index: (0, j)) for x in x1]
    right = lambda y: [
        pl.BlockSpec(
            (x.shape[0], y.shape[1]), functools.partial(lambda s, j, index: (index[s], 0), s), pipeline_mode=pl.Buffered(1)
        )
        for s, x in enumerate(x1)
    ]
    widths = (y1.shape[1], y2.shape[1])
    return pl.pallas_call(
        functools.partial(weight_kernel, n),
        grid_spec=pltpu.PrefetchScalarGridSpec(
            num_scalar_prefetch=1,
            grid=(d // tile,),
            in_specs=left + right(y1) + left + right(y2),
            out_specs=[pl.BlockSpec((tile, w), lambda j, index: (j, 0)) for w in widths],
        ),
        out_shape=[struct((d, w), BF) for w in widths],
        compiler_params=params(),
        cost_estimate=cost(2 * y1.shape[0] * d * sum(widths), 2 * y1.shape[0] * (2 * d + sum(widths)) + 2 * d * sum(widths)),
        name="weight_grads",
    )(index, *x1, *[y1] * n, *x2, *[y2] * n)


class Ring:
    SUM = ("near", "part", "far", "own_sem", "core_sem", "rs_send", "rs_recv")
    SPREAD = ("full", "keep_sem", "ag_send", "ag_recv", "fin_send", "fin_recv")

    def __init__(self, shape, **refs):
        self.__dict__.update(refs)
        self.chips, self.parts = shape[1], shape[2]
        dp = lax.axis_index("dp")
        self.core, chip = lax.rem(dp, 2), dp // 2
        y, z = lax.rem(chip, 2), chip // 2
        self.p = z * (1 - y) + (self.chips - 1 - z) * y
        self.peer = dp + 1 - 2 * self.core
        self.ends = [self.device(lax.rem(self.p + 1, self.chips)), self.device(lax.rem(self.p + self.chips - 1, self.chips))]

    @staticmethod
    def sum_scratch(shape):
        chips, parts = shape[1], shape[2]
        dma = pltpu.SemaphoreType.DMA
        half = pltpu.VMEM(shape[1:], BF)
        return [half, half, pltpu.VMEM((chips - 1,) + shape[2:], BF), dma((1,)), dma((2, chips)), dma((chips - 1, parts)), dma((chips - 1, parts))]

    @staticmethod
    def spread_scratch(shape):
        chips, parts = shape[1], shape[2]
        dma = pltpu.SemaphoreType.DMA
        return [pltpu.VMEM(shape[1:], BF), dma((1,))] + [dma((chips - 1, parts))] * 2 + [dma((chips, parts))] * 2

    @staticmethod
    def cut(x):
        chips = lax.axis_size("dp") // 2
        rows, d = x.shape
        parts = min(8, rows // (32 * chips))
        return x.reshape(2, chips, parts, rows // (2 * chips * parts), d)

    def device(self, pos):
        high = pos // (self.chips // 2)
        return ((1 - high) * 2 * pos + high * (2 * (self.chips - 1 - pos) + 1)) * 2 + self.core

    def remote(self, src, dst, send, recv, t):
        return pltpu.make_async_remote_copy(
            src_ref=src, dst_ref=dst, send_sem=send, recv_sem=recv,
            device_id={"dp": t}, device_id_type=pl.DeviceIdType.MESH,
        )

    def chunk(self, s, d):
        return lax.rem(self.p + 2 * self.chips - s, self.chips) if d % 2 == 0 else lax.rem(self.p + s, self.chips)

    def swap(self, c):
        return self.remote(
            self.x.at[1 - self.core, c], self.near.at[c], self.core_sem.at[0, c], self.core_sem.at[1, c], self.peer
        )

    def reduce(self, s, d):
        return self.remote(
            self.part.at[self.chunk(s, d), d], self.far.at[s, d], self.rs_send.at[s, d], self.rs_recv.at[s, d], self.ends[d % 2]
        )

    def gather(self, s, d):
        ref = self.full.at[self.chunk(self.chips - 1 + s, d), d]
        return self.remote(ref, ref, self.ag_send.at[s, d], self.ag_recv.at[s, d], self.ends[d % 2])

    def across(self, s, d, half):
        c = self.chunk(self.chips - 1 + s, d)
        return self.remote(self.full.at[c, d], self.out.at[half, c, d], self.fin_send.at[s, d], self.fin_recv.at[s, d], self.peer)

    def mine(self):
        return pltpu.make_async_copy(self.x.at[self.core], self.part, self.own_sem.at[0])

    def keep(self):
        return pltpu.make_async_copy(self.full, self.out.at[self.core], self.keep_sem.at[0])

    @staticmethod
    def add(a, b):
        return (a.astype(F32) + b.astype(F32)).astype(BF)

    def meet(self):
        barrier = pltpu.get_barrier_semaphore()
        for t in (*self.ends, self.peer):
            pl.semaphore_signal(barrier, inc=1, device_id={"dp": t}, device_id_type=pl.DeviceIdType.MESH)
        pl.semaphore_wait(barrier, 3)

    def sum_begin(self):
        self.mine().start()
        for c in range(self.chips):
            self.swap(c).start()

    def sum_step(self, s, place):
        chips, parts, part, far = self.chips, range(self.parts), self.part, self.far

        @pl.when(s == 0)
        def _():
            self.mine().wait()

            def settle(c, carry):
                self.swap(c).wait_recv()
                part[c] = self.add(part[c], self.near[c])
                return carry

            lax.fori_loop(0, chips, settle, 0)
            for d in parts:
                self.reduce(0, d).start()

        @pl.when((s > 0) & (s < chips - 1))
        def _():
            for d in parts:
                self.reduce(s - 1, d).wait_recv()
                c = self.chunk(s, d)
                part[c, d] = self.add(part[c, d], far[s - 1, d])
                self.reduce(s, d).start()

        @pl.when(s == chips - 1)
        def _():
            for d in parts:
                self.reduce(chips - 2, d).wait_recv()
                place(d, self.add(part[self.chunk(chips - 1, d), d], far[chips - 2, d]))

    def sum_finish(self):
        for c in range(self.chips):
            self.swap(c).wait_send()
        for d in range(self.parts):
            for s in range(self.chips - 1):
                self.reduce(s, d).wait_send()

    def spread_part(self, d):
        self.gather(0, d).start()
        self.across(0, d, self.core).start()

    def spread_step(self, s):
        chips, parts = self.chips, range(self.parts)

        @pl.when((s > 0) & (s < chips - 1))
        def _():
            for d in parts:
                self.gather(s - 1, d).wait_recv()
                self.gather(s, d).start()
                self.across(s, d, self.core).start()

        @pl.when(s == chips - 1)
        def _():
            for d in parts:
                self.gather(chips - 2, d).wait_recv()
                self.across(chips - 1, d, self.core).start()

    def spread_finish(self):
        self.keep().start()
        for d in range(self.parts):
            for s in range(self.chips - 1):
                self.gather(s, d).wait_send()
            for s in range(self.chips):
                self.across(s, d, self.core).wait_send()
                self.across(s, d, 1 - self.core).wait_recv()
        self.keep().wait()


def paced(place, places, limit, step):
    lax.fori_loop((place * limit) // places, ((place + 1) * limit) // places, lambda s, carry: (step(s), carry)[1], 0)


class Places:
    def __init__(self, work, per_grid, limit, step):
        self.work, self.total, self.limit, self.step, self.done, self.point = work, POINTS * per_grid, limit, step, 0, 0

    def add(self, work):
        self.done += work
        if self.done * POINTS >= (self.point + 1) * self.work:
            paced(pl.program_id(0) * POINTS + self.point, self.total, self.limit, self.step)
            self.point += 1


def tail_kernel(steps, others, shapes, gqkv, context, wqkv, wout, back, update, hidden, *refs):
    count = len(shapes)
    sent, refs = refs[:others], refs[others:]
    xs, (share, result, sq), refs = refs[:count], refs[count : count + 3], refs[count + 3 :]
    outs, refs = refs[:count], refs[count:]
    (own_grad, own_context, sems), refs = refs[:3], refs[3:]
    rings = []
    for k, shape in enumerate(shapes):
        names = Ring.SUM + Ring.SPREAD
        rings.append(Ring(shape, x=xs[k], out=outs[k], **dict(zip(names, refs[k * len(names) : (k + 1) * len(names)]))))
    chips = rings[0].chips
    i = pl.program_id(0)
    rows = own_grad.shape[0]
    height = back.shape[0]
    limit = 2 * chips - 1
    base = pl.ds(lax.axis_index("mp") * rows, rows)
    fetch = [
        pltpu.make_async_copy(gqkv.at[base], own_grad, sems.at[0]),
        pltpu.make_async_copy(context.at[base], own_context, sems.at[1]),
    ]

    @pl.when(i == 0)
    def _():
        for c in fetch:
            c.start()
        rings[0].meet()
        for ring in rings:
            ring.sum_begin()
        sq[...] = jnp.zeros_like(sq)
        for c in fetch:
            c.wait()

    def advance(s):
        for ring in rings:

            def place(d, value, ring=ring):
                ring.full[ring.chunk(chips - 1, d), d] = value
                ring.spread_part(d)

            ring.sum_step(s, place)
            ring.spread_step(s - (chips - 1))

    paced(i, steps, limit, advance)
    here = pl.ds(i * height, height)
    share[...] = (nt(own_grad[here, :], wqkv[...]) + back[...]).astype(BF)
    y = (nn(own_context[here, :], wout[...]) + update[...]).astype(BF).astype(F32)
    y = hidden[...].astype(F32) + (y + sum(p[...].astype(F32) for p in sent))
    result[...] = y.astype(BF)
    sq[...] += jnp.sum((y * y).reshape(height // 8, 8, -1), axis=0)

    @pl.when(i == steps - 1)
    def _():
        for ring in rings:
            ring.sum_finish()
            ring.spread_finish()


def tail(xs, gqkv, context, wqkv, wout, back, update, hidden, sent, collective_id):
    cuts = [Ring.cut(x) for x in xs]
    shapes = [c.shape for c in cuts]
    rows, d = hidden.shape
    steps = 16
    any_ = pl.BlockSpec(memory_space=pl.ANY)
    row = pl.BlockSpec((rows // steps, d), lambda i: (i, 0))
    share, result, sq, *totals = pl.pallas_call(
        functools.partial(tail_kernel, steps, len(sent), shapes),
        grid=(steps,),
        in_specs=[any_, any_, whole(wqkv.shape), whole(wout.shape), row, row, row] + [row] * len(sent) + [any_] * len(xs),
        out_specs=[row, row, pl.BlockSpec((8, d), lambda i: (0, 0))] + [any_] * len(xs),
        out_shape=[struct((rows, d), BF), struct((rows, d), BF), struct((8, d), F32)] + [struct(c, BF) for c in shapes],
        scratch_shapes=[
            pltpu.VMEM((rows, gqkv.shape[1]), BF), pltpu.VMEM((rows, context.shape[1]), BF), pltpu.SemaphoreType.DMA((2,)),
        ]
        + [r for c in shapes for r in Ring.sum_scratch(c) + Ring.spread_scratch(c)],
        compiler_params=params(collective_id=collective_id, has_side_effects=True),
        cost_estimate=cost(2 * rows * d * (gqkv.shape[1] + context.shape[1]), sum(4 * x.size for x in xs) + 20 * rows * d),
        name="tail",
    )(gqkv, context, wqkv, wout, back, update, hidden, *sent, *cuts)
    return share, result, sq, *[t.reshape(x.shape) for t, x in zip(totals, xs)]


def small_kernel(n_dp, n_mp, x, out, held, kept, send, recv):
    me = lax.axis_index("dp") * n_mp + lax.axis_index("mp")
    rounds = held.shape[0]

    def target(k):
        t = me + 2**k * (1 - 2 * lax.rem(me // 2**k, 2))
        return dict(device_id={"dp": t // n_mp, "mp": lax.rem(t, n_mp)}, device_id_type=pl.DeviceIdType.MESH)

    barrier = pltpu.get_barrier_semaphore()
    for k in range(rounds):
        pl.semaphore_signal(barrier, inc=1, **target(k))
    pl.semaphore_wait(barrier, rounds)
    kept[0] = x[...]
    for k in range(rounds):
        copy = pltpu.make_async_remote_copy(
            src_ref=kept.at[k], dst_ref=held.at[k], send_sem=send.at[k], recv_sem=recv.at[k], **target(k)
        )
        copy.start()
        copy.wait()
        kept[k + 1] = kept[k] + held[k]
    out[...] = kept[rounds]


def small_sum(x, collective_id):
    n_dp, n_mp = lax.axis_size("dp"), lax.axis_size("mp")
    rounds = (n_dp * n_mp).bit_length() - 1
    dma = pltpu.SemaphoreType.DMA
    vmem = pl.BlockSpec(memory_space=pltpu.VMEM)
    return pl.pallas_call(
        functools.partial(small_kernel, n_dp, n_mp),
        out_shape=struct(x.shape, F32),
        in_specs=[vmem],
        out_specs=vmem,
        scratch_shapes=[
            pltpu.VMEM((rounds,) + x.shape, F32), pltpu.VMEM((rounds + 1,) + x.shape, F32), dma((rounds,)), dma((rounds,)),
        ],
        compiler_params=params(collective_id=collective_id, has_side_effects=True),
        name="small_sum",
    )(x)


def norm_kernel(x_ref, scale, bias, out):
    x = x_ref[...].astype(F32)
    mean = jnp.mean(x, axis=1, keepdims=True)
    centred = x - mean
    var = jnp.mean(centred * centred, axis=1, keepdims=True)
    out[...] = (centred * lax.rsqrt(var + epsilon) * scale[...] + bias[...]).astype(BF)


def norm(x, scale, bias):
    rows, d = x.shape
    tile = pl.BlockSpec((min(TILE, rows), d), lambda i: (i, 0))
    return pl.pallas_call(
        norm_kernel,
        grid=(rows // min(TILE, rows),),
        in_specs=[tile, whole((1, d)), whole((1, d))],
        out_specs=tile,
        out_shape=struct((rows, d), BF),
        compiler_params=params(),
        cost_estimate=cost(10 * rows * d, 4 * rows * d),
        name="norm",
    )(x, scale, bias)


def norm_back_kernel(n, x_ref, dy, scale, *refs):
    parts, out, gain, bias = refs[:n], refs[n], refs[n + 1], refs[n + 2]

    @pl.when(pl.program_id(0) == 0)
    def _():
        gain[...] = jnp.zeros_like(gain)
        bias[...] = jnp.zeros_like(bias)

    x = x_ref[...].astype(F32)
    mean = jnp.mean(x, axis=1, keepdims=True)
    centred = x - mean
    var = jnp.mean(centred * centred, axis=1, keepdims=True)
    inv = lax.rsqrt(var + epsilon)
    unit = centred * inv
    grad = sum(p[...].astype(F32) for p in parts)
    g = grad * scale[...]
    out[...] = dy[...].astype(F32) + inv * (
        g - jnp.mean(g, axis=1, keepdims=True) - unit * jnp.mean(g * unit, axis=1, keepdims=True)
    )
    fold = lambda v: jnp.sum(v.reshape(v.shape[0] // 8, 8, -1), axis=0)
    gain[...] += fold(grad * unit)
    bias[...] += fold(grad)


def norm_back(x, dy, scale, parts):
    rows, d = x.shape
    tile = pl.BlockSpec((min(TILE, rows), d), lambda i: (i, 0))
    acc = pl.BlockSpec((8, d), lambda i: (0, 0))
    return pl.pallas_call(
        functools.partial(norm_back_kernel, len(parts)),
        grid=(rows // min(TILE, rows),),
        in_specs=[tile, tile, whole((1, d))] + [tile] * len(parts),
        out_specs=[tile, acc, acc],
        out_shape=[struct((rows, d), F32), struct((8, d), F32), struct((8, d), F32)],
        compiler_params=params(),
        cost_estimate=cost(20 * rows * d, 12 * rows * d),
        name="norm_back",
    )(x, dy, scale, *parts)


def layout(lengths, group_rows):
    seg_ends = jnp.cumsum(lengths)
    positions = jnp.arange(group_rows, dtype=jnp.int32)
    closed = seg_ends[None, :] <= positions[:, None]
    segment = jnp.sum(closed.astype(jnp.int32), axis=1)
    seg_start = jnp.sum(jnp.where(closed, lengths[None, :], 0), axis=1)
    return segment, positions - seg_start


def table_kernel(ends_ref, lens_ref, freq, cos, fwd, back, hot, neg):
    rows = cos.shape[0]
    lane = lane_ids(rows)
    where = lax.broadcasted_iota(jnp.int32, (rows, LANES), 0) + pl.program_id(0) * rows
    segment = jnp.zeros((rows, LANES), jnp.int32)
    start = jnp.zeros((rows, LANES), jnp.int32)
    for j in range(ends_ref.shape[0]):
        closed = where >= ends_ref[j]
        segment = segment + closed.astype(jnp.int32)
        start = start + jnp.where(closed, lens_ref[j], 0)
    angle = (where - start).astype(F32) * freq[...]
    dim = lax.rem(lane, HEAD)
    sin = jnp.sin(angle)
    cos[...] = jnp.where(dim < ROT, jnp.cos(angle), 1.0)
    fwd[...] = jnp.where(dim < ROT // 2, -sin, 0.0)
    back[...] = jnp.where((dim >= ROT // 2) & (dim < ROT), sin, 0.0)
    same = lane - HEAD == segment
    hot[...] = jnp.where(same, 1.0, 0.0).astype(BF)
    neg[...] = jnp.where(same | (lane < HEAD) | (lane >= HEAD + ends_ref.shape[0]), 0.0, excluded).astype(BF)


def tables(lengths, group_rows):
    half = ROT // 2
    freq = jnp.power(rope_base, -2.0 * jnp.arange(half, dtype=F32) / ROT)
    freq = jnp.pad(jnp.tile(freq, 2), (0, HEAD - ROT))
    freq = jnp.tile(freq, LANES // HEAD)[None, :]
    block = pl.BlockSpec((TILE, LANES), lambda i, *_: (i, 0))
    return pl.pallas_call(
        table_kernel,
        grid_spec=pltpu.PrefetchScalarGridSpec(
            num_scalar_prefetch=2,
            grid=(group_rows // TILE,),
            in_specs=[whole((1, LANES))],
            out_specs=[block] * 5,
        ),
        out_shape=[struct((group_rows, LANES), F32)] * 3 + [struct((group_rows, LANES), BF)] * 2,
        compiler_params=params(),
        name="tables",
    )(jnp.cumsum(lengths).astype(jnp.int32), lengths, freq)


def on_device(hidden_in, seq_lengths, ln_scale, ln_bias, wqkv, wout, win, wdown, out_grad):
    rows, d = hidden_in.shape
    n = lax.axis_size("mp")
    me = lax.axis_index("mp")
    total = rows * n
    heads = wout.shape[0] // HEAD
    f = win.shape[1]
    after = lambda x, *deps: lax.optimization_barrier((x, *deps))[0]

    normed = norm(hidden_in, ln_scale[None, :], ln_bias[None, :])
    pieces = 2 if rows >= 2 * CHUNK else 1
    high = rows // pieces
    ring = lambda s: [((i + s) % n, i) for i in range(n)]
    slot = [((me + s) % n).astype(jnp.int32)[None] for s in range(n)]
    x_all, dy_all, place = [normed], [out_grad], [slot[0]]
    gate = None
    for s in range(1, n):
        for p in range(pieces):
            mine = [v[p * high : (p + 1) * high] for v in (normed, out_grad)]
            if gate is not None:
                mine = list(lax.optimization_barrier((*mine, *gate))[:2])
            gate = [lax.ppermute(v, "mp", ring(s)) for v in mine]
            x_all.append(gate[0])
            dy_all.append(gate[1])
            place.append(slot[s] * pieces + p)
    index = jnp.concatenate(place)
    table = None

    do, up, back, gdown, gin, sq = feed(slot[0], 0, 1, total, heads, [], normed, out_grad, win, wdown, wout)
    ups, backs, sqs = [up], [back], [sq]
    qkv = []
    order = gdown
    for k in range(1, len(x_all)):
        s, p = 1 + (k - 1) // pieces, (k - 1) % pieces
        last = k == len(x_all) - 1
        if last:
            table = tables(after(seq_lengths[0], order), total)
            for t in range(k):
                qkv = project(place[t], total, heads, qkv, after(x_all[t], order), wqkv, *table)
        prior = [gdown, gin, after(do, *qkv[:1])] + ([ups[s], backs[s]] if p else [])
        do, up, back, gdown, gin, sq = feed(
            place[k], p, pieces, total, heads, prior, x_all[k], dy_all[k], win, wdown, wout
        )
        order = gdown
        ups[s:] = [up]
        backs[s:] = [back]
        sqs.append(sq)
        if last:
            qkv = project(place[k], total, heads, qkv, after(x_all[k], order), wqkv, *table)
    context, wide, keep, ctx_sq, *done = attend(*qkv, [gdown, gin], 4)
    joined = [join(slot[s], False, context, wout, ups[s]) for s in range(1, n)]
    sent = [lax.ppermute(v, "mp", ring(n - s)) for s, v in enumerate(joined, 1)]
    gqkv, gdown, gin = attend_back(*qkv, after(do, *joined), wide, keep, *table[:3], done, [gdown, gin], 3)
    returned = [lax.ppermute(join(slot[s], True, gqkv, wqkv, backs[s]), "mp", ring(n - s)) for s in range(1, n)]
    gqw, gow = weight_grads(index, x_all, gqkv, dy_all, context)
    own, result, res_sq, gqw, gow = tail(
        [gqw, gow], gqkv, context, wqkv, wout, backs[0], ups[0], hidden_in, sent, 1
    )
    grad_hidden, gain, bias = norm_back(hidden_in, out_grad, ln_scale[None, :], [own] + returned)

    stats = jnp.stack([jnp.sum(res_sq), jnp.sum(ctx_sq), sum(jnp.sum(s) for s in sqs)])
    packed = jnp.concatenate([jnp.sum(gain, axis=0), jnp.sum(bias, axis=0), jnp.pad(stats, (0, 8 * LANES - 3))])
    sums = small_sum(packed.reshape(-1, LANES), 2).reshape(-1)
    devices = lax.axis_size("dp") * n
    counts = jnp.array([rows * d * devices, rows * d * devices, rows * f * n * devices], F32)
    return (
        result,
        grad_hidden,
        sums[:d],
        sums[d : 2 * d],
        gqw.astype(F32),
        gow.T.astype(F32),
        gin.astype(F32),
        gdown.astype(F32),
        jnp.sqrt(sums[2 * d : 2 * d + 3] / counts),
    )


def solution(mesh):
    tok = P(("dp", "mp"), None)
    cols, rows = P(None, "mp"), P("mp", None)
    return jax.shard_map(
        on_device,
        mesh=mesh,
        in_specs=(tok, P("dp", None), P(), P(), cols, rows, cols, rows, tok),
        out_specs=(tok, tok, P(), P(), cols, rows, cols, rows, P()),
        check_vma=False,
    )
```

time: 494 us -> 439 us (0.89)
  Pallas kernels: 422 us -> 379 us
  between operations: 15.7 us -> 2.77 us
  local copies, waits for them, and re-layouts: 3.56 us -> 12 us
  waiting for transfers between devices: 7.24 us -> 0.02 us
    pallas_call x16 -> x12, Pallas kernels: 370 us -> 344 us  [the longest x3 92.9 us: feed(): pl.pallas_call(functools.partial(feed_kernel, len(prior)), grid_spec=pltp...]
    pallas_call x1, Pallas kernels: 32.3 us -> 15.2 us  [small_sum(): pl.pallas_call(functools.partial(small_kernel, n_dp, n_mp), out_shape=str...]
    psum x2 -> x0, waiting for transfers between devices: 7.19 us -> none  [the longest x1 7.19 us: on_device(): gin, gow = lax.psum((after(gin, gdown), after(gow, gdown)), 'dp')]
  transfers between devices with their start and end apart: 6 -> 6, of which waited for: 1 -> 0; matrix products, arithmetic and copies ran while one was open for 5% -> 5% of each run, Pallas kernels for 86% -> 60%
where the time goes in v3:
time: 439 us; the launch traced here: 431 us
  Pallas kernels  379 us (86%)
  other arithmetic  29.4 us (7%)
  local copies, waits for them, and re-layouts  12 us (3%)
  starting transfers between devices  7.16 us (2%)
    pallas_call x3, Pallas kernels, feed(): pl.pallas_call(functools.partial(feed_kernel, len(prior)), grid_spec=pltp...  92.9 us
    pallas_call x1, Pallas kernels, attend_back(): pl.pallas_call(functools.partial(attend_back_kernel, heads // 2, shapes),...  78.2 us
    pallas_call x1, Pallas kernels, tail(): pl.pallas_call(functools.partial(tail_kernel, steps, len(sent), shapes),...  63.3 us
    pallas_call x1, Pallas kernels, attend(): pl.pallas_call(functools.partial(attend_kernel, heads // 2, shapes), grid...  59.5 us
    pallas_call x3, Pallas kernels, project(): pl.pallas_call(project_kernel, grid_spec=pltpu.PrefetchScalarGridSpec(num...  22.8 us
    pallas_call x1, Pallas kernels, weight_grads(): pl.pallas_call(functools.partial(weight_kernel, n), grid_spec=pltpu.Prefe...  15.3 us
    pallas_call x1, Pallas kernels, small_sum(): pl.pallas_call(functools.partial(small_kernel, n_dp, n_mp), out_shape=str...  15.2 us
    pallas_call x2, Pallas kernels, join(): pl.pallas_call(functools.partial(join_kernel, transposed), grid_spec=pltp...  12.2 us
  transfers between devices with their start and end apart: 6, of which 0 were waited for; matrix products, arithmetic and copies ran while one was open for 5% of the time, Pallas kernels for 60%

profile of v3, /device:TPU:0, one launch (start us, length us, event | category | flops | bytes accessed | tf_op | source)
XLA Modules:
  0.0 430.6 jit_solution(9212987036274676384)
XLA Ops:
  0.6 0.0 copy-start
  0.7 4.6 %norm.1.nrm.refs_0_ = bf16[1024,1024]{1,0:T(8,128)(2,1)} custom-call(bf16[1024,1024]{1,0:T(8,128)(2,1)} %x_ref.3, f32[1,1024]{1,0:T(1,128)} %bitcast.42, f32[1,1024]{1,0:T(1,128)} %bitcast.44), custom_call_target="tpu_custom_call" | custom-call | flops 10485760 | bytes 4194304 | tf_op jit(solution)/shard_map/norm/pallas_call | solution.py:816
  5.3 3.1 fusion.3
  8.4 2.9 collective-permute-start
  11.3 1.5 fusion.2
  12.8 42.8 %feed.3 = (bf16[8,2048,128]{2,1,0:T(8,128)(2,1)}, f32[1024,1024]{1,0:T(8,128)}, f32[1024,1024]{1,0:T(8,128)}, bf16[2048,1024]{1,0:T(8,128)(2,1)}, bf16[1024,2048]{1,0:T(8,128)(2,1)}, /*index=5*/f32[8,512]{1,0:T(8,128)}) custom-call(s32[1]{0:T(128)} %bitcast.3.slot, bf16[1024,1024]{1,0:T(8,128)(2,1)} %norm.1.nrm.refs_0_, bf16[1024,1024]{1,0:T(8,128)(2,1)} %dy.3, ...), custom_call_target="tpu_custom_call" | custom-call | flops 25769803776 | bytes 46137344 | tf_op jit(solution)/shard_map/feed/pallas_call | solution.py:187
  55.6 0.1 tile.7
  55.7 0.6 broadcast_in_dim_tile.3.freq
  56.3 1.3 reduce_sum.67
  57.6 0.7 pad_add_fusion.index
  58.3 2.1 collective-permute-start.2
  60.4 0.1 collective-permute-start.3
  60.5 25.1 %feed.4 = (bf16[8,2048,128]{2,1,0:T(8,128)(2,1)}, f32[1024,1024]{1,0:T(8,128)}, f32[1024,1024]{1,0:T(8,128)}, bf16[2048,1024]{1,0:T(8,128)(2,1)}, bf16[1024,2048]{1,0:T(8,128)(2,1)}, /*index=5*/f32[8,512]{1,0:T(8,128)}) custom-call(s32[1]{0:T(128)S(6)} %mul.6.slot, bf16[512,1024]{1,0:T(8,128)(2,1)} %copy-done.2, ...), custom_call_target="tpu_custom_call", output_to_operand_aliasing={{0}: (8, {})} | custom-call | flops 12884901888 | bytes 35651584 | tf_op jit(solution)/shard_map/feed/pallas_call | solution.py:187
  85.6 1.3 reduce_sum.68
  86.9 0.7 reduce-window.9
  87.5 7.5 %tables.1 = (f32[2048,128]{1,0:T(8,128)}, f32[2048,128]{1,0:T(8,128)}, f32[2048,128]{1,0:T(8,128)}, bf16[2048,128]{1,0:T(8,128)(2,1)}, bf16[2048,128]{1,0:T(8,128)(2,1)}) custom-call(s32[4]{0:T(128)} %bitcast.49, s32[4]{0:T(128)} %bitcast.45, f32[1,128]{1,0:T(1,128)} %broadcast_in_dim_tile.3.freq), custom_call_target="tpu_custom_call" | custom-call | tf_op jit(solution)/shard_map/tables/pallas_call | solution.py:904
  95.0 9.7 %project.3 = (bf16[8,2048,128]{2,1,0:T(8,128)(2,1)}, bf16[8,2048,128]{2,1,0:T(8,128)(2,1)}, bf16[8,2048,128]{2,1,0:T(8,128)(2,1)}) custom-call(s32[1]{0:T(128)} %bitcast.3.slot, bf16[1024,1024]{1,0:T(8,128)(2,1)} %norm.1.nrm.refs_0_, bf16[1024,1536]{1,0:T(8,128)(2,1)} %b.3, f32[2048,128]{1,0:T(8,128)} %get-tuple-element.78.cos, ...), custom_call_target="tpu_custom_call" | custom-call | flops 3221225472 | bytes 15728640 | tf_op jit(solution)/shard_map/project/pallas_call | solution.py:116
  104.7 6.5 %project.4 = (bf16[8,2048,128]{2,1,0:T(8,128)(2,1)}, bf16[8,2048,128]{2,1,0:T(8,128)(2,1)}, bf16[8,2048,128]{2,1,0:T(8,128)(2,1)}) custom-call(s32[1]{0:T(128)S(6)} %mul.6.slot, bf16[512,1024]{1,0:T(8,128)(2,1)} %copy-done.2, bf16[1024,1536]{1,0:T(8,128)(2,1)} %b.3, ...), custom_call_target="tpu_custom_call", output_to_operand_aliasing={{0}: (8, {}), {1}: (9, {}), {2}: (10, {})} | custom-call | flops 1610612736 | bytes 9437184 | tf_op jit(solution)/shard_map/project/pallas_call | solution.py:116
  112.4 1.0 copy-done.3
  113.4 25.0 %feed.5 = (bf16[8,2048,128]{2,1,0:T(8,128)(2,1)}, f32[1024,1024]{1,0:T(8,128)}, f32[1024,1024]{1,0:T(8,128)}, bf16[2048,1024]{1,0:T(8,128)(2,1)}, bf16[1024,2048]{1,0:T(8,128)(2,1)}, /*index=5*/f32[8,512]{1,0:T(8,128)}) custom-call(s32[1]{0:T(128)S(6)} %add.25.slot, ...), custom_call_target="tpu_custom_call", output_to_operand_aliasing={{0}: (8, {}), {1}: (9, {}), {2}: (10, {})} | custom-call | flops 12884901888 | bytes 35651584 | tf_op jit(solution)/shard_map/feed/pallas_call | solution.py:187
  138.4 1.3 reduce_sum.69
  139.8 6.5 %project.5 = (bf16[8,2048,128]{2,1,0:T(8,128)(2,1)}, bf16[8,2048,128]{2,1,0:T(8,128)(2,1)}, bf16[8,2048,128]{2,1,0:T(8,128)(2,1)}) custom-call(s32[1]{0:T(128)S(6)} %add.25.slot, bf16[512,1024]{1,0:T(8,128)(2,1)} %copy-done.3, bf16[1024,1536]{1,0:T(8,128)(2,1)} %b.3, ...), custom_call_target="tpu_custom_call", output_to_operand_aliasing={{0}: (8, {}), {1}: (9, {}), {2}: (10, {})} | custom-call | flops 1610612736 | bytes 9437184 | tf_op jit(solution)/shard_map/project/pallas_call | solution.py:116
  146.3 59.5 %attend.1 = (bf16[2048,512]{1,0:T(8,128)(2,1)}, f32[8,2048,128]{2,1,0:T(8,128)}, bf16[8,36,256,256]{3,2,1,0:T(8,128)(2,1)}, f32[8,128]{1,0:T(8,128)}, bf16[8,16,...) custom-call(bf16[8,2048,128]{2,1,0:T(8,128)(2,1)} %get-tuple-element.95.q_ref, ...), custom_call_target="tpu_custom_call" | custom-call | flops 19327352832 | bytes 41943040 | tf_op jit(solution)/shard_map/attend/pallas_call | solution.py:307
  205.8 1.3 reduce_sum.66
  207.1 4.6 %join.2 = bf16[1024,1024]{1,0:T(8,128)(2,1)} custom-call(s32[1]{0:T(128)} %bitcast.slot, bf16[2048,512]{1,0:T(8,128)(2,1)} %get-tuple-element.100.a.refs_9_.refs_10_.refs_11_.context, bf16[512,1024]{1,0:T(8,128)(2,1)} %wout.7, f32[1024,1024]{1,0:T(8,128)} %get-tuple-element.101.c), custom_call_target="tpu_custom_call" | custom-call | flops 1073741824 | bytes 8388608 | tf_op jit(solution)/shard_map/join/pallas_call | solution.py:459
  211.6 1.5 collective-permute-start.4
  213.1 78.2 %attend_back.1 = (bf16[2048,1536]{1,0:T(8,128)(2,1)}, bf16[2,8,8,16,1024]{4,3,2,1,0:T(8,128)(2,1)}, bf16[2,8,4,16,2048]{4,3,2,1,0:T(8,128)(2,1)}) custom-call(bf16[8,2048,128]{2,1,0:T(8,128)(2,1)} %get-tuple-element.95.q_ref, bf16[8,2048,128]{2,1,0:T(8,128)(2,1)} %get-tuple-element.96.k_ref, bf16[8,2048,128]{2,1,0:T(8,128)(2,1)} %get-tuple-element.97.v_ref, ...), custom_call_target="tpu_custom_call" | custom-call | flops 38654705664 | bytes 83886080 | tf_op jit(solution)/shard_map/attend_back/pallas_call | solution.py:432
  291.3 7.7 %join.3 = bf16[1024,1024]{1,0:T(8,128)(2,1)} custom-call(s32[1]{0:T(128)} %bitcast.slot, bf16[2048,1536]{1,0:T(8,128)(2,1)} %get-tuple-element.107.refs_3_.refs_4_.refs_5_.gqkv.a, bf16[1024,1536]{1,0:T(8,128)(2,1)} %b.3, f32[1024,1024]{1,0:T(8,128)} %get-tuple-element.114.c), custom_call_target="tpu_custom_call" | custom-call | flops 3221225472 | bytes 12582912 | tf_op jit(solution)/shard_map/join/pallas_call | solution.py:459
  299.0 0.6 collective-permute-start.5
  300.3 6.8 %bitcast_convert_fusion.1 = f32[1024,2048]{1,0:T(8,128)} fusion(bf16[2,8,4,16,2048]{4,3,2,1,0:T(8,128)(2,1)} %get-tuple-element.125), kind=kLoop, calls=%fused_computation.1 | loop fusion | flops 2097152 | bytes 12582912 | tf_op jit(solution)/shard_map/convert_element_type | solution.py:990
  307.1 4.7 %bitcast_convert_fusion = f32[2048,1024]{1,0:T(8,128)} fusion(bf16[2,8,8,16,1024]{4,3,2,1,0:T(8,128)(2,1)S(1)} %copy-done.1), kind=kLoop, calls=%fused_computation | loop fusion | flops 2097152 | bytes 12582912 | tf_op jit(solution)/shard_map/convert_element_type | solution.py:991
  311.8 15.3 %weight_grads.1 = (bf16[1024,1536]{1,0:T(8,128)(2,1)}, bf16[1024,512]{1,0:T(8,128)(2,1)}) custom-call(s32[3]{0:T(128)} %pad_add_fusion.index, bf16[1024,1024]{1,0:T(8,128)(2,1)} %norm.1.nrm.refs_0_, bf16[512,1024]{1,0:T(8,128)(2,1)} %copy-done.2, bf16[512,1024]{1,0:T(8,128)(2,1)} %copy-done.3, ...), custom_call_target="tpu_custom_call" | custom-call | flops 8589934592 | bytes 20971520 | tf_op jit(solution)/shard_map/weight_grads/pallas_call | solution.py:499
  327.2 0.0 copy-start.5
  327.2 1.3 copy-done.5
  328.5 63.3 %tail.1 = (bf16[1024,1024]{1,0:T(8,128)(2,1)}, bf16[1024,1024]{1,0:T(8,128)(2,1)}, f32[8,1024]{1,0:T(8,128)}, bf16[2,8,4,16,1536]{4,3,2,1,0:T(8,128)(2,1)}, bf16[2,8,4,16,512]{4,3,2,1,0:T(8,128)(2,1)}) custom-call(bf16[2048,1536]{1,0:T(8,128)(2,1)} %get-tuple-element.107.refs_3_.refs_4_.refs_5_.gqkv.a, ...), custom_call_target="tpu_custom_call" | custom-call | flops 4294967296 | bytes 29360128 | tf_op jit(solution)/shard_map/tail/pallas_call | solution.py:747
  391.8 1.4 reduce_sum.65
  393.2 1.5 bitcast_convert_fusion.3
  394.7 1.8 copy.29
  396.5 7.5 %norm_back.1 = (f32[1024,1024]{1,0:T(8,128)}, f32[8,1024]{1,0:T(8,128)}, f32[8,1024]{1,0:T(8,128)}) custom-call(bf16[1024,1024]{1,0:T(8,128)(2,1)} %x_ref.3, bf16[1024,1024]{1,0:T(8,128)(2,1)} %dy.3, f32[1,1024]{1,0:T(1,128)} %bitcast.43, bf16[1024,1024]{1,0:T(8,128)(2,1)} %get-tuple-element.113.refs_0_, bf16[1024,1024]{1,0:T(8,128)(2,1)} %collective-permute-done.5.refs_1_), custom_call_target="tpu_custom_call" | custom-call | flops 20971520 | bytes 12582912 | tf_op jit(solution)/shard_map/norm_back/pallas_call | solution.py:856
  404.0 0.8 reduce_sum.63
  404.8 0.8 reduce_sum.64
  405.5 1.4 fusion
  406.9 0.6 pad_maximum_fusion.x
  407.5 15.2 %small_sum.1 = f32[24,128]{1,0:T(8,128)} custom-call(f32[24,128]{1,0:T(8,128)} %pad_maximum_fusion.x), custom_call_target="tpu_custom_call" | custom-call | tf_op jit(solution)/shard_map/small_sum/pallas_call | solution.py:792
  422.8 1.3 slice_bitcast_fusion
  424.0 3.8 bitcast_convert_fusion.2
  427.8 1.2 fusion.1
  429.0 1.3 copy.41
  (27 shorter events, 0.1 us)
Async XLA Ops:
  0.6 10.7 %copy-start = (bf16[1024,1024]{1,0:T(8,128)(2,1)S(1)}, bf16[1024,1024]{1,0:T(8,128)(2,1)}, u32[]{:S(2)}) copy-start(bf16[1024,1024]{1,0:T(8,128)(2,1)} %dy.3) | copy-start | bytes 6291460
  8.4 49.9 %collective-permute-start = (bf16[512,1024]{1,0:T(8,128)(2,1)}, bf16[512,1024]{1,0:T(8,128)(2,1)S(1)}, u32[]{:S(2)}, u32[]{:S(2)}) collective-permute-start(bf16[512,1024]{1,0:T(8,128)(2,1)} %get-tuple-element.129), channel_id=1, source_target_pairs={{1,0},{0,1},{3,2},{2,3},{5,4},{4,5},{7,6},{6,7},{9,8},{8,9},{11,10... | collective-permute-start | bytes 3145736 | tf_op jit(solution)/shard_map/ppermute | solution.py:939
  12.8 45.5 %collective-permute-start.1 = (bf16[512,1024]{1,0:T(8,128)(2,1)}, bf16[512,1024]{1,0:T(8,128)(2,1)S(1)}, u32[]{:S(2)}, u32[]{:S(2)}) collective-permute-start(bf16[512,1024]{1,0:T(8,128)(2,1)} %get-tuple-element.127), channel_id=1, source_target_pairs={{1,0},{0,1},{3,2},{2,3},{5,4},{4,5},{7,6},{6,7},{9,8},{8,9},{11,10... | collective-permute-start | bytes 3145736 | tf_op jit(solution)/shard_map/ppermute | solution.py:939
  58.3 2.2 copy-start.2
  58.3 2.2 copy-start.7
  58.3 54.1 %collective-permute-start.2 = (bf16[512,1024]{1,0:T(8,128)(2,1)}, bf16[512,1024]{1,0:T(8,128)(2,1)S(1)}, u32[]{:S(2)}, u32[]{:S(2)}) collective-permute-start(bf16[512,1024]{1,0:T(8,128)(2,1)} %get-tuple-element.68), channel_id=1, source_target_pairs={{1,0},{0,1},{3,2},{2,3},{5,4},{4,5},{7,6},{6,7},{9,8},{8,9},{11,10... | collective-permute-start | bytes 3145736 | tf_op jit(solution)/shard_map/ppermute | solution.py:939
  60.4 52.0 %collective-permute-start.3 = (bf16[512,1024]{1,0:T(8,128)(2,1)}, bf16[512,1024]{1,0:T(8,128)(2,1)}, u32[]{:S(2)}, u32[]{:S(2)}) collective-permute-start(bf16[512,1024]{1,0:T(8,128)(2,1)} %get-tuple-element.69), channel_id=1, source_target_pairs={{1,0},{0,1},{3,2},{2,3},{5,4},{4,5},{7,6},{6,7},{9,8},{8,9},{11,10... | collective-permute-start | bytes 3145736 | tf_op jit(solution)/shard_map/ppermute | solution.py:939
  60.5 26.4 %copy-start.8 = (s32[1,4]{1,0:T(1,128)S(1)}, s32[1,4]{1,0:T(1,128)}, u32[]{:S(2)}) copy-start(s32[1,4]{1,0:T(1,128)} %param.11) | copy-start | bytes 52
  112.4 1.0 copy-start.3
  211.6 115.5 %collective-permute-start.4 = (bf16[1024,1024]{1,0:T(8,128)(2,1)}, bf16[1024,1024]{1,0:T(8,128)(2,1)S(1)}, u32[]{:S(2)}, u32[]{:S(2)}) collective-permute-start(bf16[1024,1024]{1,0:T(8,128)(2,1)} %join.2), channel_id=1, source_target_pairs={{1,0},{0,1},{3,2},{2,3},{5,4},{4,5},{7,6},{6,7},{9,8},{8,9},{11,10... | collective-permute-start | bytes 6291464 | tf_op jit(solution)/shard_map/ppermute | solution.py:969
  299.0 97.5 %collective-permute-start.5 = (bf16[1024,1024]{1,0:T(8,128)(2,1)}, bf16[1024,1024]{1,0:T(8,128)(2,1)}, u32[]{:S(2)}, u32[]{:S(2)}) collective-permute-start(bf16[1024,1024]{1,0:T(8,128)(2,1)} %join.3), channel_id=1, source_target_pairs={{1,0},{0,1},{3,2},{2,3},{5,4},{4,5},{7,6},{6,7},{9,8},{8,9},{11,10... | collective-permute-start | bytes 6291464 | tf_op jit(solution)/shard_map/ppermute | solution.py:971
  300.3 6.8 %copy-start.1 = (bf16[2,8,8,16,1024]{4,3,2,1,0:T(8,128)(2,1)S(1)}, bf16[2,8,8,16,1024]{4,3,2,1,0:T(8,128)(2,1)}, u32[]{:S(2)}) copy-start(bf16[2,8,8,16,1024]{4,3,2,1,0:T(8,128)(2,1)} %get-tuple-element.126) | copy-start | bytes 12582916
  327.2 1.3 copy-start.5
  396.5 27.5 %copy-start.4 = (bf16[2,8,4,16,1536]{4,3,2,1,0:T(8,128)(2,1)S(1)}, bf16[2,8,4,16,1536]{4,3,2,1,0:T(8,128)(2,1)}, u32[]{:S(2)}) copy-start(bf16[2,8,4,16,1536]{4,3,2,1,0:T(8,128)(2,1)} %get-tuple-element.123) | copy-start | bytes 9437188
  424.0 3.8 copy-start.9
  424.0 5.0 %copy-start.6 = (bf16[1024,1024]{1,0:T(8,128)(2,1)S(1)}, bf16[1024,1024]{1,0:T(8,128)(2,1)}, u32[]{:S(2)}) copy-start(bf16[1024,1024]{1,0:T(8,128)(2,1)} %get-tuple-element.142) | copy-start | bytes 6291460

commit v4 on v3

--- a/solution.py
+++ b/solution.py
@@ -13,6 +13,7 @@
 TILE = 256
 CHUNK = 512
 POINTS = 2
+BACK_POINTS = 2
 F32 = jnp.float32
 BF = jnp.bfloat16
 
@@ -59,17 +60,8 @@
 
 
 def gelu_parts(v):
-    x = jnp.abs(v)
-    bell = jnp.exp(v * v * (-0.5))
-    base = 1.0 + x * (0.3275911 * 0.7071067811865476)
-    t = pl.reciprocal(base, approx=True)
-    poly = t * (
-        0.254829592
-        + t * (-0.284496736 + t * (1.421413741 + t * (-1.453152027 + t * 1.061405429)))
-    )
-    tail = 0.5 * poly * bell
-    cdf = jnp.where(v >= 0, 1.0 - tail, tail)
-    return v * cdf, cdf + v * bell * 0.3989422804014327
+    cdf = 0.5 + 0.5 * lax.erf(v * 0.7071067811865476)
+    return v * cdf, cdf + v * jnp.exp(v * v * (-0.5)) * 0.3989422804014327
 
 
 def ahead(count, product, use):
@@ -269,7 +261,7 @@
         return acc
 
     items = [(h, i) for i in range(total // b) for h in range(2)]
-    places = Places(sum(i + 1 for _, i in items), pairs, chips, advance)
+    places = Places(POINTS, sum(i + 1 for _, i in items), pairs, chips, advance)
     s = scores(*items[0])
     left = None
     for t, (h, i) in enumerate(items):
@@ -395,7 +387,7 @@
         dv_acc[h, rows, :] = dv[i * b :]
 
     items = [(h, i) for i in range(total // b) for h in range(2)]
-    places = Places(sum(i + 1 for _, i in items), pairs, chips - 1, advance)
+    places = Places(BACK_POINTS, sum(i + 1 for _, i in items), pairs, chips - 1, advance)
     state = begin(*items[0])
     for t, item in enumerate(items):
         later = begin(*items[t + 1]) if t + 1 < len(items) else None
@@ -476,7 +468,9 @@
 
 
 def weight_kernel(n, index, *refs):
-    groups, outs = [refs[i * n : (i + 1) * n] for i in range(4)], refs[4 * n :]
+    groups, (widen, outs) = [refs[i * n : (i + 1) * n] for i in range(4)], (refs[4 * n : 4 * n + 2], refs[4 * n + 2 :])
+    for x, out in zip(widen, outs[2:]):
+        out[...] = x[...].astype(F32)
     for xs, ys, out in ((groups[0], groups[1], outs[0]), (groups[2], groups[3], outs[1])):
         width = out.shape[1]
         step = 512 if width % 512 == 0 else 128
@@ -485,7 +479,7 @@
             out[:, cols] = sum(tn(x[...], y[:, cols]) for x, y in zip(xs, ys)).astype(BF)
 
 
-def weight_grads(index, x1, y1, x2, y2):
+def weight_grads(index, x1, y1, x2, y2, widen):
     n, d = len(x1), x1[0].shape[1]
     tile = 256
     left = [pl.BlockSpec((x.shape[0], tile), lambda j, index: (0, j)) for x in x1]
@@ -496,19 +490,20 @@
         for s, x in enumerate(x1)
     ]
     widths = (y1.shape[1], y2.shape[1])
+    wide = [pl.BlockSpec((x.shape[0] * tile // d, x.shape[1]), lambda j, index: (j, 0)) for x in widen]
     return pl.pallas_call(
         functools.partial(weight_kernel, n),
         grid_spec=pltpu.PrefetchScalarGridSpec(
             num_scalar_prefetch=1,
             grid=(d // tile,),
-            in_specs=left + right(y1) + left + right(y2),
-            out_specs=[pl.BlockSpec((tile, w), lambda j, index: (j, 0)) for w in widths],
+            in_specs=left + right(y1) + left + right(y2) + wide,
+            out_specs=[pl.BlockSpec((tile, w), lambda j, index: (j, 0)) for w in widths] + wide,
         ),
-        out_shape=[struct((d, w), BF) for w in widths],
+        out_shape=[struct((d, w), BF) for w in widths] + [struct(x.shape, F32) for x in widen],
         compiler_params=params(),
         cost_estimate=cost(2 * y1.shape[0] * d * sum(widths), 2 * y1.shape[0] * (2 * d + sum(widths)) + 2 * d * sum(widths)),
         name="weight_grads",
-    )(index, *x1, *[y1] * n, *x2, *[y2] * n)
+    )(index, *x1, *[y1] * n, *x2, *[y2] * n, *widen)
 
 
 class Ring:
@@ -542,7 +537,7 @@
     def cut(x):
         chips = lax.axis_size("dp") // 2
         rows, d = x.shape
-        parts = min(8, rows // (32 * chips))
+        parts = min(4, rows // (32 * chips))
         return x.reshape(2, chips, parts, rows // (2 * chips * parts), d)
 
     def device(self, pos):
@@ -666,49 +661,76 @@
 
 
 def paced(place, places, limit, step):
-    lax.fori_loop((place * limit) // places, ((place + 1) * limit) // places, lambda s, carry: (step(s), carry)[1], 0)
+    upto = lambda k: (k * limit + places - 1) // places
+    lax.fori_loop(upto(place), upto(place + 1), lambda s, carry: (step(s), carry)[1], 0)
 
 
 class Places:
-    def __init__(self, work, per_grid, limit, step):
-        self.work, self.total, self.limit, self.step, self.done, self.point = work, POINTS * per_grid, limit, step, 0, 0
+    def __init__(self, points, work, per_grid, limit, step):
+        self.points, self.total, self.work, self.limit, self.step = points, points * per_grid, work, limit, step
+        self.done = self.point = 0
 
     def add(self, work):
         self.done += work
-        if self.done * POINTS >= (self.point + 1) * self.work:
-            paced(pl.program_id(0) * POINTS + self.point, self.total, self.limit, self.step)
+        if self.done * self.points >= (self.point + 1) * self.work:
+            paced(pl.program_id(0) * self.points + self.point, self.total, self.limit, self.step)
             self.point += 1
 
 
-def tail_kernel(steps, others, shapes, gqkv, context, wqkv, wout, back, update, hidden, *refs):
-    count = len(shapes)
-    sent, refs = refs[:others], refs[others:]
-    xs, (share, result, sq), refs = refs[:count], refs[count : count + 3], refs[count + 3 :]
-    outs, refs = refs[:count], refs[count:]
-    (own_grad, own_context, sems), refs = refs[:3], refs[3:]
-    rings = []
-    for k, shape in enumerate(shapes):
-        names = Ring.SUM + Ring.SPREAD
-        rings.append(Ring(shape, x=xs[k], out=outs[k], **dict(zip(names, refs[k * len(names) : (k + 1) * len(names)]))))
+def tail_kernel(steps, n_dp, n_mp, counts, shapes, gqkv, context, wqkv, wout, scale, back, update, hidden, again, dy, *refs):
+    refs = list(refs)
+    take = lambda k: [refs.pop(0) for _ in range(k)]
+    others, squares = n_mp - 1, counts
+    sent, shares, acts, (ctx_sq,), xs = take(others), take(others), take(squares), take(1), take(len(shapes))
+    result, grad, sums = take(3)
+    outs = take(len(shapes))
+    own_grad, own_context, sems, share, got, ex_send, ex_recv, sq, gain, bias, held, kept, send, recv = take(14)
+    names = Ring.SUM + Ring.SPREAD
+    rings = [Ring(shape, x=x, out=out, **dict(zip(names, take(len(names))))) for shape, x, out in zip(shapes, xs, outs)]
     chips = rings[0].chips
     i = pl.program_id(0)
-    rows = own_grad.shape[0]
-    height = back.shape[0]
-    limit = 2 * chips - 1
-    base = pl.ds(lax.axis_index("mp") * rows, rows)
+    rows, d = share.shape
+    height, tall = back.shape[0], again.shape[0]
+    first, late = rows // height, steps - rows // tall
+    mp = lax.axis_index("mp")
+    me = lax.axis_index("dp") * n_mp + mp
+    rounds = held.shape[0]
+    base = pl.ds(mp * rows, rows)
     fetch = [
         pltpu.make_async_copy(gqkv.at[base], own_grad, sems.at[0]),
         pltpu.make_async_copy(context.at[base], own_context, sems.at[1]),
     ]
 
+    def owner(s):
+        return dict(device_id={"mp": lax.rem(mp + s, n_mp)}, device_id_type=pl.DeviceIdType.MESH)
+
+    def partner(k):
+        t = me + 2**k * (1 - 2 * lax.rem(me // 2**k, 2))
+        return dict(device_id={"dp": t // n_mp, "mp": lax.rem(t, n_mp)}, device_id_type=pl.DeviceIdType.MESH)
+
+    exchange = [
+        pltpu.make_async_remote_copy(
+            src_ref=shares[s - 1], dst_ref=got.at[s - 1], send_sem=ex_send.at[s - 1], recv_sem=ex_recv.at[s - 1], **owner(s)
+        )
+        for s in range(1, n_mp)
+    ]
+
     @pl.when(i == 0)
     def _():
         for c in fetch:
             c.start()
-        rings[0].meet()
+        barrier = pltpu.get_barrier_semaphore()
+        for t in (*rings[0].ends, rings[0].peer):
+            pl.semaphore_signal(barrier, inc=1, device_id={"dp": t}, device_id_type=pl.DeviceIdType.MESH)
+        for t in [owner(s) for s in range(1, n_mp)] + [partner(k) for k in range(rounds)]:
+            pl.semaphore_signal(barrier, inc=1, **t)
+        pl.semaphore_wait(barrier, 3 + others + rounds)
         for ring in rings:
             ring.sum_begin()
-        sq[...] = jnp.zeros_like(sq)
+        for c in exchange:
+            c.start()
+        for ref in (sq, gain, bias):
+            ref[...] = jnp.zeros_like(ref)
         for c in fetch:
             c.wait()
 
@@ -722,84 +744,93 @@
             ring.sum_step(s, place)
             ring.spread_step(s - (chips - 1))
 
-    paced(i, steps, limit, advance)
-    here = pl.ds(i * height, height)
-    share[...] = (nt(own_grad[here, :], wqkv[...]) + back[...]).astype(BF)
-    y = (nn(own_context[here, :], wout[...]) + update[...]).astype(BF).astype(F32)
-    y = hidden[...].astype(F32) + (y + sum(p[...].astype(F32) for p in sent))
-    result[...] = y.astype(BF)
-    sq[...] += jnp.sum((y * y).reshape(height // 8, 8, -1), axis=0)
+    fold = lambda v: jnp.sum(v.reshape(v.shape[0] // 8, 8, -1), axis=0)
+    paced(i, steps, 2 * chips - 1, advance)
+
+    @pl.when(i < first)
+    def _():
+        here = pl.ds(i * height, height)
+        share[here, :] = (nt(own_grad[here, :], wqkv[...]) + back[...]).astype(BF)
+        y = (nn(own_context[here, :], wout[...]) + update[...]).astype(BF).astype(F32)
+        y = hidden[...].astype(F32) + (y + sum(p[...].astype(F32) for p in sent))
+        result[...] = y.astype(BF)
+        sq[...] += fold(y * y)
+
+    @pl.when(i == late)
+    def _():
+        for c in exchange:
+            c.wait()
+
+    @pl.when(i >= late)
+    def _():
+        here = pl.ds((i - late) * tall, tall)
+        x = again[...].astype(F32)
+        mean = jnp.mean(x, axis=1, keepdims=True)
+        centred = x - mean
+        var = jnp.mean(centred * centred, axis=1, keepdims=True)
+        inv = lax.rsqrt(var + epsilon)
+        unit = centred * inv
+        full = share[here, :].astype(F32) + sum(got[s, here, :].astype(F32) for s in range(others))
+        g = full * scale[...]
+        grad[...] = dy[...].astype(F32) + inv * (
+            g - jnp.mean(g, axis=1, keepdims=True) - unit * jnp.mean(g * unit, axis=1, keepdims=True)
+        )
+        gain[...] += fold(full * unit)
+        bias[...] += fold(full)
 
     @pl.when(i == steps - 1)
     def _():
+        lane = lax.broadcasted_iota(jnp.int32, (1, d), 1)
+        stats = [jnp.sum(sq[...]), jnp.sum(ctx_sq[...]), sum(jnp.sum(a[...]) for a in acts)]
+        kept[0, 0:1, :] = jnp.sum(gain[...], axis=0, keepdims=True)
+        kept[0, 1:2, :] = jnp.sum(bias[...], axis=0, keepdims=True)
+        kept[0, 2:3, :] = jnp.where(lane == 0, stats[0], jnp.where(lane == 1, stats[1], jnp.where(lane == 2, stats[2], 0.0)))
+        kept[0, 3:8, :] = jnp.zeros((5, d), F32)
+        for k in range(rounds):
+            copy = pltpu.make_async_remote_copy(
+                src_ref=kept.at[k], dst_ref=held.at[k], send_sem=send.at[k], recv_sem=recv.at[k], **partner(k)
+            )
+            copy.start()
+            copy.wait()
+            kept[k + 1] = kept[k] + held[k]
+        sums[...] = kept[rounds]
         for ring in rings:
             ring.sum_finish()
             ring.spread_finish()
 
 
-def tail(xs, gqkv, context, wqkv, wout, back, update, hidden, sent, collective_id):
+def tail(xs, gqkv, context, wqkv, wout, scale, back, update, hidden, dy, sent, shares, acts, ctx_sq, collective_id):
+    n_dp, n_mp = lax.axis_size("dp"), lax.axis_size("mp")
+    rounds = (n_dp * n_mp).bit_length() - 1
     cuts = [Ring.cut(x) for x in xs]
     shapes = [c.shape for c in cuts]
     rows, d = hidden.shape
-    steps = 16
+    steps, first, late = 16, 8, 4
     any_ = pl.BlockSpec(memory_space=pl.ANY)
-    row = pl.BlockSpec((rows // steps, d), lambda i: (i, 0))
-    share, result, sq, *totals = pl.pallas_call(
-        functools.partial(tail_kernel, steps, len(sent), shapes),
+    early = pl.BlockSpec((rows // first, d), lambda i: (jnp.minimum(i, first - 1), 0))
+    after = pl.BlockSpec((rows // late, d), lambda i: (jnp.maximum(i - (steps - late), 0), 0))
+    dma = pltpu.SemaphoreType.DMA
+    acc = pltpu.VMEM((8, d), F32)
+    result, grad, sums, *totals = pl.pallas_call(
+        functools.partial(tail_kernel, steps, n_dp, n_mp, len(acts), shapes),
         grid=(steps,),
-        in_specs=[any_, any_, whole(wqkv.shape), whole(wout.shape), row, row, row] + [row] * len(sent) + [any_] * len(xs),
-        out_specs=[row, row, pl.BlockSpec((8, d), lambda i: (0, 0))] + [any_] * len(xs),
-        out_shape=[struct((rows, d), BF), struct((rows, d), BF), struct((8, d), F32)] + [struct(c, BF) for c in shapes],
+        in_specs=[any_, any_, whole(wqkv.shape), whole(wout.shape), whole(scale.shape), early, early, early, after, after]
+        + [early] * len(sent) + [any_] * len(shares)
+        + [whole(a.shape) for a in acts] + [whole(ctx_sq.shape)] + [any_] * len(xs),
+        out_specs=[early, after, pl.BlockSpec((8, d), lambda i: (0, 0))] + [any_] * len(xs),
+        out_shape=[struct((rows, d), BF), struct((rows, d), F32), struct((8, d), F32)] + [struct(c, BF) for c in shapes],
         scratch_shapes=[
-            pltpu.VMEM((rows, gqkv.shape[1]), BF), pltpu.VMEM((rows, context.shape[1]), BF), pltpu.SemaphoreType.DMA((2,)),
+            pltpu.VMEM((rows, gqkv.shape[1]), BF), pltpu.VMEM((rows, context.shape[1]), BF), dma((2,)),
+            pltpu.VMEM((rows, d), BF), pltpu.VMEM((n_mp - 1, rows, d), BF), dma((n_mp - 1,)), dma((n_mp - 1,)),
+            acc, acc, acc,
+            pltpu.VMEM((rounds, 8, d), F32), pltpu.VMEM((rounds + 1, 8, d), F32), dma((rounds,)), dma((rounds,)),
         ]
         + [r for c in shapes for r in Ring.sum_scratch(c) + Ring.spread_scratch(c)],
         compiler_params=params(collective_id=collective_id, has_side_effects=True),
-        cost_estimate=cost(2 * rows * d * (gqkv.shape[1] + context.shape[1]), sum(4 * x.size for x in xs) + 20 * rows * d),
+        cost_estimate=cost(2 * rows * d * (gqkv.shape[1] + context.shape[1]), sum(4 * x.size for x in xs) + 30 * rows * d),
         name="tail",
-    )(gqkv, context, wqkv, wout, back, update, hidden, *sent, *cuts)
-    return share, result, sq, *[t.reshape(x.shape) for t, x in zip(totals, xs)]
-
-
-def small_kernel(n_dp, n_mp, x, out, held, kept, send, recv):
-    me = lax.axis_index("dp") * n_mp + lax.axis_index("mp")
-    rounds = held.shape[0]
-
-    def target(k):
-        t = me + 2**k * (1 - 2 * lax.rem(me // 2**k, 2))
-        return dict(device_id={"dp": t // n_mp, "mp": lax.rem(t, n_mp)}, device_id_type=pl.DeviceIdType.MESH)
-
-    barrier = pltpu.get_barrier_semaphore()
-    for k in range(rounds):
-        pl.semaphore_signal(barrier, inc=1, **target(k))
-    pl.semaphore_wait(barrier, rounds)
-    kept[0] = x[...]
-    for k in range(rounds):
-        copy = pltpu.make_async_remote_copy(
-            src_ref=kept.at[k], dst_ref=held.at[k], send_sem=send.at[k], recv_sem=recv.at[k], **target(k)
-        )
-        copy.start()
-        copy.wait()
-        kept[k + 1] = kept[k] + held[k]
-    out[...] = kept[rounds]
-
-
-def small_sum(x, collective_id):
-    n_dp, n_mp = lax.axis_size("dp"), lax.axis_size("mp")
-    rounds = (n_dp * n_mp).bit_length() - 1
-    dma = pltpu.SemaphoreType.DMA
-    vmem = pl.BlockSpec(memory_space=pltpu.VMEM)
-    return pl.pallas_call(
-        functools.partial(small_kernel, n_dp, n_mp),
-        out_shape=struct(x.shape, F32),
-        in_specs=[vmem],
-        out_specs=vmem,
-        scratch_shapes=[
-            pltpu.VMEM((rounds,) + x.shape, F32), pltpu.VMEM((rounds + 1,) + x.shape, F32), dma((rounds,)), dma((rounds,)),
-        ],
-        compiler_params=params(collective_id=collective_id, has_side_effects=True),
-        name="small_sum",
-    )(x)
+    )(gqkv, context, wqkv, wout, scale, back, update, hidden, hidden, dy, *sent, *shares, *acts, ctx_sq, *cuts)
+    return result, grad, sums, *[t.reshape(x.shape) for t, x in zip(totals, xs)]
 
 
 def norm_kernel(x_ref, scale, bias, out):
@@ -825,71 +856,36 @@
     )(x, scale, bias)
 
 
-def norm_back_kernel(n, x_ref, dy, scale, *refs):
-    parts, out, gain, bias = refs[:n], refs[n], refs[n + 1], refs[n + 2]
-
-    @pl.when(pl.program_id(0) == 0)
-    def _():
-        gain[...] = jnp.zeros_like(gain)
-        bias[...] = jnp.zeros_like(bias)
-
-    x = x_ref[...].astype(F32)
-    mean = jnp.mean(x, axis=1, keepdims=True)
-    centred = x - mean
-    var = jnp.mean(centred * centred, axis=1, keepdims=True)
-    inv = lax.rsqrt(var + epsilon)
-    unit = centred * inv
-    grad = sum(p[...].astype(F32) for p in parts)
-    g = grad * scale[...]
-    out[...] = dy[...].astype(F32) + inv * (
-        g - jnp.mean(g, axis=1, keepdims=True) - unit * jnp.mean(g * unit, axis=1, keepdims=True)
-    )
-    fold = lambda v: jnp.sum(v.reshape(v.shape[0] // 8, 8, -1), axis=0)
-    gain[...] += fold(grad * unit)
-    bias[...] += fold(grad)
-
-
-def norm_back(x, dy, scale, parts):
-    rows, d = x.shape
-    tile = pl.BlockSpec((min(TILE, rows), d), lambda i: (i, 0))
-    acc = pl.BlockSpec((8, d), lambda i: (0, 0))
-    return pl.pallas_call(
-        functools.partial(norm_back_kernel, len(parts)),
-        grid=(rows // min(TILE, rows),),
-        in_specs=[tile, tile, whole((1, d))] + [tile] * len(parts),
-        out_specs=[tile, acc, acc],
-        out_shape=[struct((rows, d), F32), struct((8, d), F32), struct((8, d), F32)],
-        compiler_params=params(),
-        cost_estimate=cost(20 * rows * d, 12 * rows * d),
-        name="norm_back",
-    )(x, dy, scale, *parts)
-
-
-def layout(lengths, group_rows):
-    seg_ends = jnp.cumsum(lengths)
-    positions = jnp.arange(group_rows, dtype=jnp.int32)
-    closed = seg_ends[None, :] <= positions[:, None]
-    segment = jnp.sum(closed.astype(jnp.int32), axis=1)
-    seg_start = jnp.sum(jnp.where(closed, lengths[None, :], 0), axis=1)
-    return segment, positions - seg_start
-
-
 def table_kernel(ends_ref, lens_ref, freq, cos, fwd, back, hot, neg):
     rows = cos.shape[0]
+    half = ROT // 2
+
+    def segments(where):
+        segment = jnp.zeros(where.shape, jnp.int32)
+        start = jnp.zeros(where.shape, jnp.int32)
+        for j in range(ends_ref.shape[0]):
+            closed = where >= ends_ref[j]
+            segment = segment + closed.astype(jnp.int32)
+            start = start + jnp.where(closed, lens_ref[j], 0)
+        return segment, where - start
+
+    _, offset = segments(lax.broadcasted_iota(jnp.int32, (half, rows), 1))
+    angle = offset.astype(F32) * freq[...]
+    dim = lax.rem(lax.broadcasted_iota(jnp.int32, (half, LANES), 1), HEAD)
+    unit = lax.broadcasted_iota(jnp.int32, (half, LANES), 0)
+
+    def spread(table, mask):
+        return lax.dot_general(
+            table, jnp.where(mask, 1.0, 0.0), (((0,), (0,)), ((), ())),
+            precision=lax.Precision.HIGHEST, preferred_element_type=F32,
+        )
+
+    sin = jnp.sin(angle)
     lane = lane_ids(rows)
-    where = lax.broadcasted_iota(jnp.int32, (rows, LANES), 0) + pl.program_id(0) * rows
-    segment = jnp.zeros((rows, LANES), jnp.int32)
-    start = jnp.zeros((rows, LANES), jnp.int32)
-    for j in range(ends_ref.shape[0]):
-        closed = where >= ends_ref[j]
-        segment = segment + closed.astype(jnp.int32)
-        start = start + jnp.where(closed, lens_ref[j], 0)
-    angle = (where - start).astype(F32) * freq[...]
-    dim = lax.rem(lane, HEAD)
-    sin = jnp.sin(angle)
-    cos[...] = jnp.where(dim < ROT, jnp.cos(angle), 1.0)
-    fwd[...] = jnp.where(dim < ROT // 2, -sin, 0.0)
-    back[...] = jnp.where((dim >= ROT // 2) & (dim < ROT), sin, 0.0)
+    cos[...] = jnp.where(lax.rem(lane, HEAD) < ROT, spread(jnp.cos(angle), (dim == unit) | (dim == unit + half)), 1.0)
+    fwd[...] = spread(-sin, dim == unit)
+    back[...] = spread(sin, dim == unit + half)
+    segment, _ = segments(lax.broadcasted_iota(jnp.int32, (rows, LANES), 0))
     same = lane - HEAD == segment
     hot[...] = jnp.where(same, 1.0, 0.0).astype(BF)
     neg[...] = jnp.where(same | (lane < HEAD) | (lane >= HEAD + ends_ref.shape[0]), 0.0, excluded).astype(BF)
@@ -897,16 +893,14 @@
 
 def tables(lengths, group_rows):
     half = ROT // 2
-    freq = jnp.power(rope_base, -2.0 * jnp.arange(half, dtype=F32) / ROT)
-    freq = jnp.pad(jnp.tile(freq, 2), (0, HEAD - ROT))
-    freq = jnp.tile(freq, LANES // HEAD)[None, :]
-    block = pl.BlockSpec((TILE, LANES), lambda i, *_: (i, 0))
+    freq = jnp.power(rope_base, -2.0 * jnp.arange(half, dtype=F32) / ROT)[:, None]
+    block = pl.BlockSpec((group_rows, LANES), lambda i, *_: (0, 0))
     return pl.pallas_call(
         table_kernel,
         grid_spec=pltpu.PrefetchScalarGridSpec(
             num_scalar_prefetch=2,
-            grid=(group_rows // TILE,),
-            in_specs=[whole((1, LANES))],
+            grid=(1,),
+            in_specs=[whole((half, 1))],
             out_specs=[block] * 5,
         ),
         out_shape=[struct((group_rows, LANES), F32)] * 3 + [struct((group_rows, LANES), BF)] * 2,
@@ -968,28 +962,24 @@
     joined = [join(slot[s], False, context, wout, ups[s]) for s in range(1, n)]
     sent = [lax.ppermute(v, "mp", ring(n - s)) for s, v in enumerate(joined, 1)]
     gqkv, gdown, gin = attend_back(*qkv, after(do, *joined), wide, keep, *table[:3], done, [gdown, gin], 3)
-    returned = [lax.ppermute(join(slot[s], True, gqkv, wqkv, backs[s]), "mp", ring(n - s)) for s in range(1, n)]
-    gqw, gow = weight_grads(index, x_all, gqkv, dy_all, context)
-    own, result, res_sq, gqw, gow = tail(
-        [gqw, gow], gqkv, context, wqkv, wout, backs[0], ups[0], hidden_in, sent, 1
+    shares = [join(slot[s], True, gqkv, wqkv, backs[s]) for s in range(1, n)]
+    gqw, gow, gdown, gin = weight_grads(index, x_all, gqkv, dy_all, context, [gdown, gin])
+    result, grad_hidden, sums, gqw, gow = tail(
+        [gqw, gow], gqkv, context, wqkv, wout, ln_scale[None, :], backs[0], ups[0], hidden_in, out_grad,
+        sent, shares, sqs, ctx_sq, 1,
     )
-    grad_hidden, gain, bias = norm_back(hidden_in, out_grad, ln_scale[None, :], [own] + returned)
-
-    stats = jnp.stack([jnp.sum(res_sq), jnp.sum(ctx_sq), sum(jnp.sum(s) for s in sqs)])
-    packed = jnp.concatenate([jnp.sum(gain, axis=0), jnp.sum(bias, axis=0), jnp.pad(stats, (0, 8 * LANES - 3))])
-    sums = small_sum(packed.reshape(-1, LANES), 2).reshape(-1)
     devices = lax.axis_size("dp") * n
     counts = jnp.array([rows * d * devices, rows * d * devices, rows * f * n * devices], F32)
     return (
         result,
         grad_hidden,
-        sums[:d],
-        sums[d : 2 * d],
+        sums[0],
+        sums[1],
         gqw.astype(F32),
         gow.T.astype(F32),
-        gin.astype(F32),
-        gdown.astype(F32),
-        jnp.sqrt(sums[2 * d : 2 * d + 3] / counts),
+        gin,
+        gdown,
+        jnp.sqrt(sums[2, :3] / counts),
     )
 
 

time: 439 us -> 410 us (0.934)
  other arithmetic: 29.4 us -> 10.2 us
  Pallas kernels: 379 us -> 366 us
    convert_element_type x2 -> x0, other arithmetic: 11.5 us -> none  [the longest x1 6.81 us: on_device(): gin.astype(F32)]
    reduce_sum x7 -> x0, other arithmetic: 8.13 us -> none  [the longest x3 3.93 us: on_device(): jnp.sum(s)]
    pallas_call x3, Pallas kernels: 92.9 us -> 84.9 us  [feed(): pl.pallas_call(functools.partial(feed_kernel, len(prior)), grid_spec=pltp...]
    pallas_call x3 -> x1, Pallas kernels: 86 us -> 78.4 us  [tail(): pl.pallas_call(functools.partial(tail_kernel, steps, n_dp, n_mp, len(acts...]
    pallas_call x1, Pallas kernels: 15.3 us -> 20.4 us  [weight_grads(): pl.pallas_call(functools.partial(weight_kernel, n), grid_spec=pltpu.Prefe...]
  transfers between devices with their start and end apart: 6 -> 5, of which waited for: 0 -> 1; matrix products, arithmetic and copies ran while one was open for 5% -> 1% of each run, Pallas kernels for 60% -> 47%
where the time goes in v4:
time: 410 us; the launch traced here: 403 us
  Pallas kernels  366 us (89%)
  local copies, waits for them, and re-layouts  15.1 us (4%)
  other arithmetic  10.2 us (2%)
  starting transfers between devices  6.46 us (2%)
  waiting for transfers between devices  4.1 us (1%)
    pallas_call x3, Pallas kernels, feed(): pl.pallas_call(functools.partial(feed_kernel, len(prior)), grid_spec=pltp...  84.9 us
    pallas_call x1, Pallas kernels, tail(): pl.pallas_call(functools.partial(tail_kernel, steps, n_dp, n_mp, len(acts...  78.4 us
    pallas_call x1, Pallas kernels, attend_back(): pl.pallas_call(functools.partial(attend_back_kernel, heads // 2, shapes),...  77.1 us
    pallas_call x1, Pallas kernels, attend(): pl.pallas_call(functools.partial(attend_kernel, heads // 2, shapes), grid...  58.5 us
    pallas_call x3, Pallas kernels, project(): pl.pallas_call(project_kernel, grid_spec=pltpu.PrefetchScalarGridSpec(num...  23.2 us
    pallas_call x1, Pallas kernels, weight_grads(): pl.pallas_call(functools.partial(weight_kernel, n), grid_spec=pltpu.Prefe...  20.4 us
    pallas_call x2, Pallas kernels, join(): pl.pallas_call(functools.partial(join_kernel, transposed), grid_spec=pltp...  12.3 us
  transfers between devices with their start and end apart: 5, of which 1 were waited for; matrix products, arithmetic and copies ran while one was open for 1% of the time, Pallas kernels for 47%

profile of v4, /device:TPU:0, one launch (start us, length us, event | category | flops | bytes accessed | tf_op | source)
XLA Modules:
  0.0 403.2 jit_solution(17777756630941708274)
XLA Ops:
  0.6 0.0 copy-start
  0.7 4.6 %norm.1.nrm.refs_0_ = bf16[1024,1024]{1,0:T(8,128)(2,1)} custom-call(bf16[1024,1024]{1,0:T(8,128)(2,1)} %again.1, f32[1,1024]{1,0:T(1,128)} %bitcast.29, f32[1,1024]{1,0:T(1,128)} %bitcast.33), custom_call_target="tpu_custom_call" | custom-call | flops 10485760 | bytes 4194304 | tf_op jit(solution)/shard_map/norm/pallas_call | solution.py:847
  5.3 3.0 fusion.1
  8.3 2.9 collective-permute-start
  11.3 0.0 copy-done
  11.3 1.5 fusion
  12.8 0.0 collective-permute-start.1
  12.8 39.0 %feed.3 = (bf16[8,2048,128]{2,1,0:T(8,128)(2,1)}, f32[1024,1024]{1,0:T(8,128)}, f32[1024,1024]{1,0:T(8,128)}, bf16[2048,1024]{1,0:T(8,128)(2,1)}, bf16[1024,2048]{1,0:T(8,128)(2,1)}, /*index=5*/f32[8,512]{1,0:T(8,128)}) custom-call(s32[1]{0:T(128)} %bitcast.3.slot, bf16[1024,1024]{1,0:T(8,128)(2,1)} %norm.1.nrm.refs_0_, bf16[1024,1024]{1,0:T(8,128)(2,1)} %dy.3, ...), custom_call_target="tpu_custom_call" | custom-call | flops 25769803776 | bytes 46137344 | tf_op jit(solution)/shard_map/feed/pallas_call | solution.py:179
  51.8 0.6 pad_add_fusion.index
  52.4 0.6 multiply_power_fusion.freq
  53.0 0.0 collective-permute-done.nrm.refs_1_
  53.0 0.0 copy-start.1
  53.0 4.1 %collective-permute-done.1.dy.refs_7_ = bf16[512,1024]{1,0:T(8,128)(2,1)S(1)} collective-permute-done((bf16[512,1024]{1,0:T(8,128)(2,1)}, bf16[512,1024]{1,0:T(8,128)(2,1)S(1)}, u32[]{:S(2)}, u32[]{:S(2)}) %collective-permute-start.1) | collective-permute-done | bytes 1048608 | tf_op jit(solution)/shard_map/ppermute | solution.py:933
  57.1 1.7 collective-permute-start.2
  58.8 0.3 collective-permute-start.3
  59.1 0.0 copy-done.1
  59.1 0.0 copy-done.6
  59.1 23.1 %feed.4 = (bf16[8,2048,128]{2,1,0:T(8,128)(2,1)}, f32[1024,1024]{1,0:T(8,128)}, f32[1024,1024]{1,0:T(8,128)}, bf16[2048,1024]{1,0:T(8,128)(2,1)}, bf16[1024,2048]{1,0:T(8,128)(2,1)}, /*index=5*/f32[8,512]{1,0:T(8,128)}) custom-call(s32[1]{0:T(128)S(6)} %mul.6.slot, bf16[512,1024]{1,0:T(8,128)(2,1)} %copy-done.1, ...), custom_call_target="tpu_custom_call", output_to_operand_aliasing={{0}: (8, {})} | custom-call | flops 12884901888 | bytes 35651584 | tf_op jit(solution)/shard_map/feed/pallas_call | solution.py:179
  82.2 0.0 copy-done.7
  82.3 0.7 reduce-window.9
  82.9 6.8 %tables.1 = (f32[2048,128]{1,0:T(8,128)}, f32[2048,128]{1,0:T(8,128)}, f32[2048,128]{1,0:T(8,128)}, bf16[2048,128]{1,0:T(8,128)(2,1)}, bf16[2048,128]{1,0:T(8,128)(2,1)}) custom-call(s32[4]{0:T(128)} %bitcast.36, s32[4]{0:T(128)} %bitcast.34, f32[8,1]{1,0:T(8,128)} %multiply_power_fusion.freq), custom_call_target="tpu_custom_call" | custom-call | tf_op jit(solution)/shard_map/tables/pallas_call | solution.py:898
  89.7 9.7 %project.3 = (bf16[8,2048,128]{2,1,0:T(8,128)(2,1)}, bf16[8,2048,128]{2,1,0:T(8,128)(2,1)}, bf16[8,2048,128]{2,1,0:T(8,128)(2,1)}) custom-call(s32[1]{0:T(128)} %bitcast.3.slot, bf16[1024,1024]{1,0:T(8,128)(2,1)} %norm.1.nrm.refs_0_, bf16[1024,1536]{1,0:T(8,128)(2,1)} %wqkv.7, f32[2048,128]{1,0:T(8,128)} %get-tuple-element.77.cos, ...), custom_call_target="tpu_custom_call" | custom-call | flops 3221225472 | bytes 15728640 | tf_op jit(solution)/shard_map/project/pallas_call | solution.py:108
  99.4 7.0 %project.4 = (bf16[8,2048,128]{2,1,0:T(8,128)(2,1)}, bf16[8,2048,128]{2,1,0:T(8,128)(2,1)}, bf16[8,2048,128]{2,1,0:T(8,128)(2,1)}) custom-call(s32[1]{0:T(128)S(6)} %mul.6.slot, bf16[512,1024]{1,0:T(8,128)(2,1)} %copy-done.1, bf16[1024,1536]{1,0:T(8,128)(2,1)} %wqkv.7, ...), custom_call_target="tpu_custom_call", output_to_operand_aliasing={{0}: (8, {}), {1}: (9, {}), {2}: (10, {})} | custom-call | flops 1610612736 | bytes 9437184 | tf_op jit(solution)/shard_map/project/pallas_call | solution.py:108
  106.4 0.0 collective-permute-done.2.nrm.refs_2_
  106.4 0.0 collective-permute-done.3.dy.refs_8_
  106.4 1.0 copy-done.2
  107.4 22.8 %feed.5 = (bf16[8,2048,128]{2,1,0:T(8,128)(2,1)}, f32[1024,1024]{1,0:T(8,128)}, f32[1024,1024]{1,0:T(8,128)}, bf16[2048,1024]{1,0:T(8,128)(2,1)}, bf16[1024,2048]{1,0:T(8,128)(2,1)}, /*index=5*/f32[8,512]{1,0:T(8,128)}) custom-call(s32[1]{0:T(128)S(6)} %add.15.slot, ...), custom_call_target="tpu_custom_call", output_to_operand_aliasing={{0}: (8, {}), {1}: (9, {}), {2}: (10, {})} | custom-call | flops 12884901888 | bytes 35651584 | tf_op jit(solution)/shard_map/feed/pallas_call | solution.py:179
  130.2 6.6 %project.5 = (bf16[8,2048,128]{2,1,0:T(8,128)(2,1)}, bf16[8,2048,128]{2,1,0:T(8,128)(2,1)}, bf16[8,2048,128]{2,1,0:T(8,128)(2,1)}) custom-call(s32[1]{0:T(128)S(6)} %add.15.slot, bf16[512,1024]{1,0:T(8,128)(2,1)} %copy-done.2, bf16[1024,1536]{1,0:T(8,128)(2,1)} %wqkv.7, ...), custom_call_target="tpu_custom_call", output_to_operand_aliasing={{0}: (8, {}), {1}: (9, {}), {2}: (10, {})} | custom-call | flops 1610612736 | bytes 9437184 | tf_op jit(solution)/shard_map/project/pallas_call | solution.py:108
  136.7 58.5 %attend.1 = (bf16[2048,512]{1,0:T(8,128)(2,1)}, f32[8,2048,128]{2,1,0:T(8,128)}, bf16[8,36,256,256]{3,2,1,0:T(8,128)(2,1)}, f32[8,128]{1,0:T(8,128)}, bf16[4,32,...) custom-call(bf16[8,2048,128]{2,1,0:T(8,128)(2,1)} %get-tuple-element.94.q_ref, ...), custom_call_target="tpu_custom_call" | custom-call | flops 19327352832 | bytes 41943040 | tf_op jit(solution)/shard_map/attend/pallas_call | solution.py:299
  195.2 4.6 %join.2 = bf16[1024,1024]{1,0:T(8,128)(2,1)} custom-call(s32[1]{0:T(128)} %bitcast.slot, bf16[2048,512]{1,0:T(8,128)(2,1)} %get-tuple-element.99.a.refs_9_.refs_10_.refs_11_.context, bf16[512,1024]{1,0:T(8,128)(2,1)} %wout.7, f32[1024,1024]{1,0:T(8,128)} %get-tuple-element.100.c), custom_call_target="tpu_custom_call" | custom-call | flops 1073741824 | bytes 8388608 | tf_op jit(solution)/shard_map/join/pallas_call | solution.py:451
  199.8 1.5 collective-permute-start.4
  201.3 77.1 %attend_back.1 = (bf16[2048,1536]{1,0:T(8,128)(2,1)}, bf16[2,8,4,32,1024]{4,3,2,1,0:T(8,128)(2,1)}, bf16[2,8,4,16,2048]{4,3,2,1,0:T(8,128)(2,1)}) custom-call(bf16[8,2048,128]{2,1,0:T(8,128)(2,1)} %get-tuple-element.94.q_ref, bf16[8,2048,128]{2,1,0:T(8,128)(2,1)} %get-tuple-element.95.k_ref, bf16[8,2048,128]{2,1,0:T(8,128)(2,1)} %get-tuple-element.96.v_ref, ...), custom_call_target="tpu_custom_call" | custom-call | flops 38654705664 | bytes 83886080 | tf_op jit(solution)/shard_map/attend_back/pallas_call | solution.py:424
  278.4 7.7 %join.3.refs_1_ = bf16[1024,1024]{1,0:T(8,128)(2,1)} custom-call(s32[1]{0:T(128)} %bitcast.slot, bf16[2048,1536]{1,0:T(8,128)(2,1)} %get-tuple-element.106.a.refs_3_.refs_4_.refs_5_.gqkv, bf16[1024,1536]{1,0:T(8,128)(2,1)} %wqkv.7, f32[1024,1024]{1,0:T(8,128)} %get-tuple-element.109.c), custom_call_target="tpu_custom_call" | custom-call | flops 3221225472 | bytes 12582912 | tf_op jit(solution)/shard_map/join/pallas_call | solution.py:451
  286.1 20.4 %weight_grads.1 = (bf16[1024,1536]{1,0:T(8,128)(2,1)}, bf16[1024,512]{1,0:T(8,128)(2,1)}, f32[2048,1024]{1,0:T(8,128)}, f32[1024,2048]{1,0:T(8,128)}) custom-call(s32[3]{0:T(128)} %pad_add_fusion.index, bf16[1024,1024]{1,0:T(8,128)(2,1)} %norm.1.nrm.refs_0_, bf16[512,1024]{1,0:T(8,128)(2,1)} %copy-done.1, bf16[512,1024]{1,0:T(8,128)(2,1)} %copy-done.2, ...), custom_call_target="tpu_custom_call" | custom-call | flops 8589934592 | bytes 20971520 | tf_op jit(solution)/shard_map/weight_grads/pallas_call | solution.py:494
  306.5 0.0 collective-permute-done.4.refs_0_
  306.5 0.0 copy-start.5
  306.5 1.3 copy-done.5
  307.8 78.4 %tail.1 = (bf16[1024,1024]{1,0:T(8,128)(2,1)}, f32[1024,1024]{1,0:T(8,128)}, f32[8,1024]{1,0:T(8,128)}, bf16[2,8,4,16,1536]{4,3,2,1,0:T(8,128)(2,1)}, bf16[2,8,4,16,512]{4,3,2,1,0:T(8,128)(2,1)}) custom-call(bf16[2048,1536]{1,0:T(8,128)(2,1)} %get-tuple-element.106.a.refs_3_.refs_4_.refs_5_.gqkv, ...), custom_call_target="tpu_custom_call" | custom-call | flops 4294967296 | bytes 39845888 | tf_op jit(solution)/shard_map/tail/pallas_call | solution.py:814
  386.2 1.4 fusion.2
  387.7 0.0 copy-done.8
  387.7 1.2 sqrt_bitcast_fusion
  388.9 1.5 bitcast_convert_fusion.1
  390.4 1.8 copy.29
  392.2 5.6 %bitcast_convert_fusion = f32[1024,1536]{1,0:T(8,128)} fusion(bf16[2,8,4,16,1536]{4,3,2,1,0:T(8,128)(2,1)} %get-tuple-element.121), kind=kLoop, calls=%fused_computation | loop fusion | flops 1572864 | bytes 9437184 | tf_op jit(solution)/shard_map/convert_element_type | solution.py:978
  397.8 0.0 copy-done.4
  397.8 1.3 copy.42
  399.1 1.6 copy-done.3
  400.8 2.0 copy.43
  (6 shorter events, 0.0 us)
Async XLA Ops:
  0.6 10.6 %copy-start = (bf16[1024,1024]{1,0:T(8,128)(2,1)S(1)}, bf16[1024,1024]{1,0:T(8,128)(2,1)}, u32[]{:S(2)}) copy-start(bf16[1024,1024]{1,0:T(8,128)(2,1)} %dy.3) | copy-start | bytes 6291460
  8.3 44.7 %collective-permute-start = (bf16[512,1024]{1,0:T(8,128)(2,1)}, bf16[512,1024]{1,0:T(8,128)(2,1)S(1)}, u32[]{:S(2)}, u32[]{:S(2)}) collective-permute-start(bf16[512,1024]{1,0:T(8,128)(2,1)} %get-tuple-element.127), channel_id=1, source_target_pairs={{1,0},{0,1},{3,2},{2,3},{5,4},{4,5},{7,6},{6,7},{9,8},{8,9},{11,10... | collective-permute-start | bytes 3145736 | tf_op jit(solution)/shard_map/ppermute | solution.py:933
  12.8 44.3 %collective-permute-start.1 = (bf16[512,1024]{1,0:T(8,128)(2,1)}, bf16[512,1024]{1,0:T(8,128)(2,1)S(1)}, u32[]{:S(2)}, u32[]{:S(2)}) collective-permute-start(bf16[512,1024]{1,0:T(8,128)(2,1)} %get-tuple-element.125), channel_id=1, source_target_pairs={{1,0},{0,1},{3,2},{2,3},{5,4},{4,5},{7,6},{6,7},{9,8},{8,9},{11,10... | collective-permute-start | bytes 3145736 | tf_op jit(solution)/shard_map/ppermute | solution.py:933
  53.0 6.1 %copy-start.1 = (bf16[512,1024]{1,0:T(8,128)(2,1)}, bf16[512,1024]{1,0:T(8,128)(2,1)S(1)}, u32[]{:S(2)}) copy-start(bf16[512,1024]{1,0:T(8,128)(2,1)S(1)} %collective-permute-done.nrm.refs_1_) | copy-start | bytes 3145732
  57.1 2.0 copy-start.6
  57.1 49.3 %collective-permute-start.2 = (bf16[512,1024]{1,0:T(8,128)(2,1)}, bf16[512,1024]{1,0:T(8,128)(2,1)S(1)}, u32[]{:S(2)}, u32[]{:S(2)}) collective-permute-start(bf16[512,1024]{1,0:T(8,128)(2,1)} %get-tuple-element.67), channel_id=1, source_target_pairs={{1,0},{0,1},{3,2},{2,3},{5,4},{4,5},{7,6},{6,7},{9,8},{8,9},{11,10... | collective-permute-start | bytes 3145736 | tf_op jit(solution)/shard_map/ppermute | solution.py:933
  58.8 47.5 %collective-permute-start.3 = (bf16[512,1024]{1,0:T(8,128)(2,1)}, bf16[512,1024]{1,0:T(8,128)(2,1)}, u32[]{:S(2)}, u32[]{:S(2)}) collective-permute-start(bf16[512,1024]{1,0:T(8,128)(2,1)} %get-tuple-element.68), channel_id=1, source_target_pairs={{1,0},{0,1},{3,2},{2,3},{5,4},{4,5},{7,6},{6,7},{9,8},{8,9},{11,10... | collective-permute-start | bytes 3145736 | tf_op jit(solution)/shard_map/ppermute | solution.py:933
  59.1 23.1 %copy-start.7 = (s32[1,4]{1,0:T(1,128)S(1)}, s32[1,4]{1,0:T(1,128)}, u32[]{:S(2)}) copy-start(s32[1,4]{1,0:T(1,128)} %param.11) | copy-start | bytes 52
  106.4 1.0 copy-start.2
  199.8 106.7 %collective-permute-start.4 = (bf16[1024,1024]{1,0:T(8,128)(2,1)}, bf16[1024,1024]{1,0:T(8,128)(2,1)S(1)}, u32[]{:S(2)}, u32[]{:S(2)}) collective-permute-start(bf16[1024,1024]{1,0:T(8,128)(2,1)} %join.2), channel_id=1, source_target_pairs={{1,0},{0,1},{3,2},{2,3},{5,4},{4,5},{7,6},{6,7},{9,8},{8,9},{11,10... | collective-permute-start | bytes 6291464 | tf_op jit(solution)/shard_map/ppermute | solution.py:963
  306.5 1.3 copy-start.5
  307.8 79.8 %copy-start.8 = (f32[1,3]{1,0:T(1,128)S(1)}, f32[1,3]{1,0:T(1,128)}, u32[]{:S(2)}) copy-start(f32[1,3]{1,0:T(1,128)} %constant.41) | copy-start | bytes 40
  392.2 5.6 %copy-start.4 = (bf16[1024,1024]{1,0:T(8,128)(2,1)S(1)}, bf16[1024,1024]{1,0:T(8,128)(2,1)}, u32[]{:S(2)}) copy-start(bf16[1024,1024]{1,0:T(8,128)(2,1)} %get-tuple-element.140) | copy-start | bytes 6291460
  397.8 2.9 copy-start.3

commit v5 on v4

--- a/solution.py
+++ b/solution.py
@@ -411,6 +411,8 @@
     @pl.when(pl.program_id(0) == pairs - 1)
     def _():
         for ring in rings:
+            ring.keep().start()
+        for ring in rings:
             ring.spread_finish()
 
 
@@ -650,7 +652,6 @@
                 self.across(chips - 1, d, self.core).start()
 
     def spread_finish(self):
-        self.keep().start()
         for d in range(self.parts):
             for s in range(self.chips - 1):
                 self.gather(s, d).wait_send()
@@ -780,6 +781,8 @@
 
     @pl.when(i == steps - 1)
     def _():
+        for ring in rings:
+            ring.keep().start()
         lane = lax.broadcasted_iota(jnp.int32, (1, d), 1)
         stats = [jnp.sum(sq[...]), jnp.sum(ctx_sq[...]), sum(jnp.sum(a[...]) for a in acts)]
         kept[0, 0:1, :] = jnp.sum(gain[...], axis=0, keepdims=True)
@@ -833,6 +836,26 @@
     return result, grad, sums, *[t.reshape(x.shape) for t, x in zip(totals, xs)]
 
 
+def widen_kernel(x, y, x_out, y_out):
+    x_out[...] = x[...].astype(F32)
+    y_out[...] = jnp.transpose(y[...].astype(F32))
+
+
+def widen(x, y):
+    rows = x.shape[0]
+    tile = TILE
+    return pl.pallas_call(
+        widen_kernel,
+        grid=(rows // tile,),
+        in_specs=[pl.BlockSpec((tile, x.shape[1]), lambda i: (i, 0)), pl.BlockSpec((tile, y.shape[1]), lambda i: (i, 0))],
+        out_specs=[pl.BlockSpec((tile, x.shape[1]), lambda i: (i, 0)), pl.BlockSpec((y.shape[1], tile), lambda i: (0, i))],
+        out_shape=[struct(x.shape, F32), struct(y.shape[::-1], F32)],
+        compiler_params=params(),
+        cost_estimate=cost(0, 6 * (x.size + y.size)),
+        name="widen",
+    )(x, y)
+
+
 def norm_kernel(x_ref, scale, bias, out):
     x = x_ref[...].astype(F32)
     mean = jnp.mean(x, axis=1, keepdims=True)
@@ -843,10 +866,10 @@
 
 def norm(x, scale, bias):
     rows, d = x.shape
-    tile = pl.BlockSpec((min(TILE, rows), d), lambda i: (i, 0))
+    tile = pl.BlockSpec((min(CHUNK, rows), d), lambda i: (i, 0))
     return pl.pallas_call(
         norm_kernel,
-        grid=(rows // min(TILE, rows),),
+        grid=(rows // min(CHUNK, rows),),
         in_specs=[tile, whole((1, d)), whole((1, d))],
         out_specs=tile,
         out_shape=struct((rows, d), BF),
@@ -968,6 +991,7 @@
         [gqw, gow], gqkv, context, wqkv, wout, ln_scale[None, :], backs[0], ups[0], hidden_in, out_grad,
         sent, shares, sqs, ctx_sq, 1,
     )
+    gqw, gow = widen(gqw, gow)
     devices = lax.axis_size("dp") * n
     counts = jnp.array([rows * d * devices, rows * d * devices, rows * f * n * devices], F32)
     return (
@@ -975,8 +999,8 @@
         grad_hidden,
         sums[0],
         sums[1],
-        gqw.astype(F32),
-        gow.T.astype(F32),
+        gqw,
+        gow,
         gin,
         gdown,
         jnp.sqrt(sums[2, :3] / counts),

time: 410 us -> 404 us (0.985)
  other arithmetic: 10.2 us -> 3.09 us
    convert_element_type x2 -> x0, other arithmetic: 7.12 us -> none  [the longest x1 5.61 us: on_device(): gqw.astype(F32)]
    pallas_call x1 -> x2, Pallas kernels: 4.64 us -> 9.81 us  [the longest x1 5.93 us: widen(): pl.pallas_call(widen_kernel, grid=(rows // tile,), in_specs=[pl.BlockSpec...]
  transfers between devices with their start and end apart: 5 -> 5, of which waited for: 1 -> 1; matrix products, arithmetic and copies ran while one was open for 1% -> 1% of each run, Pallas kernels for 47% -> 48%
where the time goes in v5:
time: 404 us; the launch traced here: 397 us
  Pallas kernels  368 us (91%)
  local copies, waits for them, and re-layouts  13.4 us (3%)
  starting transfers between devices  6.42 us (2%)
  waiting for transfers between devices  4.05 us (1%)
    pallas_call x3, Pallas kernels, feed(): pl.pallas_call(functools.partial(feed_kernel, len(prior)), grid_spec=pltp...  84.9 us
    pallas_call x1, Pallas kernels, tail(): pl.pallas_call(functools.partial(tail_kernel, steps, n_dp, n_mp, len(acts...  76.6 us
    pallas_call x1, Pallas kernels, attend_back(): pl.pallas_call(functools.partial(attend_back_kernel, heads // 2, shapes),...  75.9 us
    pallas_call x1, Pallas kernels, attend(): pl.pallas_call(functools.partial(attend_kernel, heads // 2, shapes), grid...  58.5 us
    pallas_call x3, Pallas kernels, project(): pl.pallas_call(project_kernel, grid_spec=pltpu.PrefetchScalarGridSpec(num...  23.2 us
    pallas_call x1, Pallas kernels, weight_grads(): pl.pallas_call(functools.partial(weight_kernel, n), grid_spec=pltpu.Prefe...  20.4 us
    pallas_call x2, Pallas kernels, join(): pl.pallas_call(functools.partial(join_kernel, transposed), grid_spec=pltp...  12.3 us
  transfers between devices with their start and end apart: 5, of which 1 were waited for; matrix products, arithmetic and copies ran while one was open for 1% of the time, Pallas kernels for 48%

profile of v5, /device:TPU:0, one launch (start us, length us, event | category | flops | bytes accessed | tf_op | source)
XLA Modules:
  0.0 396.5 jit_solution(4330551109259636912)
XLA Ops:
  0.6 0.0 copy-start
  0.7 3.9 norm.1.nrm.refs_0_
  4.5 3.0 fusion.1
  7.6 2.9 collective-permute-start
  10.5 0.0 copy-done
  10.5 1.5 fusion
  12.0 0.0 collective-permute-start.1
  12.0 39.0 %feed.3 = (bf16[8,2048,128]{2,1,0:T(8,128)(2,1)}, f32[1024,1024]{1,0:T(8,128)}, f32[1024,1024]{1,0:T(8,128)}, bf16[2048,1024]{1,0:T(8,128)(2,1)}, bf16[1024,2048]{1,0:T(8,128)(2,1)}, /*index=5*/f32[8,512]{1,0:T(8,128)}) custom-call(s32[1]{0:T(128)} %bitcast.3.slot, bf16[1024,1024]{1,0:T(8,128)(2,1)} %norm.1.nrm.refs_0_, bf16[1024,1024]{1,0:T(8,128)(2,1)} %dy.3, ...), custom_call_target="tpu_custom_call" | custom-call | flops 25769803776 | bytes 46137344 | tf_op jit(solution)/shard_map/feed/pallas_call | solution.py:179
  51.1 0.6 pad_add_fusion.index
  51.7 0.6 multiply_power_fusion.freq
  52.3 0.0 collective-permute-done.nrm.refs_1_
  52.3 0.0 copy-start.1
  52.3 4.0 %collective-permute-done.1.dy.refs_7_ = bf16[512,1024]{1,0:T(8,128)(2,1)S(1)} collective-permute-done((bf16[512,1024]{1,0:T(8,128)(2,1)}, bf16[512,1024]{1,0:T(8,128)(2,1)S(1)}, u32[]{:S(2)}, u32[]{:S(2)}) %collective-permute-start.1) | collective-permute-done | bytes 1048608 | tf_op jit(solution)/shard_map/ppermute | solution.py:956
  56.3 0.0 copy-start.6
  56.3 1.7 collective-permute-start.2
  58.1 0.3 collective-permute-start.3
  58.4 0.0 copy-done.1
  58.4 0.0 copy-done.6
  58.4 23.2 %feed.4 = (bf16[8,2048,128]{2,1,0:T(8,128)(2,1)}, f32[1024,1024]{1,0:T(8,128)}, f32[1024,1024]{1,0:T(8,128)}, bf16[2048,1024]{1,0:T(8,128)(2,1)}, bf16[1024,2048]{1,0:T(8,128)(2,1)}, /*index=5*/f32[8,512]{1,0:T(8,128)}) custom-call(s32[1]{0:T(128)S(6)} %mul.6.slot, bf16[512,1024]{1,0:T(8,128)(2,1)} %copy-done.1, ...), custom_call_target="tpu_custom_call", output_to_operand_aliasing={{0}: (8, {})} | custom-call | flops 12884901888 | bytes 35651584 | tf_op jit(solution)/shard_map/feed/pallas_call | solution.py:179
  81.5 0.0 copy-done.7
  81.5 0.7 reduce-window.9
  82.2 6.8 %tables.1 = (f32[2048,128]{1,0:T(8,128)}, f32[2048,128]{1,0:T(8,128)}, f32[2048,128]{1,0:T(8,128)}, bf16[2048,128]{1,0:T(8,128)(2,1)}, bf16[2048,128]{1,0:T(8,128)(2,1)}) custom-call(s32[4]{0:T(128)} %bitcast.32, s32[4]{0:T(128)} %bitcast.30, f32[8,1]{1,0:T(8,128)} %multiply_power_fusion.freq), custom_call_target="tpu_custom_call" | custom-call | tf_op jit(solution)/shard_map/tables/pallas_call | solution.py:921
  89.0 9.7 %project.3 = (bf16[8,2048,128]{2,1,0:T(8,128)(2,1)}, bf16[8,2048,128]{2,1,0:T(8,128)(2,1)}, bf16[8,2048,128]{2,1,0:T(8,128)(2,1)}) custom-call(s32[1]{0:T(128)} %bitcast.3.slot, bf16[1024,1024]{1,0:T(8,128)(2,1)} %norm.1.nrm.refs_0_, bf16[1024,1536]{1,0:T(8,128)(2,1)} %wqkv.7, f32[2048,128]{1,0:T(8,128)} %get-tuple-element.79.cos, ...), custom_call_target="tpu_custom_call" | custom-call | flops 3221225472 | bytes 15728640 | tf_op jit(solution)/shard_map/project/pallas_call | solution.py:108
  98.7 7.0 %project.4 = (bf16[8,2048,128]{2,1,0:T(8,128)(2,1)}, bf16[8,2048,128]{2,1,0:T(8,128)(2,1)}, bf16[8,2048,128]{2,1,0:T(8,128)(2,1)}) custom-call(s32[1]{0:T(128)S(6)} %mul.6.slot, bf16[512,1024]{1,0:T(8,128)(2,1)} %copy-done.1, bf16[1024,1536]{1,0:T(8,128)(2,1)} %wqkv.7, ...), custom_call_target="tpu_custom_call", output_to_operand_aliasing={{0}: (8, {}), {1}: (9, {}), {2}: (10, {})} | custom-call | flops 1610612736 | bytes 9437184 | tf_op jit(solution)/shard_map/project/pallas_call | solution.py:108
  105.7 0.0 collective-permute-done.2.nrm.refs_2_
  105.7 0.0 collective-permute-done.3.dy.refs_8_
  105.7 1.0 copy-done.2
  106.7 22.7 %feed.5 = (bf16[8,2048,128]{2,1,0:T(8,128)(2,1)}, f32[1024,1024]{1,0:T(8,128)}, f32[1024,1024]{1,0:T(8,128)}, bf16[2048,1024]{1,0:T(8,128)(2,1)}, bf16[1024,2048]{1,0:T(8,128)(2,1)}, /*index=5*/f32[8,512]{1,0:T(8,128)}) custom-call(s32[1]{0:T(128)S(6)} %add.15.slot, ...), custom_call_target="tpu_custom_call", output_to_operand_aliasing={{0}: (8, {}), {1}: (9, {}), {2}: (10, {})} | custom-call | flops 12884901888 | bytes 35651584 | tf_op jit(solution)/shard_map/feed/pallas_call | solution.py:179
  129.4 6.6 %project.5 = (bf16[8,2048,128]{2,1,0:T(8,128)(2,1)}, bf16[8,2048,128]{2,1,0:T(8,128)(2,1)}, bf16[8,2048,128]{2,1,0:T(8,128)(2,1)}) custom-call(s32[1]{0:T(128)S(6)} %add.15.slot, bf16[512,1024]{1,0:T(8,128)(2,1)} %copy-done.2, bf16[1024,1536]{1,0:T(8,128)(2,1)} %wqkv.7, ...), custom_call_target="tpu_custom_call", output_to_operand_aliasing={{0}: (8, {}), {1}: (9, {}), {2}: (10, {})} | custom-call | flops 1610612736 | bytes 9437184 | tf_op jit(solution)/shard_map/project/pallas_call | solution.py:108
  136.0 58.5 %attend.1 = (bf16[2048,512]{1,0:T(8,128)(2,1)}, f32[8,2048,128]{2,1,0:T(8,128)}, bf16[8,36,256,256]{3,2,1,0:T(8,128)(2,1)}, f32[8,128]{1,0:T(8,128)}, bf16[4,32,...) custom-call(bf16[8,2048,128]{2,1,0:T(8,128)(2,1)} %get-tuple-element.96.q_ref, ...), custom_call_target="tpu_custom_call" | custom-call | flops 19327352832 | bytes 41943040 | tf_op jit(solution)/shard_map/attend/pallas_call | solution.py:299
  194.5 4.6 %join.2 = bf16[1024,1024]{1,0:T(8,128)(2,1)} custom-call(s32[1]{0:T(128)} %bitcast.slot, bf16[2048,512]{1,0:T(8,128)(2,1)} %get-tuple-element.101.a.refs_9_.refs_10_.refs_11_.context, bf16[512,1024]{1,0:T(8,128)(2,1)} %wout.7, f32[1024,1024]{1,0:T(8,128)} %get-tuple-element.102.c), custom_call_target="tpu_custom_call" | custom-call | flops 1073741824 | bytes 8388608 | tf_op jit(solution)/shard_map/join/pallas_call | solution.py:453
  199.1 1.5 collective-permute-start.4
  200.5 75.9 %attend_back.1 = (bf16[2048,1536]{1,0:T(8,128)(2,1)}, bf16[2,8,4,32,1024]{4,3,2,1,0:T(8,128)(2,1)}, bf16[2,8,4,16,2048]{4,3,2,1,0:T(8,128)(2,1)}) custom-call(bf16[8,2048,128]{2,1,0:T(8,128)(2,1)} %get-tuple-element.96.q_ref, bf16[8,2048,128]{2,1,0:T(8,128)(2,1)} %get-tuple-element.97.k_ref, bf16[8,2048,128]{2,1,0:T(8,128)(2,1)} %get-tuple-element.98.v_ref, ...), custom_call_target="tpu_custom_call" | custom-call | flops 38654705664 | bytes 83886080 | tf_op jit(solution)/shard_map/attend_back/pallas_call | solution.py:426
  276.4 7.7 %join.3.refs_1_ = bf16[1024,1024]{1,0:T(8,128)(2,1)} custom-call(s32[1]{0:T(128)} %bitcast.slot, bf16[2048,1536]{1,0:T(8,128)(2,1)} %get-tuple-element.108.a.refs_3_.refs_4_.refs_5_.gqkv, bf16[1024,1536]{1,0:T(8,128)(2,1)} %wqkv.7, f32[1024,1024]{1,0:T(8,128)} %get-tuple-element.111.c), custom_call_target="tpu_custom_call" | custom-call | flops 3221225472 | bytes 12582912 | tf_op jit(solution)/shard_map/join/pallas_call | solution.py:453
  284.1 20.4 %weight_grads.1 = (bf16[1024,1536]{1,0:T(8,128)(2,1)}, bf16[1024,512]{1,0:T(8,128)(2,1)}, f32[2048,1024]{1,0:T(8,128)}, f32[1024,2048]{1,0:T(8,128)}) custom-call(s32[3]{0:T(128)} %pad_add_fusion.index, bf16[1024,1024]{1,0:T(8,128)(2,1)} %norm.1.nrm.refs_0_, bf16[512,1024]{1,0:T(8,128)(2,1)} %copy-done.1, bf16[512,1024]{1,0:T(8,128)(2,1)} %copy-done.2, ...), custom_call_target="tpu_custom_call" | custom-call | flops 8589934592 | bytes 20971520 | tf_op jit(solution)/shard_map/weight_grads/pallas_call | solution.py:496
  304.5 0.0 collective-permute-done.4.refs_0_
  304.5 0.0 copy-start.5
  304.5 1.3 copy-done.5
  305.8 76.6 %tail.1 = (bf16[1024,1024]{1,0:T(8,128)(2,1)}, f32[1024,1024]{1,0:T(8,128)}, f32[8,1024]{1,0:T(8,128)}, bf16[2,8,4,16,1536]{4,3,2,1,0:T(8,128)(2,1)}, bf16[2,8,4,16,512]{4,3,2,1,0:T(8,128)(2,1)}) custom-call(bf16[2048,1536]{1,0:T(8,128)(2,1)} %get-tuple-element.108.a.refs_3_.refs_4_.refs_5_.gqkv, ...), custom_call_target="tpu_custom_call" | custom-call | flops 4294967296 | bytes 39845888 | tf_op jit(solution)/shard_map/tail/pallas_call | solution.py:817
  382.4 0.0 copy-start.4
  382.5 1.5 fusion.2
  384.0 0.0 copy-done.8
  384.0 1.2 sqrt_bitcast_fusion
  385.2 5.9 %widen.1 = (f32[1024,1536]{1,0:T(8,128)}, f32[512,1024]{1,0:T(8,128)}) custom-call(bf16[1024,1536]{1,0:T(8,128)(2,1)} %bitcast.21, bf16[1024,512]{1,0:T(8,128)(2,1)} %bitcast.23), custom_call_target="tpu_custom_call" | custom-call | bytes 12582912 | tf_op jit(solution)/shard_map/widen/pallas_call | solution.py:847
  391.1 0.0 copy-done.4
  391.1 1.3 copy.41
  392.4 1.6 copy-done.3
  394.1 2.0 copy.42
  (4 shorter events, 0.0 us)
Async XLA Ops:
  0.6 9.9 %copy-start = (bf16[1024,1024]{1,0:T(8,128)(2,1)S(1)}, bf16[1024,1024]{1,0:T(8,128)(2,1)}, u32[]{:S(2)}) copy-start(bf16[1024,1024]{1,0:T(8,128)(2,1)} %dy.3) | copy-start | bytes 6291460
  7.6 44.7 %collective-permute-start = (bf16[512,1024]{1,0:T(8,128)(2,1)}, bf16[512,1024]{1,0:T(8,128)(2,1)S(1)}, u32[]{:S(2)}, u32[]{:S(2)}) collective-permute-start(bf16[512,1024]{1,0:T(8,128)(2,1)} %get-tuple-element.131), channel_id=1, source_target_pairs={{1,0},{0,1},{3,2},{2,3},{5,4},{4,5},{7,6},{6,7},{9,8},{8,9},{11,10... | collective-permute-start | bytes 3145736 | tf_op jit(solution)/shard_map/ppermute | solution.py:956
  12.0 44.3 %collective-permute-start.1 = (bf16[512,1024]{1,0:T(8,128)(2,1)}, bf16[512,1024]{1,0:T(8,128)(2,1)S(1)}, u32[]{:S(2)}, u32[]{:S(2)}) collective-permute-start(bf16[512,1024]{1,0:T(8,128)(2,1)} %get-tuple-element.129), channel_id=1, source_target_pairs={{1,0},{0,1},{3,2},{2,3},{5,4},{4,5},{7,6},{6,7},{9,8},{8,9},{11,10... | collective-permute-start | bytes 3145736 | tf_op jit(solution)/shard_map/ppermute | solution.py:956
  52.3 6.1 %copy-start.1 = (bf16[512,1024]{1,0:T(8,128)(2,1)}, bf16[512,1024]{1,0:T(8,128)(2,1)S(1)}, u32[]{:S(2)}) copy-start(bf16[512,1024]{1,0:T(8,128)(2,1)S(1)} %collective-permute-done.nrm.refs_1_) | copy-start | bytes 3145732
  56.3 2.0 copy-start.6
  56.3 49.3 %collective-permute-start.2 = (bf16[512,1024]{1,0:T(8,128)(2,1)}, bf16[512,1024]{1,0:T(8,128)(2,1)S(1)}, u32[]{:S(2)}, u32[]{:S(2)}) collective-permute-start(bf16[512,1024]{1,0:T(8,128)(2,1)} %get-tuple-element.69), channel_id=1, source_target_pairs={{1,0},{0,1},{3,2},{2,3},{5,4},{4,5},{7,6},{6,7},{9,8},{8,9},{11,10... | collective-permute-start | bytes 3145736 | tf_op jit(solution)/shard_map/ppermute | solution.py:956
  58.1 47.6 %collective-permute-start.3 = (bf16[512,1024]{1,0:T(8,128)(2,1)}, bf16[512,1024]{1,0:T(8,128)(2,1)}, u32[]{:S(2)}, u32[]{:S(2)}) collective-permute-start(bf16[512,1024]{1,0:T(8,128)(2,1)} %get-tuple-element.70), channel_id=1, source_target_pairs={{1,0},{0,1},{3,2},{2,3},{5,4},{4,5},{7,6},{6,7},{9,8},{8,9},{11,10... | collective-permute-start | bytes 3145736 | tf_op jit(solution)/shard_map/ppermute | solution.py:956
  58.4 23.2 %copy-start.7 = (s32[1,4]{1,0:T(1,128)S(1)}, s32[1,4]{1,0:T(1,128)}, u32[]{:S(2)}) copy-start(s32[1,4]{1,0:T(1,128)} %param.11) | copy-start | bytes 52
  105.7 1.0 copy-start.2
  199.1 105.4 %collective-permute-start.4 = (bf16[1024,1024]{1,0:T(8,128)(2,1)}, bf16[1024,1024]{1,0:T(8,128)(2,1)S(1)}, u32[]{:S(2)}, u32[]{:S(2)}) collective-permute-start(bf16[1024,1024]{1,0:T(8,128)(2,1)} %join.2), channel_id=1, source_target_pairs={{1,0},{0,1},{3,2},{2,3},{5,4},{4,5},{7,6},{6,7},{9,8},{8,9},{11,10... | collective-permute-start | bytes 6291464 | tf_op jit(solution)/shard_map/ppermute | solution.py:986
  304.5 1.3 copy-start.5
  305.8 78.2 %copy-start.8 = (f32[1,3]{1,0:T(1,128)S(1)}, f32[1,3]{1,0:T(1,128)}, u32[]{:S(2)}) copy-start(f32[1,3]{1,0:T(1,128)} %constant.41) | copy-start | bytes 40
  382.4 8.7 %copy-start.4 = (bf16[1024,1024]{1,0:T(8,128)(2,1)S(1)}, bf16[1024,1024]{1,0:T(8,128)(2,1)}, u32[]{:S(2)}) copy-start(bf16[1024,1024]{1,0:T(8,128)(2,1)} %get-tuple-element.144) | copy-start | bytes 6291460
  391.1 2.9 copy-start.3

commit v6 on v5

--- a/solution.py
+++ b/solution.py
@@ -856,27 +856,36 @@
     )(x, y)
 
 
-def norm_kernel(x_ref, scale, bias, out):
+def norm_kernel(x_ref, dy, scale, bias, out, *copies):
     x = x_ref[...].astype(F32)
     mean = jnp.mean(x, axis=1, keepdims=True)
     centred = x - mean
     var = jnp.mean(centred * centred, axis=1, keepdims=True)
-    out[...] = (centred * lax.rsqrt(var + epsilon) * scale[...] + bias[...]).astype(BF)
-
-
-def norm(x, scale, bias):
+    y = (centred * lax.rsqrt(var + epsilon) * scale[...] + bias[...]).astype(BF)
+    out[...] = y
+    for p in range(len(copies) // 2):
+
+        @pl.when(pl.program_id(0) == p)
+        def _(p=p):
+            copies[2 * p][...] = y
+            copies[2 * p + 1][...] = dy[...]
+
+
+def norm(x, dy, scale, bias, pieces):
     rows, d = x.shape
-    tile = pl.BlockSpec((min(CHUNK, rows), d), lambda i: (i, 0))
+    high = rows // pieces
+    tile = pl.BlockSpec((high, d), lambda i: (i, 0))
+    copies = 2 * pieces if pieces > 1 else 0
     return pl.pallas_call(
         norm_kernel,
-        grid=(rows // min(CHUNK, rows),),
-        in_specs=[tile, whole((1, d)), whole((1, d))],
-        out_specs=tile,
-        out_shape=struct((rows, d), BF),
+        grid=(pieces,),
+        in_specs=[tile, tile, whole((1, d)), whole((1, d))],
+        out_specs=[tile] + [whole((high, d))] * copies,
+        out_shape=[struct((rows, d), BF)] + [struct((high, d), BF)] * copies,
         compiler_params=params(),
-        cost_estimate=cost(10 * rows * d, 4 * rows * d),
+        cost_estimate=cost(10 * rows * d, 10 * rows * d),
         name="norm",
-    )(x, scale, bias)
+    )(x, dy, scale, bias)
 
 
 def table_kernel(ends_ref, lens_ref, freq, cos, fwd, back, hot, neg):
@@ -941,16 +950,16 @@
     f = win.shape[1]
     after = lambda x, *deps: lax.optimization_barrier((x, *deps))[0]
 
-    normed = norm(hidden_in, ln_scale[None, :], ln_bias[None, :])
     pieces = 2 if rows >= 2 * CHUNK else 1
-    high = rows // pieces
+    normed, *copies = norm(hidden_in, out_grad, ln_scale[None, :], ln_bias[None, :], pieces)
+    copies = copies or [normed, out_grad]
     ring = lambda s: [((i + s) % n, i) for i in range(n)]
     slot = [((me + s) % n).astype(jnp.int32)[None] for s in range(n)]
     x_all, dy_all, place = [normed], [out_grad], [slot[0]]
     gate = None
     for s in range(1, n):
         for p in range(pieces):
-            mine = [v[p * high : (p + 1) * high] for v in (normed, out_grad)]
+            mine = copies[2 * p : 2 * p + 2]
             if gate is not None:
                 mine = list(lax.optimization_barrier((*mine, *gate))[:2])
             gate = [lax.ppermute(v, "mp", ring(s)) for v in mine]

time: 404 us -> 403 us (level)
  local copies, waits for them, and re-layouts: 13.4 us -> 8.79 us
    slice x2 -> x0, local copies, waits for them, and re-layouts: 4.56 us -> none  [on_device(): mine = [v[p * high:(p + 1) * high] for v in (normed, out_grad)]]
  transfers between devices with their start and end apart: 5 -> 5, of which waited for: 1 -> 1; matrix products, arithmetic and copies ran while one was open for 1% -> 0% of each run, Pallas kernels for 48% -> 48%
where the time goes in v6:
time: 403 us; the launch traced here: 396 us
  Pallas kernels  370 us (92%)
  local copies, waits for them, and re-layouts  8.79 us (2%)
  starting transfers between devices  6.55 us (2%)
  waiting for transfers between devices  5.48 us (1%)
    pallas_call x3, Pallas kernels, feed(): pl.pallas_call(functools.partial(feed_kernel, len(prior)), grid_spec=pltp...  84.9 us
    pallas_call x1, Pallas kernels, tail(): pl.pallas_call(functools.partial(tail_kernel, steps, n_dp, n_mp, len(acts...  76.7 us
    pallas_call x1, Pallas kernels, attend_back(): pl.pallas_call(functools.partial(attend_back_kernel, heads // 2, shapes),...  76 us
    pallas_call x1, Pallas kernels, attend(): pl.pallas_call(functools.partial(attend_kernel, heads // 2, shapes), grid...  58.5 us
    pallas_call x3, Pallas kernels, project(): pl.pallas_call(project_kernel, grid_spec=pltpu.PrefetchScalarGridSpec(num...  23.2 us
    pallas_call x1, Pallas kernels, weight_grads(): pl.pallas_call(functools.partial(weight_kernel, n), grid_spec=pltpu.Prefe...  20.4 us
    pallas_call x2, Pallas kernels, join(): pl.pallas_call(functools.partial(join_kernel, transposed), grid_spec=pltp...  12.3 us
  transfers between devices with their start and end apart: 5, of which 1 were waited for; matrix products, arithmetic and copies ran while one was open for 0% of the time, Pallas kernels for 48%

profile of v6, /device:TPU:0, one launch (start us, length us, event | category | flops | bytes accessed | tf_op | source)
XLA Modules:
  0.0 395.5 jit_solution(14109644281711527876)
XLA Ops:
  0.6 5.8 %norm.1 = (bf16[1024,1024]{1,0:T(8,128)(2,1)}, bf16[512,1024]{1,0:T(8,128)(2,1)}, bf16[512,1024]{1,0:T(8,128)(2,1)}, bf16[512,1024]{1,0:T(8,128)(2,1)}, bf16[512,1024]{1,0:T(8,128)(2,1)}) custom-call(bf16[1024,1024]{1,0:T(8,128)(2,1)} %again.1, bf16[1024,1024]{1,0:T(8,128)(2,1)} %dy.5, f32[1,1024]{1,0:T(1,128)} %bitcast.25, f32[1,1024]{1,0:T(1,128)} %bitcast.29), custom_call_target="tpu_custom_call" | custom-call | flops 10485760 | bytes 10485760 | tf_op jit(solution)/shard_map/norm/pallas_call | solution.py:879
  6.4 2.9 collective-permute-start
  9.3 0.1 collective-permute-start.1
  9.4 39.0 %feed.3 = (bf16[8,2048,128]{2,1,0:T(8,128)(2,1)}, f32[1024,1024]{1,0:T(8,128)}, f32[1024,1024]{1,0:T(8,128)}, bf16[2048,1024]{1,0:T(8,128)(2,1)}, bf16[1024,2048]{1,0:T(8,128)(2,1)}, /*index=5*/f32[8,512]{1,0:T(8,128)}) custom-call(s32[1]{0:T(128)} %bitcast.3.slot, bf16[1024,1024]{1,0:T(8,128)(2,1)} %get-tuple-element.94.nrm.refs_0_, bf16[1024,1024]{1,0:T(8,128)(2,1)} %dy.5, ...), custom_call_target="tpu_custom_call" | custom-call | flops 25769803776 | bytes 46137344 | tf_op jit(solution)/shard_map/feed/pallas_call | solution.py:179
  48.5 0.7 pad_add_fusion.index
  49.1 0.6 multiply_power_fusion.freq
  49.7 0.0 collective-permute-done.nrm.refs_1_
  49.7 0.0 copy-start
  49.7 5.5 %collective-permute-done.1.dy.refs_7_ = bf16[512,1024]{1,0:T(8,128)(2,1)S(1)} collective-permute-done((bf16[512,1024]{1,0:T(8,128)(2,1)}, bf16[512,1024]{1,0:T(8,128)(2,1)S(1)}, u32[]{:S(2)}, u32[]{:S(2)}) %collective-permute-start.1) | collective-permute-done | bytes 1048608 | tf_op jit(solution)/shard_map/ppermute | solution.py:965
  55.2 0.0 copy-start.5
  55.2 1.7 collective-permute-start.2
  56.9 0.3 collective-permute-start.3
  57.2 0.0 copy-done
  57.2 0.0 copy-done.5
  57.2 0.0 copy-start.6
  57.2 23.1 %feed.4 = (bf16[8,2048,128]{2,1,0:T(8,128)(2,1)}, f32[1024,1024]{1,0:T(8,128)}, f32[1024,1024]{1,0:T(8,128)}, bf16[2048,1024]{1,0:T(8,128)(2,1)}, bf16[1024,2048]{1,0:T(8,128)(2,1)}, /*index=5*/f32[8,512]{1,0:T(8,128)}) custom-call(s32[1]{0:T(128)S(6)} %mul.6.slot, bf16[512,1024]{1,0:T(8,128)(2,1)} %copy-done, ...), custom_call_target="tpu_custom_call", output_to_operand_aliasing={{0}: (8, {})} | custom-call | flops 12884901888 | bytes 35651584 | tf_op jit(solution)/shard_map/feed/pallas_call | solution.py:179
  80.3 0.0 copy-done.6
  80.3 0.7 reduce-window.9
  81.0 6.8 %tables.1 = (f32[2048,128]{1,0:T(8,128)}, f32[2048,128]{1,0:T(8,128)}, f32[2048,128]{1,0:T(8,128)}, bf16[2048,128]{1,0:T(8,128)(2,1)}, bf16[2048,128]{1,0:T(8,128)(2,1)}) custom-call(s32[4]{0:T(128)} %bitcast.32, s32[4]{0:T(128)} %bitcast.30, f32[8,1]{1,0:T(8,128)} %multiply_power_fusion.freq), custom_call_target="tpu_custom_call" | custom-call | tf_op jit(solution)/shard_map/tables/pallas_call | solution.py:930
  87.8 9.7 %project.3 = (bf16[8,2048,128]{2,1,0:T(8,128)(2,1)}, bf16[8,2048,128]{2,1,0:T(8,128)(2,1)}, bf16[8,2048,128]{2,1,0:T(8,128)(2,1)}) custom-call(s32[1]{0:T(128)} %bitcast.3.slot, bf16[1024,1024]{1,0:T(8,128)(2,1)} %get-tuple-element.94.nrm.refs_0_, bf16[1024,1536]{1,0:T(8,128)(2,1)} %wqkv.7, f32[2048,128]{1,0:T(8,128)} %get-tuple-element.89.cos, ...), custom_call_target="tpu_custom_call" | custom-call | flops 3221225472 | bytes 15728640 | tf_op jit(solution)/shard_map/project/pallas_call | solution.py:108
  97.5 7.0 %project.4 = (bf16[8,2048,128]{2,1,0:T(8,128)(2,1)}, bf16[8,2048,128]{2,1,0:T(8,128)(2,1)}, bf16[8,2048,128]{2,1,0:T(8,128)(2,1)}) custom-call(s32[1]{0:T(128)S(6)} %mul.6.slot, bf16[512,1024]{1,0:T(8,128)(2,1)} %copy-done, bf16[1024,1536]{1,0:T(8,128)(2,1)} %wqkv.7, ...), custom_call_target="tpu_custom_call", output_to_operand_aliasing={{0}: (8, {}), {1}: (9, {}), {2}: (10, {})} | custom-call | flops 1610612736 | bytes 9437184 | tf_op jit(solution)/shard_map/project/pallas_call | solution.py:108
  104.4 0.0 collective-permute-done.2.nrm.refs_2_
  104.4 0.0 copy-start.1
  104.5 0.0 collective-permute-done.3.dy.refs_8_
  104.5 1.0 copy-done.1
  105.4 22.7 %feed.5 = (bf16[8,2048,128]{2,1,0:T(8,128)(2,1)}, f32[1024,1024]{1,0:T(8,128)}, f32[1024,1024]{1,0:T(8,128)}, bf16[2048,1024]{1,0:T(8,128)(2,1)}, bf16[1024,2048]{1,0:T(8,128)(2,1)}, /*index=5*/f32[8,512]{1,0:T(8,128)}) custom-call(s32[1]{0:T(128)S(6)} %add.15.slot, ...), custom_call_target="tpu_custom_call", output_to_operand_aliasing={{0}: (8, {}), {1}: (9, {}), {2}: (10, {})} | custom-call | flops 12884901888 | bytes 35651584 | tf_op jit(solution)/shard_map/feed/pallas_call | solution.py:179
  128.2 6.6 %project.5 = (bf16[8,2048,128]{2,1,0:T(8,128)(2,1)}, bf16[8,2048,128]{2,1,0:T(8,128)(2,1)}, bf16[8,2048,128]{2,1,0:T(8,128)(2,1)}) custom-call(s32[1]{0:T(128)S(6)} %add.15.slot, bf16[512,1024]{1,0:T(8,128)(2,1)} %copy-done.1, bf16[1024,1536]{1,0:T(8,128)(2,1)} %wqkv.7, ...), custom_call_target="tpu_custom_call", output_to_operand_aliasing={{0}: (8, {}), {1}: (9, {}), {2}: (10, {})} | custom-call | flops 1610612736 | bytes 9437184 | tf_op jit(solution)/shard_map/project/pallas_call | solution.py:108
  134.7 58.5 %attend.1 = (bf16[2048,512]{1,0:T(8,128)(2,1)}, f32[8,2048,128]{2,1,0:T(8,128)}, bf16[8,36,256,256]{3,2,1,0:T(8,128)(2,1)}, f32[8,128]{1,0:T(8,128)}, bf16[4,32,...) custom-call(bf16[8,2048,128]{2,1,0:T(8,128)(2,1)} %get-tuple-element.106.q_ref, ...), custom_call_target="tpu_custom_call" | custom-call | flops 19327352832 | bytes 41943040 | tf_op jit(solution)/shard_map/attend/pallas_call | solution.py:299
  193.2 4.6 %join.2 = bf16[1024,1024]{1,0:T(8,128)(2,1)} custom-call(s32[1]{0:T(128)} %bitcast.slot, bf16[2048,512]{1,0:T(8,128)(2,1)} %get-tuple-element.111.a.refs_9_.refs_10_.refs_11_.context, bf16[512,1024]{1,0:T(8,128)(2,1)} %wout.7, f32[1024,1024]{1,0:T(8,128)} %get-tuple-element.112.c), custom_call_target="tpu_custom_call" | custom-call | flops 1073741824 | bytes 8388608 | tf_op jit(solution)/shard_map/join/pallas_call | solution.py:453
  197.8 1.5 collective-permute-start.4
  199.4 76.0 %attend_back.1 = (bf16[2048,1536]{1,0:T(8,128)(2,1)}, bf16[2,8,4,32,1024]{4,3,2,1,0:T(8,128)(2,1)}, bf16[2,8,4,16,2048]{4,3,2,1,0:T(8,128)(2,1)}) custom-call(bf16[8,2048,128]{2,1,0:T(8,128)(2,1)} %get-tuple-element.106.q_ref, bf16[8,2048,128]{2,1,0:T(8,128)(2,1)} %get-tuple-element.107.k_ref, bf16[8,2048,128]{2,1,0:T(8,128)(2,1)} %get-tuple-element.108.v_ref, ...), custom_call_target="tpu_custom_call" | custom-call | flops 38654705664 | bytes 83886080 | tf_op jit(solution)/shard_map/attend_back/pallas_call | solution.py:426
  275.4 7.7 %join.3.refs_1_ = bf16[1024,1024]{1,0:T(8,128)(2,1)} custom-call(s32[1]{0:T(128)} %bitcast.slot, bf16[2048,1536]{1,0:T(8,128)(2,1)} %get-tuple-element.118.a.refs_3_.refs_4_.refs_5_.gqkv, bf16[1024,1536]{1,0:T(8,128)(2,1)} %wqkv.7, f32[1024,1024]{1,0:T(8,128)} %get-tuple-element.121.c), custom_call_target="tpu_custom_call" | custom-call | flops 3221225472 | bytes 12582912 | tf_op jit(solution)/shard_map/join/pallas_call | solution.py:453
  283.0 20.4 %weight_grads.1 = (bf16[1024,1536]{1,0:T(8,128)(2,1)}, bf16[1024,512]{1,0:T(8,128)(2,1)}, f32[2048,1024]{1,0:T(8,128)}, f32[1024,2048]{1,0:T(8,128)}) custom-call(s32[3]{0:T(128)} %pad_add_fusion.index, bf16[1024,1024]{1,0:T(8,128)(2,1)} %get-tuple-element.94.nrm.refs_0_, bf16[512,1024]{1,0:T(8,128)(2,1)} %copy-done, bf16[512,1024]{1,0:T(8,128)(2,1)} %copy-done.1, ...), custom_call_target="tpu_custom_call" | custom-call | flops 8589934592 | bytes 20971520 | tf_op jit(solution)/shard_map/weight_grads/pallas_call | solution.py:496
  303.4 0.0 collective-permute-done.4.refs_0_
  303.4 0.0 copy-start.4
  303.4 1.3 copy-done.4
  304.8 0.0 copy-start.7
  304.8 76.7 %tail.1 = (bf16[1024,1024]{1,0:T(8,128)(2,1)}, f32[1024,1024]{1,0:T(8,128)}, f32[8,1024]{1,0:T(8,128)}, bf16[2,8,4,16,1536]{4,3,2,1,0:T(8,128)(2,1)}, bf16[2,8,4,16,512]{4,3,2,1,0:T(8,128)(2,1)}) custom-call(bf16[2048,1536]{1,0:T(8,128)(2,1)} %get-tuple-element.118.a.refs_3_.refs_4_.refs_5_.gqkv, ...), custom_call_target="tpu_custom_call" | custom-call | flops 4294967296 | bytes 39845888 | tf_op jit(solution)/shard_map/tail/pallas_call | solution.py:817
  381.5 0.0 copy-start.3
  381.5 1.5 fusion
  383.0 0.0 copy-done.7
  383.0 1.2 sqrt_bitcast_fusion
  384.2 5.9 %widen.1 = (f32[1024,1536]{1,0:T(8,128)}, f32[512,1024]{1,0:T(8,128)}) custom-call(bf16[1024,1536]{1,0:T(8,128)(2,1)} %bitcast.21, bf16[1024,512]{1,0:T(8,128)(2,1)} %bitcast.23), custom_call_target="tpu_custom_call" | custom-call | bytes 12582912 | tf_op jit(solution)/shard_map/widen/pallas_call | solution.py:847
  390.1 0.0 copy-start.2
  390.1 0.0 copy-done.3
  390.2 1.3 copy.41
  391.5 1.6 copy-done.2
  393.1 2.0 copy.42
Async XLA Ops:
  6.4 43.3 %collective-permute-start = (bf16[512,1024]{1,0:T(8,128)(2,1)}, bf16[512,1024]{1,0:T(8,128)(2,1)S(1)}, u32[]{:S(2)}, u32[]{:S(2)}) collective-permute-start(bf16[512,1024]{1,0:T(8,128)(2,1)} %get-tuple-element.76), channel_id=1, source_target_pairs={{1,0},{0,1},{3,2},{2,3},{5,4},{4,5},{7,6},{6,7},{9,8},{8,9},{11,10... | collective-permute-start | bytes 3145736 | tf_op jit(solution)/shard_map/ppermute | solution.py:965
  9.3 45.8 %collective-permute-start.1 = (bf16[512,1024]{1,0:T(8,128)(2,1)}, bf16[512,1024]{1,0:T(8,128)(2,1)S(1)}, u32[]{:S(2)}, u32[]{:S(2)}) collective-permute-start(bf16[512,1024]{1,0:T(8,128)(2,1)} %get-tuple-element.77), channel_id=1, source_target_pairs={{1,0},{0,1},{3,2},{2,3},{5,4},{4,5},{7,6},{6,7},{9,8},{8,9},{11,10... | collective-permute-start | bytes 3145736 | tf_op jit(solution)/shard_map/ppermute | solution.py:965
  49.7 7.5 %copy-start = (bf16[512,1024]{1,0:T(8,128)(2,1)}, bf16[512,1024]{1,0:T(8,128)(2,1)S(1)}, u32[]{:S(2)}) copy-start(bf16[512,1024]{1,0:T(8,128)(2,1)S(1)} %collective-permute-done.nrm.refs_1_) | copy-start | bytes 3145732
  55.2 2.0 copy-start.5
  55.2 49.3 %collective-permute-start.2 = (bf16[512,1024]{1,0:T(8,128)(2,1)}, bf16[512,1024]{1,0:T(8,128)(2,1)S(1)}, u32[]{:S(2)}, u32[]{:S(2)}) collective-permute-start(bf16[512,1024]{1,0:T(8,128)(2,1)} %get-tuple-element.78), channel_id=1, source_target_pairs={{1,0},{0,1},{3,2},{2,3},{5,4},{4,5},{7,6},{6,7},{9,8},{8,9},{11,10... | collective-permute-start | bytes 3145736 | tf_op jit(solution)/shard_map/ppermute | solution.py:965
  56.9 47.5 %collective-permute-start.3 = (bf16[512,1024]{1,0:T(8,128)(2,1)}, bf16[512,1024]{1,0:T(8,128)(2,1)}, u32[]{:S(2)}, u32[]{:S(2)}) collective-permute-start(bf16[512,1024]{1,0:T(8,128)(2,1)} %get-tuple-element.79), channel_id=1, source_target_pairs={{1,0},{0,1},{3,2},{2,3},{5,4},{4,5},{7,6},{6,7},{9,8},{8,9},{11,10... | collective-permute-start | bytes 3145736 | tf_op jit(solution)/shard_map/ppermute | solution.py:965
  57.2 23.1 %copy-start.6 = (s32[1,4]{1,0:T(1,128)S(1)}, s32[1,4]{1,0:T(1,128)}, u32[]{:S(2)}) copy-start(s32[1,4]{1,0:T(1,128)} %param.11) | copy-start | bytes 52
  104.4 1.0 copy-start.1
  197.8 105.6 %collective-permute-start.4 = (bf16[1024,1024]{1,0:T(8,128)(2,1)}, bf16[1024,1024]{1,0:T(8,128)(2,1)S(1)}, u32[]{:S(2)}, u32[]{:S(2)}) collective-permute-start(bf16[1024,1024]{1,0:T(8,128)(2,1)} %join.2), channel_id=1, source_target_pairs={{1,0},{0,1},{3,2},{2,3},{5,4},{4,5},{7,6},{6,7},{9,8},{8,9},{11,10... | collective-permute-start | bytes 6291464 | tf_op jit(solution)/shard_map/ppermute | solution.py:995
  303.4 1.3 copy-start.4
  304.8 78.3 %copy-start.7 = (f32[1,3]{1,0:T(1,128)S(1)}, f32[1,3]{1,0:T(1,128)}, u32[]{:S(2)}) copy-start(f32[1,3]{1,0:T(1,128)} %constant.41) | copy-start | bytes 40
  381.5 8.7 %copy-start.3 = (bf16[1024,1024]{1,0:T(8,128)(2,1)S(1)}, bf16[1024,1024]{1,0:T(8,128)(2,1)}, u32[]{:S(2)}) copy-start(bf16[1024,1024]{1,0:T(8,128)(2,1)} %get-tuple-element.150) | copy-start | bytes 6291460
  390.1 2.9 copy-start.2
